TPU v7x, 32 devices: a whole 2x2x4 slice. The times are simulated.
32 devices in a mesh: gz: 4 (over z), row: 8 (over y, x, core).
Axes of the slice: x: 2, y: 2, z: 4, core: 2. Of those that a mesh axis runs over, the one named last changes fastest.
Arguments:
- rhs_local: float32 [8, 8, 8, 8192], P(None, None, None, ('gz', 'row')), may hold values from -10 to 10
- stretch: float32 [3, 8192], P(None, ('gz', 'row')), may hold values from 0.25 to 4
Outputs:
- precond: float32 [8, 8, 8, 8192], P(None, None, None, ('gz', 'row'))
All inputs are finite; a program needn't handle non-finite values.
Results may differ from a plain program's by a relative error of at most 0.0003.
Values sent between devices are 32-bit elements; how exact they have to be, the bound alone decides.
No kernel may reach another device: no remote copies, remote signals or barrier semaphores. Data moves between devices by JAX's collectives and lax.ppermute only.
A program may use at most 128 MiB of HBM per device.

v0:
```python
import math

import jax
import jax.numpy as jnp
from jax import lax
from jax.sharding import PartitionSpec as P

ORDER = 7
MID = 3
ITERS = 5
EZ = 4
EA = 4
ER = 16


LOW_BOUND = 0.4
HIGH_BOUND = 4.0
HIGHEST = lax.Precision.HIGHEST


def with_halo(cells, sides, width):
    for axis, dim in sides:
        count = lax.axis_size(axis)
        head = lax.slice_in_dim(cells, 0, width, axis=dim)
        tail = lax.slice_in_dim(cells, cells.shape[dim] - width, cells.shape[dim], axis=dim)
        cells = jnp.concatenate(
            [
                lax.ppermute(tail, axis, [(i, (i + 1) % count) for i in range(count)]),
                cells,
                lax.ppermute(head, axis, [((i + 1) % count, i) for i in range(count)]),
            ],
            axis=dim,
        )
    return cells


def node_points(order):
    steps = jnp.arange(order + 1).astype(jnp.float32)
    return -jnp.cos(steps * (math.pi / order))


def level_tables(order):
    points = node_points(order)
    count = order + 1
    identity = jnp.eye(count, dtype=jnp.float32)
    distance = points[:, None] - points[None, :] + identity
    barycentric = 1.0 / jnp.prod(distance, axis=1)
    offdiag = barycentric[None, :] / barycentric[:, None] / distance * (1.0 - identity)
    derivative = offdiag - jnp.diag(jnp.sum(offdiag, axis=1))
    place = jnp.arange(count).astype(jnp.float32)
    running = jnp.ones((count,), jnp.float32)
    for freq in range(1, order // 2 + 1):
        factor = 2.0
        running = running - factor / (4.0 * freq * freq - 1.0) * jnp.cos(
            2.0 * freq * place * math.pi / order
        )
    endpoint = jnp.where((place == 0) | (place == order), 1.0, 2.0).astype(jnp.float32)
    weights = endpoint / order * running
    stiffness = jnp.dot(derivative.T * weights[None, :], derivative, precision=HIGHEST)
    return (weights, stiffness)


def interpolation(fine_order, coarse_order):
    fine_points = node_points(fine_order)
    coarse_points = node_points(coarse_order)
    columns = []
    for column in range(coarse_order + 1):
        value = jnp.ones((fine_order + 1,), jnp.float32)
        for other in range(coarse_order + 1):
            if other != column:
                value = (
                    value
                    * (fine_points - coarse_points[other])
                    / (coarse_points[column] - coarse_points[other])
                )
        columns.append(value)
    return jnp.stack(columns, axis=1)


def weight_shape(values, position, ndim):
    shape = [1] * ndim
    shape[position] = values.shape[0]
    return values.reshape(shape)


def element_apply(field, coeff, weights, stiffness):
    ndim = field.ndim
    along_z = weight_shape(weights, 0, ndim)
    along_a = weight_shape(weights, 1, ndim)
    along_r = weight_shape(weights, 2, ndim)
    part_z = jnp.einsum("ij,jbc...->ibc...", stiffness, field, precision=HIGHEST)
    part_a = jnp.einsum("ij,ajc...->aic...", stiffness, field, precision=HIGHEST)
    part_r = jnp.einsum("ij,abj...->abi...", stiffness, field, precision=HIGHEST)
    return (
        coeff[0] * along_a * along_r * part_z
        + coeff[1] * along_z * along_r * part_a
        + coeff[2] * along_z * along_a * part_r
    )


def element_diagonal(coeff, weights, stiffness, ndim):
    diag_k = jnp.diagonal(stiffness)
    term_z = (
        weight_shape(diag_k, 0, ndim)
        * weight_shape(weights, 1, ndim)
        * weight_shape(weights, 2, ndim)
    )
    term_a = (
        weight_shape(weights, 0, ndim)
        * weight_shape(diag_k, 1, ndim)
        * weight_shape(weights, 2, ndim)
    )
    term_r = (
        weight_shape(weights, 0, ndim)
        * weight_shape(weights, 1, ndim)
        * weight_shape(diag_k, 2, ndim)
    )
    return coeff[0] * term_z + coeff[1] * term_a + coeff[2] * term_r


def face_add(field, node_dim, stride, count, direction_kind):
    size = field.shape[0]
    moved = jnp.moveaxis(field, node_dim, 0)
    low_face = moved[0]
    high_face = moved[size - 1]
    elems = low_face.shape[-1]
    position = jnp.arange(elems) // stride % count
    zero_block = jnp.zeros(low_face.shape[:-1] + (stride,), jnp.float32)
    below_local = jnp.concatenate([zero_block, high_face[..., : elems - stride]], axis=-1)
    above_local = jnp.concatenate([low_face[..., stride:], zero_block], axis=-1)
    if direction_kind == "radial":
        from_below = jnp.where(position > 0, below_local, 0.0)
        from_above = jnp.where(position < count - 1, above_local, 0.0)
    else:
        outer = elems // (stride * count)
        split_shape = low_face.shape[:-1] + (outer, count, stride)
        low_edge = low_face.reshape(split_shape)[..., 0, :]
        high_edge = high_face.reshape(split_shape)[..., count - 1, :]
        stacked = jnp.stack([low_edge, high_edge], axis=0)
        if direction_kind == "azimuth":
            padded = with_halo(stacked, (("row", 0),), 1)
        else:
            padded = with_halo(stacked, (("gz", 0),), 1)
        remote_below = jnp.broadcast_to(padded[0][..., None, :], split_shape).reshape(
            low_face.shape
        )
        remote_above = jnp.broadcast_to(padded[3][..., None, :], split_shape).reshape(
            low_face.shape
        )
        from_below = jnp.where(position == 0, remote_below, below_local)
        from_above = jnp.where(position == count - 1, remote_above, above_local)
    moved = moved.at[0].set(low_face + from_below)
    moved = moved.at[size - 1].set(high_face + from_above)
    return jnp.moveaxis(moved, 0, node_dim)


def assemble(field):
    field = face_add(field, 2, 1, ER, "radial")
    field = face_add(field, 1, ER, EA, "azimuth")
    return face_add(field, 0, EA * ER, EZ, "axial")


def level_data(order):
    weights, stiffness = level_tables(order)
    count = order + 1
    node_index = jnp.arange(count)
    radial = jnp.arange(EZ * EA * ER) % ER
    at_wall = (node_index[:, None] == 0) & (radial[None, :] == 0) | (
        node_index[:, None] == count - 1
    ) & (radial[None, :] == ER - 1)
    wall_mask = jnp.where(at_wall, 0.0, 1.0).astype(jnp.float32)[None, None]
    edge = jnp.where((node_index == 0) | (node_index == count - 1), 0.5, 1.0).astype(jnp.float32)
    share = (edge[:, None, None] * edge[None, :, None] * edge[None, None, :])[..., None]
    return (weights, stiffness, wall_mask, share)


def chebyshev(operate, inverse_diag, rhs):
    theta = 0.5 * (HIGH_BOUND + LOW_BOUND)
    delta = 0.5 * (HIGH_BOUND - LOW_BOUND)
    rho_now = delta / theta
    step = inverse_diag * rhs / theta
    solution = step
    residual = rhs - operate(step)
    rho_next = 1.0 / (2.0 * theta / delta - rho_now)
    step = rho_next * rho_now * step + 2.0 * rho_next / delta * inverse_diag * residual
    return (solution + step, step, residual)


def restrict(field, table):
    return jnp.einsum("ia,jb,kc,ijke->abce", table, table, table, field, precision=HIGHEST)


def prolong(field, table):
    return jnp.einsum("ia,jb,kc,abce->ijke", table, table, table, field, precision=HIGHEST)


def coarse_spread(low_b, low_op, weight):

    def squared_norm(values):
        return lax.psum(jnp.sum(weight * values * values), ("gz", "row"))

    low_sol = jnp.zeros_like(low_b)
    low_res = low_b
    direction = low_b
    norm_now = squared_norm(low_res)
    for iteration in range(ITERS):
        image = low_op(direction)
        alpha = norm_now / lax.psum(jnp.sum(weight * direction * image), ("gz", "row"))
        low_sol = low_sol + alpha * direction
        low_res = low_res - alpha * image
        norm_next = squared_norm(low_res)
        direction = low_res + norm_next / norm_now * direction
        norm_now = norm_next
    return low_sol


def per_device(rhs_local, stretch):
    fine_tab = level_data(ORDER)
    mid_tab = level_data(MID)
    low_tab = level_data(1)

    def make_operator(tables):

        def operate(field):
            return tables[2] * assemble(element_apply(field, stretch, tables[0], tables[1]))

        return operate

    fine_op = make_operator(fine_tab)
    mid_op = make_operator(mid_tab)
    low_op = make_operator(low_tab)
    fine_inv = fine_tab[2] / assemble(element_diagonal(stretch, fine_tab[0], fine_tab[1], 4))
    mid_inv = mid_tab[2] / assemble(element_diagonal(stretch, mid_tab[0], mid_tab[1], 4))
    to_mid = interpolation(ORDER, MID)
    to_low = interpolation(MID, 1)
    fine_b = fine_tab[2] * assemble(rhs_local)
    fine_sol, fine_step, fine_res = chebyshev(fine_op, fine_inv, fine_b)
    fine_res = fine_res - fine_op(fine_step)
    mid_b = mid_tab[2] * assemble(restrict(fine_tab[3] * fine_res, to_mid))
    mid_sol, mid_step, mid_res = chebyshev(mid_op, mid_inv, mid_b)
    mid_res = mid_res - mid_op(mid_step)
    low_b = low_tab[2] * assemble(restrict(mid_tab[3] * mid_res, to_low))
    low_sol = coarse_spread(low_b, low_op, low_tab[2] * low_tab[3])
    lifted = prolong(low_sol, to_low)
    mid_sol = mid_sol + lifted
    mid_res = mid_res - mid_op(lifted)
    mid_sol = mid_sol + chebyshev(mid_op, mid_inv, mid_res)[0]
    raised = prolong(mid_sol, to_mid)
    fine_sol = fine_sol + raised
    fine_res = fine_res - fine_op(raised)
    return fine_sol + chebyshev(fine_op, fine_inv, fine_res)[0]


def solution(mesh):
    placed = (P(None, None, None, ("gz", "row")), P(None, ("gz", "row")))
    return jax.shard_map(
        per_device,
        mesh=mesh,
        in_specs=placed,
        out_specs=P(None, None, None, ("gz", "row")),
        check_vma=False,
    )
```

profile of v0, /device:TPU:0, one launch (start us, length us, event | category | flops | bytes accessed | tf_op | source)
XLA Modules:
  0.0 743.0 jit_solution(9740172112269053551)
XLA Ops:
  7.6 2.9 collective-permute-start.1
  36.4 4.4 collective-permute-start.7
  72.1 4.0 collective-permute-start.11
  109.3 4.2 collective-permute-start.19
  134.5 3.9 collective-permute-start.23
  138.7 3.9 collective-permute-start.15
  147.2 2.7 collective-permute-start.25
  152.2 3.9 collective-permute-start.27
  162.5 2.7 collective-permute-start.29
  167.4 3.8 collective-permute-start.31
  181.2 3.5 collective-permute-start.35
  186.0 4.0 collective-permute-done.34
  192.6 2.7 collective-permute-start.37
  203.4 38.1 %all-reduce.108 = (f32[]{:T(128)}, f32[]{:T(128)}) all-reduce(f32[]{:T(128)} %get-tuple-element.1302, f32[]{:T(128)} %get-tuple-element.1301), channel_id=1, replica_groups=mesh['gz'=4,'row'=8] {'gz','row'}, use_global_device_ids=true, to_apply=%region_5.6 | all-reduce | flops 2 | bytes 16 | tf_op jit(solution)/shard_map/psum | solution.py:200
  243.4 42.0 %psum.72 = f32[]{:T(128)} all-reduce(f32[]{:T(128)} %get-tuple-element.1311), channel_id=1, replica_groups=mesh['gz'=4,'row'=8] {'gz','row'}, use_global_device_ids=true, to_apply=%region_11.12 | all-reduce | flops 1 | bytes 8 | tf_op jit(solution)/shard_map/psum | solution.py:200
  287.9 2.7 collective-permute-start.41
  296.0 3.4 collective-permute-done.42
  300.3 38.0 %psum.73 = f32[]{:T(128)} all-reduce(f32[]{:T(128)} %multiply_reduce_fusion.3), channel_id=1, replica_groups=mesh['gz'=4,'row'=8] {'gz','row'}, use_global_device_ids=true, to_apply=%region_13.14 | all-reduce | flops 1 | bytes 8 | tf_op jit(solution)/shard_map/psum | solution.py:208
  340.2 43.1 %psum.74 = f32[]{:T(128)} all-reduce(f32[]{:T(128)} %get-tuple-element.1309), channel_id=1, replica_groups=mesh['gz'=4,'row'=8] {'gz','row'}, use_global_device_ids=true, to_apply=%region_15.16 | all-reduce | flops 1 | bytes 8 | tf_op jit(solution)/shard_map/psum | solution.py:200
  394.9 3.4 collective-permute-done.46
  399.2 37.6 %psum.75 = f32[]{:T(128)} all-reduce(f32[]{:T(128)} %multiply_reduce_fusion.2), channel_id=1, replica_groups=mesh['gz'=4,'row'=8] {'gz','row'}, use_global_device_ids=true, to_apply=%region_17.18 | all-reduce | flops 1 | bytes 8 | tf_op jit(solution)/shard_map/psum | solution.py:208
  438.6 43.1 %psum.76 = f32[]{:T(128)} all-reduce(f32[]{:T(128)} %get-tuple-element.1307), channel_id=1, replica_groups=mesh['gz'=4,'row'=8] {'gz','row'}, use_global_device_ids=true, to_apply=%region_19.20 | all-reduce | flops 1 | bytes 8 | tf_op jit(solution)/shard_map/psum | solution.py:200
  493.4 3.4 collective-permute-done.50
  497.6 37.7 %psum.77 = f32[]{:T(128)} all-reduce(f32[]{:T(128)} %get-tuple-element.1305), channel_id=1, replica_groups=mesh['gz'=4,'row'=8] {'gz','row'}, use_global_device_ids=true, to_apply=%region_21.22 | all-reduce | flops 1 | bytes 8 | tf_op jit(solution)/shard_map/psum | solution.py:208
  537.4 43.1 %psum.78 = f32[]{:T(128)} all-reduce(f32[]{:T(128)} %fusion.101), channel_id=1, replica_groups=mesh['gz'=4,'row'=8] {'gz','row'}, use_global_device_ids=true, to_apply=%region_23.24 | all-reduce | flops 1 | bytes 8 | tf_op jit(solution)/shard_map/psum | solution.py:200
  591.0 3.4 collective-permute-done.54
  595.2 37.6 %psum.79 = f32[]{:T(128)} all-reduce(f32[]{:T(128)} %multiply_reduce_fusion), channel_id=1, replica_groups=mesh['gz'=4,'row'=8] {'gz','row'}, use_global_device_ids=true, to_apply=%region_25.26 | all-reduce | flops 1 | bytes 8 | tf_op jit(solution)/shard_map/psum | solution.py:208
  636.6 2.7 collective-permute-start.57
  641.5 2.9 collective-permute-start.58
  656.0 3.2 collective-permute-start.63
  689.8 4.1 collective-permute-start.67
  728.2 2.8 collective-permute-start.71
  (1053 shorter events, 271.8 us)
Async XLA Ops:
  6.0 21.3 %collective-permute-start = (f32[1,8,8,4,16]{4,3,2,1,0:T(4,128)}, f32[1,8,8,4,16]{4,3,2,1,0:T(4,128)S(1)}, u32[]{:S(2)}, u32[]{:S(2)}) collective-permute-start(f32[1,8,8,4,16]{4,3,2,1,0:T(4,128)} %bitcast.9), channel_id=1, source_target_pairs={{0,1},{1,2},{2,3},{3,4},{4,5},{5,6},{6,7},{7,0},{8,9},{9,10},{10,1... | collective-permute-start | bytes 49160 | tf_op jit(solution)/shard_map/ppermute | solution.py:28
  7.6 19.1 %collective-permute-start.1 = (f32[1,8,8,4,16]{4,3,2,1,0:T(4,128)}, f32[1,8,8,4,16]{4,3,2,1,0:T(4,128)S(1)}, u32[]{:S(2)}, u32[]{:S(2)}) collective-permute-start(f32[1,8,8,4,16]{4,3,2,1,0:T(4,128)} %bitcast.13), channel_id=1, source_target_pairs={{1,0},{2,1},{3,2},{4,3},{5,4},{6,5},{7,6},{0,7},{9,8},{10,9},{11,1... | collective-permute-start | bytes 49160 | tf_op jit(solution)/shard_map/ppermute | solution.py:30
  12.8 15.0 %collective-permute-start.4 = (f32[1,8,8,4,16]{4,3,2,1,0:T(4,128)}, f32[1,8,8,4,16]{4,3,2,1,0:T(4,128)}, u32[]{:S(2)}, u32[]{:S(2)}) collective-permute-start(f32[1,8,8,4,16]{4,3,2,1,0:T(4,128)} %bitcast.30), channel_id=1, source_target_pairs={{0,1},{1,2},{2,3},{3,4},{4,5},{5,6},{6,7},{7,0},{8,9},{9,10},{10,1... | collective-permute-start | bytes 49160 | tf_op jit(solution)/shard_map/ppermute | solution.py:28
  14.0 15.4 %collective-permute-start.5 = (f32[1,8,8,4,16]{4,3,2,1,0:T(4,128)}, f32[1,8,8,4,16]{4,3,2,1,0:T(4,128)S(1)}, u32[]{:S(2)}, u32[]{:S(2)}) collective-permute-start(f32[1,8,8,4,16]{4,3,2,1,0:T(4,128)} %bitcast.34), channel_id=1, source_target_pairs={{1,0},{2,1},{3,2},{4,3},{5,4},{6,5},{7,6},{0,7},{9,8},{10,9},{11,1... | collective-permute-start | bytes 49160 | tf_op jit(solution)/shard_map/ppermute | solution.py:30
  31.3 13.4 %collective-permute-start.2 = (f32[1,8,8,1,64]{4,1,2,3,0:T(8,128)S(1)}, f32[1,8,8,1,64]{4,1,2,3,0:T(8,128)S(1)}, u32[]{:S(2)}, u32[]{:S(2)}) collective-permute-start(f32[1,8,8,1,64]{4,1,2,3,0:T(8,128)S(1)} %bitcast.1489), channel_id=1, source_target_pairs={{0,8},{8,16},{16,24},{24,0},{1,9},{9,17},{17,25},{25,1},{2,10},{10... | collective-permute-start | bytes 49160 | tf_op jit(solution)/shard_map/ppermute | solution.py:28
  33.8 11.1 %collective-permute-start.3 = (f32[1,8,8,1,64]{4,1,2,3,0:T(8,128)S(1)}, f32[1,8,8,1,64]{4,1,2,3,0:T(8,128)S(1)}, u32[]{:S(2)}, u32[]{:S(2)}) collective-permute-start(f32[1,8,8,1,64]{4,1,2,3,0:T(8,128)S(1)} %bitcast.1488), channel_id=1, source_target_pairs={{8,0},{16,8},{24,16},{0,24},{9,1},{17,9},{25,17},{1,25},{10,2},{18... | collective-permute-start | bytes 49160 | tf_op jit(solution)/shard_map/ppermute | solution.py:30
  36.2 8.9 %collective-permute-start.6 = (f32[1,8,8,1,64]{4,2,1,3,0:T(8,128)S(1)}, f32[1,8,8,1,64]{4,2,1,3,0:T(8,128)S(1)}, u32[]{:S(2)}, u32[]{:S(2)}) collective-permute-start(f32[1,8,8,1,64]{4,2,1,3,0:T(8,128)S(1)} %bitcast.1492), channel_id=1, source_target_pairs={{0,8},{8,16},{16,24},{24,0},{1,9},{9,17},{17,25},{25,1},{2,10},{10... | collective-permute-start | bytes 49160 | tf_op jit(solution)/shard_map/ppermute | solution.py:28
  36.4 8.8 %collective-permute-start.7 = (f32[1,8,8,1,64]{4,2,1,3,0:T(8,128)S(1)}, f32[1,8,8,1,64]{4,2,1,3,0:T(8,128)S(1)}, u32[]{:S(2)}, u32[]{:S(2)}) collective-permute-start(f32[1,8,8,1,64]{4,2,1,3,0:T(8,128)S(1)} %bitcast.1491), channel_id=1, source_target_pairs={{8,0},{16,8},{24,16},{0,24},{9,1},{17,9},{25,17},{1,25},{10,2},{18... | collective-permute-start | bytes 49160 | tf_op jit(solution)/shard_map/ppermute | solution.py:30
  51.3 9.7 %collective-permute-start.8 = (f32[1,8,8,4,16]{4,3,2,1,0:T(4,128)}, f32[1,8,8,4,16]{4,3,2,1,0:T(4,128)S(1)}, u32[]{:S(2)}, u32[]{:S(2)}) collective-permute-start(f32[1,8,8,4,16]{4,3,2,1,0:T(4,128)} %bitcast.58), channel_id=1, source_target_pairs={{0,1},{1,2},{2,3},{3,4},{4,5},{5,6},{6,7},{7,0},{8,9},{9,10},{10,1... | collective-permute-start | bytes 49160 | tf_op jit(solution)/shard_map/ppermute | solution.py:28
  65.7 10.4 %collective-permute-start.10 = (f32[1,8,8,1,64]{4,1,2,3,0:T(8,128)S(1)}, f32[1,8,8,1,64]{4,1,2,3,0:T(8,128)S(1)}, u32[]{:S(2)}, u32[]{:S(2)}) collective-permute-start(f32[1,8,8,1,64]{4,1,2,3,0:T(8,128)S(1)} %bitcast.1497), channel_id=1, source_target_pairs={{0,8},{8,16},{16,24},{24,0},{1,9},{9,17},{17,25},{25,1},{2,10},{10... | collective-permute-start | bytes 49160 | tf_op jit(solution)/shard_map/ppermute | solution.py:28
  72.1 5.6 collective-permute-start.11
  86.8 11.3 %collective-permute-start.16 = (f32[1,8,8,4,16]{4,3,2,1,0:T(4,128)}, f32[1,8,8,4,16]{4,3,2,1,0:T(4,128)}, u32[]{:S(2)}, u32[]{:S(2)}) collective-permute-start(f32[1,8,8,4,16]{4,3,2,1,0:T(4,128)} %bitcast.104), channel_id=1, source_target_pairs={{0,1},{1,2},{2,3},{3,4},{4,5},{5,6},{6,7},{7,0},{8,9},{9,10},{10,1... | collective-permute-start | bytes 49160 | tf_op jit(solution)/shard_map/ppermute | solution.py:28
  95.5 6.9 collective-permute-start.17
  107.1 6.4 collective-permute-start.18
  109.3 7.5 %collective-permute-start.19 = (f32[1,8,8,1,64]{4,1,2,3,0:T(8,128)S(1)}, f32[1,8,8,1,64]{4,1,2,3,0:T(8,128)S(1)}, u32[]{:S(2)}, u32[]{:S(2)}) collective-permute-start(f32[1,8,8,1,64]{4,1,2,3,0:T(8,128)S(1)} %bitcast.1500), channel_id=1, source_target_pairs={{8,0},{16,8},{24,16},{0,24},{9,1},{17,9},{25,17},{1,25},{10,2},{18... | collective-permute-start | bytes 49160 | tf_op jit(solution)/shard_map/ppermute | solution.py:30
  134.2 8.4 %collective-permute-start.22 = (f32[1,4,4,1,64]{4,1,2,3,0:T(4,128)S(1)}, f32[1,4,4,1,64]{4,1,2,3,0:T(4,128)S(1)}, u32[]{:S(2)}, u32[]{:S(2)}) collective-permute-start(f32[1,4,4,1,64]{4,1,2,3,0:T(4,128)S(1)} %bitcast.1548), channel_id=1, source_target_pairs={{0,8},{8,16},{16,24},{24,0},{1,9},{9,17},{17,25},{25,1},{2,10},{10... | collective-permute-start | bytes 12296 | tf_op jit(solution)/shard_map/ppermute | solution.py:28
  134.5 8.3 %collective-permute-start.23 = (f32[1,4,4,1,64]{4,1,2,3,0:T(4,128)S(1)}, f32[1,4,4,1,64]{4,1,2,3,0:T(4,128)S(1)}, u32[]{:S(2)}, u32[]{:S(2)}) collective-permute-start(f32[1,4,4,1,64]{4,1,2,3,0:T(4,128)S(1)} %bitcast.1549), channel_id=1, source_target_pairs={{8,0},{16,8},{24,16},{0,24},{9,1},{17,9},{25,17},{1,25},{10,2},{18... | collective-permute-start | bytes 12296 | tf_op jit(solution)/shard_map/ppermute | solution.py:30
  138.5 5.5 collective-permute-start.14
  152.1 7.2 collective-permute-start.26
  152.2 7.1 collective-permute-start.27
  167.1 5.5 collective-permute-start.30
  167.4 5.5 collective-permute-start.31
  641.5 5.5 collective-permute-start.58
  655.1 5.5 collective-permute-start.62
  670.5 6.3 collective-permute-start.64
  673.5 6.6 collective-permute-start.65
  689.6 5.9 collective-permute-start.66
  689.8 5.9 collective-permute-start.67
  709.2 5.7 collective-permute-start.68
  712.3 7.3 collective-permute-start.69
  725.6 6.3 collective-permute-start.70
  728.2 7.8 %collective-permute-start.71 = (f32[1,8,8,1,64]{4,1,2,3,0:T(8,128)}, f32[1,8,8,1,64]{4,1,2,3,0:T(8,128)}, u32[]{:S(2)}, u32[]{:S(2)}) collective-permute-start(f32[1,8,8,1,64]{4,1,2,3,0:T(8,128)} %bitcast.435), channel_id=1, source_target_pairs={{8,0},{16,8},{24,16},{0,24},{9,1},{17,9},{25,17},{1,25},{10,2},{18... | collective-permute-start | bytes 49160 | tf_op jit(solution)/shard_map/ppermute | solution.py:30
  (100 other events, 625.8 us)
where the time goes:
time: 753 us; the launch traced here: 743 us
  blocking collectives  360 us (48%)
  local copies, waits for them, and re-layouts  125 us (17%)
  starting transfers between devices  109 us (14%)
  waiting for transfers between devices  55.9 us (7%)
  other arithmetic  38.8 us (5%)
  between operations  32.5 us (4%)
  matrix products  21.9 us (3%)
    psum x5, blocking collectives, squared_norm(): return lax.psum(jnp.sum(weight * values * values), ('gz', 'row'))  209 us
    psum x4, blocking collectives, coarse_spread(): lax.psum(jnp.sum(weight * direction * image), ('gz', 'row'))  151 us
    ppermute x36, starting transfers between devices, with_halo(): lax.ppermute(head, axis, [((i + 1) % count, i) for i in range(count)])  95.4 us
    ppermute x36, waiting for transfers between devices, with_halo(): lax.ppermute(tail, axis, [(i, (i + 1) % count) for i in range(count)])  41.2 us
    unnamed x143, local copies, waits for them, and re-layouts  19.4 us
    scatter x37, local copies, waits for them, and re-layouts, face_add(): moved = moved.at[size - 1].set(high_face + from_above)  15.4 us
  transfers between devices with their start and end apart: 72, of which 41 were waited for; matrix products, arithmetic and copies ran while one was open for 9% of the time, Pallas kernels for 0%

commit v1 on v0

v1 whole, which is shorter than its diff:
```python
import functools

import jax
import jax.numpy as jnp
import numpy as np
from jax import lax
from jax.experimental import pallas as pl
from jax.experimental.pallas import tpu as pltpu
from jax.sharding import PartitionSpec as P

ITERS = 5
EZ = 4
EA = 4
ER = 16
HALF = 128
GROUP = EA * ER

THETA = 2.2
DELTA = 1.8
RHO = DELTA / THETA
RHO2 = 1.0 / (2.0 * THETA / DELTA - RHO)
C1 = RHO2 * RHO
C2 = 2.0 * RHO2 / DELTA


def points_of(order):
    return -np.cos(np.pi * np.arange(order + 1) / order)


def tables_of(order):
    x = points_of(order)
    n = order + 1
    dist = x[:, None] - x[None, :] + np.eye(n)
    bary = 1.0 / np.prod(dist, axis=1)
    off = bary[None, :] / bary[:, None] / dist * (1.0 - np.eye(n))
    deriv = off - np.diag(off.sum(axis=1))
    place = np.arange(n)
    run = np.ones(n)
    for j in range(1, order // 2 + 1):
        b = 1.0 if 2 * j == order else 2.0
        run = run - b / (4.0 * j * j - 1.0) * np.cos(2.0 * j * place * np.pi / order)
    ends = np.where((place == 0) | (place == order), 1.0, 2.0)
    w = ends / order * run
    k = deriv.T @ np.diag(w) @ deriv
    return w, k


def interp_of(fine, coarse):
    x, y = points_of(fine), points_of(coarse)
    cols = []
    for j in range(coarse + 1):
        v = np.ones(fine + 1)
        for k in range(coarse + 1):
            if k != j:
                v = v * (x - y[k]) / (y[j] - y[k])
        cols.append(v)
    return np.stack(cols, axis=1)


W7, K7 = tables_of(7)
W3, K3 = tables_of(3)
J73 = interp_of(7, 3)
J31 = interp_of(3, 1)
KRON73 = np.kron(np.kron(J73, J73), J73).astype(np.float32)


def weighted_sum(coefs, vals):
    total = None
    for c, v in zip(coefs, vals):
        term = v * float(c)
        total = term if total is None else total + term
    return total


def along(table, vals):
    rows, cols = table.shape
    half = cols // 2
    even = [vals[j] + vals[cols - 1 - j] for j in range(half)]
    odd = [vals[j] - vals[cols - 1 - j] for j in range(half)]
    out = [None] * rows
    for i in range(rows // 2):
        e = weighted_sum([(table[i, j] + table[i, cols - 1 - j]) / 2 for j in range(half)], even)
        o = weighted_sum([(table[i, j] - table[i, cols - 1 - j]) / 2 for j in range(half)], odd)
        out[i] = e + o
        out[rows - 1 - i] = e - o
    return out


def sub_iota(shape=(8, HALF)):
    return lax.broadcasted_iota(jnp.int32, shape, len(shape) - 2)


def lane_iota(shape=(8, HALF)):
    return lax.broadcasted_iota(jnp.int32, shape, len(shape) - 1)


def column(values):
    it = sub_iota()
    out = jnp.full((8, HALF), float(values[0]), jnp.float32)
    for i in range(1, 8):
        out = jnp.where(it == i, float(values[i]), out)
    return out


def lroll(v, shift):
    n = v.shape[-1]
    shift = shift % n
    return v if shift == 0 else pltpu.roll(v, shift, v.ndim - 1)


def sroll(v, shift):
    n = v.shape[-2]
    shift = shift % n
    return v if shift == 0 else pltpu.roll(v, shift, v.ndim - 2)


def half_of(h):
    return slice(h * HALF, (h + 1) * HALF)


def radial_masks():
    sub, lane = sub_iota(), lane_iota()
    r = lane % ER
    low = (sub == 0) & (r > 0)
    high = (sub == 7) & (r < ER - 1)
    wall = ((sub == 0) & (r == 0)) | ((sub == 7) & (r == ER - 1))
    return low, high, wall


def radial_add(v, masks):
    below = lroll(sroll(v, 1), 1)
    above = lroll(sroll(v, 7), HALF - 1)
    return v + jnp.where(masks[0], below, jnp.where(masks[1], above, 0.0))


def radial_columns():
    return [column([K7[i, (i - s) % 8] for i in range(8)]) for s in range(8)]


def radial_apply(rolls, v):
    total = rolls[0] * v
    for s in range(1, 8):
        total = total + rolls[s] * sroll(v, s)
    return total


def fine_apply(src, dst, base, s_half, sign):
    rolls = radial_columns()
    wr = column(W7)
    for h in range(2):
        sl = half_of(h)
        s0, s1, s2 = [v * sign for v in stretch_rows(s_half[h])]
        s0, s1 = s0 * wr, s1 * wr
        for iz in range(8):
            vals = [src[iz, ia, :, sl] for ia in range(8)]
            part_a = along(K7, vals)
            s1z = s1 * float(W7[iz])
            s2z = s2 * float(W7[iz])
            for ia in range(8):
                part = part_a[ia] * s1z + radial_apply(rolls, vals[ia]) * (s2z * float(W7[ia]))
                dst[iz, ia, :, sl] = part if base is None else base[iz, ia, :, sl] + part
        for ia in range(8):
            vals = [src[iz, ia, :, sl] for iz in range(8)]
            part_z = along(K7, vals)
            s0a = s0 * float(W7[ia])
            for iz in range(8):
                dst[iz, ia, :, sl] = dst[iz, ia, :, sl] + part_z[iz] * s0a


def diag_at(s_ref, h, iz, ia, wr, kr):
    sl = half_of(h)
    s0, s1, s2 = (jnp.broadcast_to(s_ref[c : c + 1, sl], (8, HALF)) for c in range(3))
    ends = s0 * float(K7[iz, iz] * W7[ia]) + s1 * float(W7[iz] * K7[ia, ia])
    return ends * wr + s2 * (kr * float(W7[iz] * W7[ia]))


def pack_a(plane, slot):
    place = (lane_iota() // ER) % EA
    out = []
    for i in range(4):
        parts = [plane(0, i), plane(1, i), plane(0, i + 4), plane(1, i + 4)]
        parts = [lroll(v, (s - slot) * ER) for s, v in enumerate(parts)]
        out.append(jnp.where(place == 0, parts[0], jnp.where(place == 1, parts[1], jnp.where(place == 2, parts[2], parts[3]))))
    return out


def unpack_a(msg, slot, h, iz):
    s = h + 2 * (iz // 4)
    return lroll(msg[iz % 4], (slot - s) * ER)


def pack_z(plane, upper):
    low = lane_iota() < GROUP
    out = []
    for i in range(4):
        a, b = plane(i), plane(i + 4)
        out.append(jnp.where(low, lroll(a, GROUP) if upper else a, b if upper else lroll(b, GROUP)))
    return out


def unpack_z(msg, ia, upper):
    m = msg[ia % 4]
    return lroll(m, GROUP) if (ia < 4) == upper else m


def parity(axis):
    return lax.axis_index(axis) % 2 == 0


def choose(flag, a, b):
    return [jnp.where(flag, x, y) for x, y in zip(a, b)]


def got(axis, r1, r2, lo, hi):
    even = parity(axis)
    one = [r1[i] for i in range(lo, hi)]
    two = [r2[i] for i in range(lo, hi)]
    return choose(even, two, one), choose(even, one, two)


def post(axis, lower, upper, m1, m2, start):
    even = parity(axis)
    for i, (lo, up) in enumerate(zip(lower, upper)):
        m1[start + i] = jnp.where(even, up, lo)
        m2[start + i] = jnp.where(even, lo, up)


def place_of():
    return (lane_iota() // ER) % EA


def every_fine():
    for h in range(2):
        for iz in range(8):
            for ia in range(8):
                yield iz, ia, half_of(h)


def join_a(y, iz, h, left, right):
    place, sl = place_of(), half_of(h)
    lo, hi = y[iz, 0, :, sl], y[iz, 7, :, sl]
    y[iz, 0, :, sl] = lo + jnp.where(place > 0, lroll(hi, ER), left)
    y[iz, 7, :, sl] = hi + jnp.where(place < EA - 1, lroll(lo, HALF - ER), right)


def join_z(y, ia, beyond):
    low = lane_iota() < GROUP
    lo0, lo1 = y[0, ia, :, half_of(0)], y[0, ia, :, half_of(1)]
    hi0, hi1 = y[7, ia, :, half_of(0)], y[7, ia, :, half_of(1)]
    up0, up1 = lroll(hi0, GROUP), lroll(hi1, GROUP)
    dn0, dn1 = lroll(lo0, GROUP), lroll(lo1, GROUP)
    y[0, ia, :, half_of(0)] = lo0 + jnp.where(low, beyond, up0)
    y[0, ia, :, half_of(1)] = lo1 + jnp.where(low, up0, up1)
    y[7, ia, :, half_of(0)] = hi0 + jnp.where(low, dn0, dn1)
    y[7, ia, :, half_of(1)] = hi1 + jnp.where(low, dn1, beyond)


def sum_inside(y):
    for iz in range(8):
        for h in range(2):
            join_a(y, iz, h, 0.0, 0.0)
    for ia in range(8):
        join_z(y, ia, 0.0)


FIRST, LATER = 17, 9


def send_z(q, inverse, m1, m2):
    top_q = pack_z(lambda ia: q[7, ia, :, half_of(1)], True)
    bottom_q = pack_z(lambda ia: q[0, ia, :, half_of(0)], False)
    post("gz", bottom_q, top_q, m1, m2, 0)

    def behind(ia, h):
        nodes = range(7) if h else range(1, 8)
        row = K7[7 if h else 0] / THETA
        return weighted_sum([row[j] for j in nodes], [inverse(j, ia, h) * q[j, ia, :, half_of(h)] for j in nodes])

    top_t = pack_z(lambda ia: behind(ia, 1), True)
    bottom_t = pack_z(lambda ia: behind(ia, 0), False)
    post("gz", bottom_t, top_t, m1, m2, 4)


def edge_lines(f, ia, h):
    slot = lane_iota() // ER
    source = (EA - 1 if ia else 0) + (EA if h else 0)
    out = None
    for j in range(1, 8):
        v = lroll(f[7 - j if h else j, ia, :, half_of(h)], (j - 1 - source) * ER)
        out = v if out is None else jnp.where(slot == j - 1, v, out)
    return out


def k_first(rhs_any, s_any, q, g, m1, m2, s_ref, rhs, sems):
    copy_s = pltpu.make_async_copy(s_any, s_ref, sems.at[0])
    copy_rhs = pltpu.make_async_copy(rhs_any, rhs, sems.at[1])
    copy_s.start()
    copy_rhs.start()
    masks = radial_masks()
    wr, kr = column(W7), column(np.diag(K7))
    copy_s.wait()
    for iz, ia, sl in every_fine():
        g[iz, ia, :, sl] = radial_add(diag_at(s_ref, sl.start // HALF, iz, ia, wr, kr), masks)
    sum_inside(g)
    copy_rhs.wait()
    for iz, ia, sl in every_fine():
        q[iz, ia, :, sl] = radial_add(rhs[iz, ia, :, sl], masks)
    sum_inside(q)
    send_z(q, lambda iz, ia, h: jnp.where(masks[2], 0.0, 1.0 / g[iz, ia, :, half_of(h)]), m1, m2)
    post(
        "gz",
        pack_z(lambda ia: g[0, ia, :, half_of(0)], False),
        pack_z(lambda ia: g[7, ia, :, half_of(1)], True),
        m1,
        m2,
        8,
    )
    lines = [[edge_lines(f, ia, h) for f in (q, g) for ia in (0, 7)] for h in range(2)]
    post("gz", lines[0], lines[1], m1, m2, 12)
    even = parity("gz")
    top, bottom = lroll(s_ref[:, half_of(1)], GROUP), s_ref[:, half_of(0)]
    m1[16] = jnp.where(even, top, bottom)
    m2[16] = jnp.where(even, bottom, top)


def with_z(f, below, above, iz, ia, h):
    v = f[iz, ia, :, half_of(h)]
    low = lane_iota() < GROUP
    if iz == 0 and h == 0:
        v = v + jnp.where(low, unpack_z(below, ia, False), 0.0)
    if iz == 7 and h == 1:
        v = v + jnp.where(low, 0.0, unpack_z(above, ia, True))
    return v


def both_z(below, above, ia):
    return jnp.where(lane_iota() < GROUP, unpack_z(below, ia, False), unpack_z(above, ia, True))


def send_a(first, q, g, z1, z2, m1, m2):
    wall = radial_masks()[2]
    q_below, q_above = got("gz", z1, z2, 0, 4)
    if first:
        g_below, g_above = got("gz", z1, z2, 8, 12)
        diag = lambda iz, ia, h: with_z(g, g_below, g_above, iz, ia, h)
        inverse = lambda iz, ia, h: jnp.where(wall, 0.0, 1.0 / diag(iz, ia, h))
    else:
        inverse = lambda iz, ia, h: g[iz, ia, :, half_of(h)]
    full = lambda iz, ia, h: with_z(q, q_below, q_above, iz, ia, h)
    post("row", pack_a(lambda h, iz: full(iz, 0, h), 0), pack_a(lambda h, iz: full(iz, 7, h), EA - 1), m1, m2, 0)
    left, right = {}, {}
    for h in range(2):
        for iz in range(8):
            scaled = [inverse(iz, ia, h) * full(iz, ia, h) for ia in range(8)]
            left[h, iz] = weighted_sum(K7[0, 1:] / THETA, scaled[1:])
            right[h, iz] = weighted_sum(K7[7, :7] / THETA, scaled[:7])
    post("row", pack_a(lambda h, iz: left[h, iz], 0), pack_a(lambda h, iz: right[h, iz], EA - 1), m1, m2, 4)


def k_first_a(q, g, s_ref, z1, z2, m1, m2):
    send_a(True, q, g, z1, z2, m1, m2)
    g_below, g_above = got("gz", z1, z2, 8, 12)
    full = lambda iz, ia, h: with_z(g, g_below, g_above, iz, ia, h)
    post("row", pack_a(lambda h, iz: full(iz, 0, h), 0), pack_a(lambda h, iz: full(iz, 7, h), EA - 1), m1, m2, 8)
    below, above = got("gz", z1, z2, 12, 16)
    post("row", [below[0], below[2], above[0], above[2]], [below[1], below[3], above[1], above[3]], m1, m2, 12)
    s_below, s_above = got("gz", z1, z2, 16, 17)
    s_z = jnp.where(lane_iota() < GROUP, s_below[0], lroll(s_above[0], GROUP))
    place = place_of()
    even = parity("row")

    def stretch_of(slot):
        parts = [s_ref[:, half_of(0)], s_ref[:, half_of(1)], s_z]
        parts = [lroll(v, (s - slot) * ER) for s, v in enumerate(parts)]
        return jnp.where(place == 0, parts[0], jnp.where(place == 1, parts[1], parts[2]))

    to_left, to_right = stretch_of(0), stretch_of(EA - 1)
    m1[16] = jnp.where(even, to_right, to_left)
    m2[16] = jnp.where(even, to_left, to_right)


def k_later_a(q, inv, z1, z2, m1, m2):
    send_a(False, q, inv, z1, z2, m1, m2)
    below, above = got("gz", z1, z2, 4, 8)
    post("row", [both_z(below, above, 0)], [both_z(below, above, 7)], m1, m2, 8)


def complete(f, z1, z2, r1, r2, start, put):
    place = place_of()
    below, above = got("gz", z1, z2, start, start + 4)
    left, right = got("row", r1, r2, start, start + 4)
    for h in range(2):
        for iz in range(8):
            for ia in range(8):
                v = with_z(f, below, above, iz, ia, h)
                if ia == 0:
                    v = v + jnp.where(place == 0, unpack_a(left, 0, h, iz), 0.0)
                if ia == 7:
                    v = v + jnp.where(place == EA - 1, unpack_a(right, EA - 1, h, iz), 0.0)
                put(iz, ia, h, v)


def halves(ghost):
    return [ghost[4], ghost[5]]


def stretch_rows(v):
    return [jnp.broadcast_to(v[k : k + 1], (8, HALF)) for k in range(3)]


def meanwhile(q, z1, z2, inverse, ghost, d, y):
    place = place_of()
    below, above = got("gz", z1, z2, 0, 4)
    for iz, ia, sl in every_fine():
        h = sl.start // HALF
        v = inverse(iz, ia, h) * with_z(q, below, above, iz, ia, h) * (1.0 / THETA)
        if ia == 0:
            v = jnp.where(place == 0, 0.0, v)
        if ia == 7:
            v = jnp.where(place == EA - 1, 0.0, v)
        d[iz, ia, :, sl] = v
    fine_apply(d, y, None, ghost, 1.0)


def k_first_mean(q, g, s_ref, z1, z2, inv, d, y):
    wall = radial_masks()[2]
    below, above = got("gz", z1, z2, 8, 12)
    for iz, ia, sl in every_fine():
        inv[iz, ia, :, sl] = jnp.where(wall, 0.0, 1.0 / with_z(g, below, above, iz, ia, sl.start // HALF))
    meanwhile(q, z1, z2, lambda iz, ia, h: inv[iz, ia, :, half_of(h)], [s_ref[:, half_of(0)], s_ref[:, half_of(1)]], d, y)


def k_later_mean(q, inv, ghost, z1, z2, d, y):
    meanwhile(q, z1, z2, lambda iz, ia, h: inv[iz, ia, :, half_of(h)], halves(ghost), d, y)


def with_face(d, face):
    def whole(iz, ia, h):
        v = d[iz, ia, :, half_of(h)]
        if ia == 0:
            v = jnp.where(place_of() == 0, face[iz, h], v)
        if ia == 7:
            v = jnp.where(place_of() == EA - 1, face[iz, h], v)
        return v

    return whole


def edge_faces(q, inv, z1, z2, r1, r2, put):
    place = place_of()
    below, above = got("gz", z1, z2, 0, 4)
    left, right = got("row", r1, r2, 0, 4)
    for h in range(2):
        for iz in range(8):
            low = with_z(q, below, above, iz, 0, h) + jnp.where(place == 0, unpack_a(left, 0, h, iz), 0.0)
            high = with_z(q, below, above, iz, 7, h) + jnp.where(place == EA - 1, unpack_a(right, EA - 1, h, iz), 0.0)
            put(iz, h, low, high)


def add_beyond(d, y0, y, face, s_own, s_n, s_z, s_m, t_left, t_right, t_z):
    place, low = place_of(), lane_iota() < GROUP
    wr, rolls = column(W7), radial_columns()
    w0, k00 = float(W7[0]), float(K7[0, 0])
    first, last = place == 0, place == EA - 1
    k_face = [jnp.where(last, float(K7[ia, 7]), float(K7[ia, 0])) for ia in range(8)]
    t_edge = []
    for h in range(2):
        sl = half_of(h)
        s0, s1, s2 = s_n[h]
        o0, o1, o2 = s_own[h]
        vals = [face[iz, h] for iz in range(8)]
        part_z = along(K7, vals)
        for iz in range(8):
            t = jnp.where(last, unpack_a(t_right, EA - 1, h, iz), unpack_a(t_left, 0, h, iz))
            if (h, iz) in ((0, 0), (1, 7)):
                t_edge.append(t)
            wz = float(W7[iz])
            part_z_w, part_r = w0 * wr * part_z[iz], (w0 * wz) * radial_apply(rolls, vals[iz])
            beyond = (s1 * wr) * (vals[iz] * k00 + t) * wz + s0 * part_z_w + s2 * part_r
            inside = o0 * part_z_w + o2 * part_r
            lines = (o1 * wr) * (vals[iz] * wz)
            for ia in range(1, 7):
                y[iz, ia, :, sl] = y0[iz, ia, :, sl] + lines * k_face[ia]
            lo = y0[iz, 0, :, sl] + lines * k_face[0] + jnp.where(first, inside, 0.0)
            hi = y0[iz, 7, :, sl] + lines * k_face[7] + jnp.where(last, inside, 0.0)
            y[iz, 0, :, sl] = lo + jnp.where(first, beyond, lroll(hi, ER))
            y[iz, 7, :, sl] = hi + jnp.where(last, beyond, lroll(lo, HALF - ER))
    t_a = jnp.where(low, t_edge[0], t_edge[1])
    vals = [jnp.where(low, d(0, ia, 0), d(7, ia, 1)) for ia in range(8)]
    part_a = along(K7, vals)
    s0, s1, s2 = s_z
    beyond = []
    for ia in range(8):
        wa = float(W7[ia])
        beyond.append((s0 * wr) * (vals[ia] * k00 + t_z[ia]) * wa + w0 * (s1 * wr * part_a[ia] + s2 * wa * radial_apply(rolls, vals[ia])))
    edge = jnp.where(place == EA - 1, vals[7], vals[0])
    edge_t = jnp.where(place == EA - 1, t_z[7], t_z[0])
    s0, s1, s2 = s_m
    corner = w0 * wr * (s0 * (edge * k00 + edge_t) + s1 * (edge * k00 + t_a)) + (w0 * w0) * s2 * radial_apply(rolls, edge)
    lo = beyond[0] + jnp.where(place > 0, lroll(beyond[7], ER), corner)
    hi = beyond[7] + jnp.where(place < EA - 1, lroll(beyond[0], -ER), corner)
    beyond[0], beyond[7] = lo, hi
    for ia in range(8):
        join_z(y, ia, beyond[ia])


def k_first_done(rhs, q, g, inv0, d, y0, s_ref, table, z1, z2, r1, r2, inv, x, rho, mid, ghost, face, y):
    masks = radial_masks()
    place, low = place_of(), lane_iota() < GROUP
    first, last = place == 0, place == EA - 1
    for iz in range(8):
        for h in range(2):
            for ia in range(1, 7):
                inv[iz, ia, :, half_of(h)] = inv0[iz, ia, :, half_of(h)]
    g_below, g_above = got("gz", z1, z2, 8, 12)
    g_left, g_right = got("row", r1, r2, 8, 12)
    for iz in range(8):
        for h in range(2):
            v = with_z(g, g_below, g_above, iz, 0, h) + jnp.where(first, unpack_a(g_left, 0, h, iz), 0.0)
            inv[iz, 0, :, half_of(h)] = jnp.where(masks[2], 0.0, 1.0 / v)
            v = with_z(g, g_below, g_above, iz, 7, h) + jnp.where(last, unpack_a(g_right, EA - 1, h, iz), 0.0)
            inv[iz, 7, :, half_of(h)] = jnp.where(masks[2], 0.0, 1.0 / v)

    def put_face(iz, h, lo, hi):
        lo, hi = inv[iz, 0, :, half_of(h)] * lo, inv[iz, 7, :, half_of(h)] * hi
        face[iz, h] = jnp.where(first, lo, jnp.where(last, hi, 0.0)) * (1.0 / THETA)

    edge_faces(q, inv, z1, z2, r1, r2, put_face)
    below, above = got("gz", z1, z2, 16, 17)
    left, right = got("row", r1, r2, 16, 17)
    ghost[2] = jnp.where(low, below[0], lroll(above[0], GROUP))
    ghost[4] = s_ref[:, half_of(0)]
    ghost[5] = s_ref[:, half_of(1)]
    for k, s in ((0, 0), (1, 1), (3, 2)):
        ghost[k] = jnp.where(place == EA - 1, lroll(right[0], (EA - 1 - s) * ER), lroll(left[0], -s * ER))
    z_lines = got("gz", z1, z2, 12, 16)
    a_lines = got("row", r1, r2, 12, 16)
    slot = lane_iota() // ER
    weight = jnp.zeros((8, HALF), jnp.float32)
    for j in range(1, 8):
        weight = jnp.where(slot == j - 1, float(K7[0, j] / THETA), weight)
    t_edge = [[None, None], [None, None]]
    for side in range(2):
        for end in range(2):
            qs = z_lines[end][side] + a_lines[side][2 * end]
            gs = z_lines[end][2 + side] + a_lines[side][2 * end + 1]
            v = jnp.where(masks[2] | (slot == 7), 0.0, weight * qs / gs)
            for shift in (64, 32, 16):
                v = v + lroll(v, shift)
            t_edge[side][end] = v
    below, above = got("gz", z1, z2, 4, 8)
    t_z = [both_z(below, above, ia) for ia in range(8)]
    t_z[0] = jnp.where(place == 0, jnp.where(low, t_edge[0][0], t_edge[0][1]), t_z[0])
    t_z[7] = jnp.where(place == EA - 1, jnp.where(low, t_edge[1][0], t_edge[1][1]), t_z[7])
    t_left, t_right = got("row", r1, r2, 4, 8)
    s_n, s_z, s_m = [stretch_rows(ghost[0]), stretch_rows(ghost[1])], stretch_rows(ghost[2]), stretch_rows(ghost[3])
    s_own = [stretch_rows(v) for v in halves(ghost)]
    whole = with_face(d, face)
    add_beyond(whole, y0, y, face, s_own, s_n, s_z, s_m, t_left, t_right, t_z)

    def put_x(iz, ia, h, v):
        sl = half_of(h)
        r = v - radial_add(y[iz, ia, :, sl], masks)
        x[iz, ia, :, sl] = (1.0 + C1) * whole(iz, ia, h) + C2 * inv[iz, ia, :, sl] * r

    complete(q, z1, z2, r1, r2, 0, put_x)
    fine_apply(x, rho, rhs, halves(ghost), -1.0)
    for iz, ia, sl in every_fine():
        y[iz, ia, :, sl] = jnp.where(masks[2], 0.0, rho[iz, ia, :, sl])
    down = jnp.dot(table[...], y[...].reshape(512, 256), preferred_element_type=jnp.float32, precision=lax.Precision.HIGHEST)
    inner = lane_iota((56, HALF)) % ER > 0
    for h in range(2):
        sl = half_of(h)
        mid[:, sl] = down[0:56, sl] + jnp.where(inner, lroll(down[56:112, sl], 1), 0.0)
    mid[48:56, :] = s_ref[...]


def k_last(q, inv, d, y0, x, ghost, z1, z2, r1, r2, out, face, y):
    masks = radial_masks()
    place = place_of()
    first, last = place == 0, place == EA - 1

    def put_face(iz, h, lo, hi):
        lo, hi = inv[iz, 0, :, half_of(h)] * lo, inv[iz, 7, :, half_of(h)] * hi
        face[iz, h] = jnp.where(first, lo, jnp.where(last, hi, 0.0)) * (1.0 / THETA)

    edge_faces(q, inv, z1, z2, r1, r2, put_face)
    below, above = got("gz", z1, z2, 4, 8)
    t_z = [both_z(below, above, ia) for ia in range(8)]
    left, right = got("row", r1, r2, 8, 9)
    t_z[0] = t_z[0] + jnp.where(first, lroll(left[0], -(EA - 1) * ER), 0.0)
    t_z[7] = t_z[7] + jnp.where(last, lroll(right[0], (EA - 1) * ER), 0.0)
    t_left, t_right = got("row", r1, r2, 4, 8)
    s_n, s_z, s_m = [stretch_rows(ghost[0]), stretch_rows(ghost[1])], stretch_rows(ghost[2]), stretch_rows(ghost[3])
    s_own = [stretch_rows(v) for v in halves(ghost)]
    whole = with_face(d, face)
    add_beyond(whole, y0, y, face, s_own, s_n, s_z, s_m, t_left, t_right, t_z)

    def put_out(iz, ia, h, v):
        sl = half_of(h)
        r = v - radial_add(y[iz, ia, :, sl], masks)
        out[iz, ia, :, sl] = x[iz, ia, :, sl] + (1.0 + C1) * whole(iz, ia, h) + C2 * inv[iz, ia, :, sl] * r

    complete(q, z1, z2, r1, r2, 0, put_out)


NODES = [(iz, ia, ir) for iz in range(3) for ia in range(3) for ir in range(3)]


def node(iz, ia, ir):
    return (iz * 3 + ia) * 3 + ir


def restrict_rows():
    picks = [(iz, ia, ir) for iz, ia, ir in NODES]
    picks += [(iz, 3, ir) for iz in range(3) for ir in range(3)]
    picks += [(3, ia, ir) for ia in range(3) for ir in range(3)]
    picks += [(3, 3, ir) for ir in range(3)]
    out = np.zeros((112, 512))
    for i, (iz, ia, ir) in enumerate(picks):
        out[i] = np.kron(np.kron(J73[:, iz], J73[:, ia]), J73[:, ir])
        if ir == 0:
            out[56 + i] = np.kron(np.kron(J73[:, iz], J73[:, ia]), J73[:, 3])
    return out.astype(np.float32)


RESTRICT = restrict_rows()
PACKED = 17


def prev_z(v):
    return sroll(v, 1)


def prev_a(v):
    return lroll(v, ER)


def prev_r(v):
    return lroll(v, 1)


def next_z(v):
    return sroll(v, -1)


def next_a(v):
    return lroll(v, -ER)


def next_r(v):
    return lroll(v, -1)


def mid_coefs(s):
    prev = (prev_z, prev_a, prev_r)
    out = []
    for direction in range(3):
        one, two = [k for k in range(3) if k != direction]
        table = {}
        for e1 in range(2):
            v = s[direction] * float(W3[e1])
            v = v + prev[one](v) if e1 == 0 else v
            for e2 in range(2):
                u = v * float(W3[e2])
                table[e1, e2] = u + prev[two](u) if e2 == 0 else u
        out.append(table)
    return out


def mid_inverse(c, inner):
    out = {}
    for ez in range(2):
        for ea in range(2):
            for er in range(2):
                total = None
                for v, e, prev in ((c[0][ea, er], ez, prev_z), (c[1][ez, er], ea, prev_a), (c[2][ez, ea], er, prev_r)):
                    term = v * float(K3[1, 1]) if e else (v + prev(v)) * float(K3[0, 0])
                    total = term if total is None else total + term
                value = 1.0 / total
                out[ez, ea, er] = value if er else jnp.where(inner, value, 0.0)
    return out


def end(i):
    return 0 if i == 0 else 1


def mid_apply(get, nz, na, nr, c, acc):
    for ia in range(3):
        for ir in range(3):
            part = along(K3, [get(0, ia, ir), get(1, ia, ir), get(2, ia, ir), nz(ia, ir)])
            part = [v * c[0][end(ia), end(ir)] for v in part]
            acc[node(0, ia, ir)] = part[0] + prev_z(part[3])
            acc[node(1, ia, ir)] = part[1]
            acc[node(2, ia, ir)] = part[2]
    for iz in range(3):
        for ir in range(3):
            part = along(K3, [get(iz, 0, ir), get(iz, 1, ir), get(iz, 2, ir), na(iz, ir)])
            part = [v * c[1][end(iz), end(ir)] for v in part]
            acc[node(iz, 0, ir)] = acc[node(iz, 0, ir)] + part[0] + prev_a(part[3])
            acc[node(iz, 1, ir)] = acc[node(iz, 1, ir)] + part[1]
            acc[node(iz, 2, ir)] = acc[node(iz, 2, ir)] + part[2]
    for iz in range(3):
        for ia in range(3):
            part = along(K3, [get(iz, ia, 0), get(iz, ia, 1), get(iz, ia, 2), nr(iz, ia)])
            part = [v * c[2][end(iz), end(ia)] for v in part]
            acc[node(iz, ia, 0)] = acc[node(iz, ia, 0)] + part[0] + prev_r(part[3])
            acc[node(iz, ia, 1)] = acc[node(iz, ia, 1)] + part[1]
            acc[node(iz, ia, 2)] = acc[node(iz, ia, 2)] + part[2]


def k_column(rows, *refs):
    blocks, out, wide = refs[:-2], refs[-2], refs[-1]
    for k, block in enumerate(blocks):
        for z in range(EZ):
            v = block[:, half_of(z // 2)]
            wide[pl.ds((2 - EZ * k + z) % rows, 56, stride=rows), :] = lroll(v, GROUP) if z % 2 else v

    def entry(i):
        return wide[i * rows : (i + 1) * rows, :]

    shape = (rows, HALF)
    lane = lane_iota(shape)
    own, face = {}, {}
    for iz, ia, ir in NODES:
        v = entry(node(iz, ia, ir))
        own[iz, ia, ir] = v + prev_z(entry(36 + ia * 3 + ir)) if iz == 0 else v
    for iz in range(3):
        for ir in range(3):
            v = entry(27 + iz * 3 + ir)
            v = v + prev_z(entry(45 + ir)) if iz == 0 else v
            face[iz * 3 + ir] = v
            own[iz, 0, ir] = own[iz, 0, ir] + jnp.where(lane >= ER, prev_a(v), 0.0)
    flat = [own[n] for n in NODES] + [entry(48 + k) for k in range(3)]
    for p in range(15):
        out[p] = jnp.where(lane < GROUP, flat[2 * p], lroll(flat[2 * p + 1], GROUP))
    for p in range(2):
        v = None
        for slot, i in enumerate(range(8 * p, min(9, 8 * p + 8))):
            moved = lroll(face[i], (slot - (EA - 1)) * ER)
            v = moved if v is None else jnp.where(lane // ER == slot, moved, v)
        out[15 + p] = v


def k_mid(own, r1, r2, coarse, res, x, inv_out, c_out, b, d, y, y2):
    rows = own.shape[1]
    even = parity("row")
    lane = lane_iota((rows, HALF))

    def sides(i):
        one, two = r1[i], r2[i]
        return jnp.where(even, two, one), jnp.where(even, one, two)

    def halo(i):
        p, base = i // 2, GROUP * (i % 2)
        left, right = sides(p)
        left, right = lroll(left, 96 - base), lroll(right, 96 - base)
        mine = lroll(own[p], 32 - base)
        first = jnp.where(lane < 32, left, jnp.where(lane < 96, mine, right))
        return first, jnp.where(lane < 32, right, left)

    for iz, ia, ir in NODES:
        n = node(iz, ia, ir)
        first, second = halo(n)
        if ia == 0:
            i = iz * 3 + ir
            left, _ = sides(15 + i // 8)
            slot = i % 8
            from_left = lroll(left, 32 - slot * ER)
            to_right = lroll(own[15 + i // 8], 96 - slot * ER)
            first = first + jnp.where((lane >= 32) & (lane < 48), from_left, jnp.where((lane >= 96) & (lane < 112), to_right, 0.0))
        b[n, :, 0:HALF] = first
        b[n, :, HALF:] = second
    s = []
    for k in range(3):
        first, second = halo(27 + k)
        second = jnp.where((lane >= 32) & (lane < 96), 1.0, second)
        coarse[1 + k] = lroll(first, -32)[:, 0:GROUP]
        s.append(jnp.concatenate([first, second], axis=1))

    inner = lane_iota((rows, 2 * HALF)) % ER > 0
    c = mid_coefs(s)
    inverse = mid_inverse(c, inner)
    for i, e in enumerate([(ez, ea, er) for ez in range(2) for ea in range(2) for er in range(2)]):
        inv_out[i] = inverse[e][0:8, 0:HALF]
    for k in range(3):
        for i, e in enumerate([(0, 0), (0, 1), (1, 0), (1, 1)]):
            c_out[4 * k + i] = c[k][e][0:8, 0:HALF]

    def kind(iz, ia, ir):
        return inverse[end(iz), end(ia), end(ir)]

    def get(iz, ia, ir):
        return d[node(iz, ia, ir)]

    for iz, ia, ir in NODES:
        n = node(iz, ia, ir)
        d[n] = kind(iz, ia, ir) * b[n] * (1.0 / THETA)
    mid_apply(
        get,
        lambda ia, ir: next_z(get(0, ia, ir)),
        lambda iz, ir: next_a(get(iz, 0, ir)),
        lambda iz, ia: next_r(get(iz, ia, 0)),
        c,
        y,
    )
    for iz, ia, ir in NODES:
        n = node(iz, ia, ir)
        d[n] = (1.0 + C1) * d[n] + C2 * kind(iz, ia, ir) * (b[n] - y[n])
        x[n] = d[n, 0:8, 0:HALF]

    def near(iz, ia, ir):
        return d[node(iz, ia, ir), :, 0:HALF]

    mid_apply(
        near,
        lambda ia, ir: next_z(near(0, ia, ir)),
        lambda iz, ir: next_a(get(iz, 0, ir))[:, 0:HALF],
        lambda iz, ia: next_r(near(iz, ia, 0)),
        [{e: v[:, 0:HALF] for e, v in t.items()} for t in c],
        y2,
    )
    inner = lane % ER > 0
    for iz, ia, ir in NODES:
        n = node(iz, ia, ir)
        r = b[n, :, 0:HALF] - y2[n]
        r = r if ir else jnp.where(inner, r, 0.0)
        y2[n] = r
        res[n] = r[0:8]

    def gather(v, prev):
        return v[0] + v[1] * float(J31[1, 0]) + v[2] * float(J31[2, 0]) + prev(v[1] * float(J31[1, 1]) + v[2] * float(J31[2, 1]))

    planes = []
    for iz in range(3):
        lines = [gather([y2[node(iz, ia, ir)] for ir in range(3)], prev_r) for ia in range(3)]
        planes.append(gather(lines, prev_a))
    vertex = jnp.where(inner, gather(planes, prev_z), 0.0)
    coarse[0] = lroll(vertex, -32)[:, 0:GROUP]


def vertex_solve(s0, s1, s2, b):
    shape = b.shape
    inner = (lane_iota(shape) % ER) > 0

    def pair(v, f):
        return v + f(v)

    edge_z = 0.5 * pair(pair(s0, prev_a), prev_r)
    edge_a = 0.5 * pair(pair(s1, prev_z), prev_r)
    edge_r = 0.5 * pair(pair(s2, prev_z), prev_a)
    back_z, back_a, back_r = prev_z(edge_z), prev_a(edge_a), prev_r(edge_r)
    middle = edge_z + back_z + edge_a + back_a + edge_r + back_r

    def operate(q):
        y = middle * q - edge_z * next_z(q) - back_z * prev_z(q)
        y = y - edge_a * next_a(q) - back_a * prev_a(q)
        y = y - edge_r * next_r(q) - back_r * prev_r(q)
        return jnp.where(inner, y, 0.0)

    def total(v):
        return jnp.sum(jnp.sum(v, axis=0, keepdims=True), axis=1, keepdims=True)

    e = jnp.zeros(shape, jnp.float32)
    r = b
    q = b
    rr = total(r * r)
    for _ in range(ITERS):
        y = operate(q)
        alpha = rr / total(q * y)
        e = e + alpha * q
        r = r - alpha * y
        rn = total(r * r)
        q = r + (rn / rr) * q
        rr = rn
    return e


def k_fifth(whole, res, xm, inv3, c_in, x, rho, inv, ghost, kron, x_out, q, m1, m2, lift, dm, rm, xs, g):
    e = vertex_solve(whole[1], whole[2], whole[3], whole[0])
    lanes = e.shape[1]
    e = pltpu.roll(e, (lanes + 32 - GROUP * lax.axis_index("row")) % lanes, 1)
    corner = {}
    for cz in range(2):
        for ca in range(2):
            for cr in range(2):
                v = next_z(e) if cz else e
                corner[cz, ca, cr] = lroll(v, -(ca * ER + cr))[0:8, 0:HALF]

    def three(a, b):
        return [a] + [a * float(J31[i, 0]) + b * float(J31[i, 1]) for i in (1, 2)]

    along_r = {(cz, ca): three(corner[cz, ca, 0], corner[cz, ca, 1]) for cz in range(2) for ca in range(2)}
    along_ra = {cz: [three(along_r[cz, 0][ir], along_r[cz, 1][ir]) for ir in range(3)] for cz in range(2)}
    beyond_a = {ir: three(along_r[0, 1][ir], along_r[1, 1][ir]) for ir in range(3)}
    for ia in range(3):
        for ir in range(3):
            for iz, v in enumerate(three(along_ra[0][ir][ia], along_ra[1][ir][ia])):
                lift[node(iz, ia, ir)] = v

    c = [{e_: c_in[4 * k + i] for i, e_ in enumerate([(0, 0), (0, 1), (1, 0), (1, 1)])} for k in range(3)]

    def kind(iz, ia, ir):
        return inv3[(end(iz) * 2 + end(ia)) * 2 + end(ir)]

    def get_lift(iz, ia, ir):
        return lift[node(iz, ia, ir)]

    def get_d(iz, ia, ir):
        return dm[node(iz, ia, ir)]

    mid_apply(
        get_lift,
        lambda ia, ir: along_ra[1][ir][ia],
        lambda iz, ir: beyond_a[ir][iz],
        lambda iz, ia: next_r(get_lift(iz, ia, 0)),
        c,
        rm,
    )
    for iz, ia, ir in NODES:
        n = node(iz, ia, ir)
        r = kind(iz, ia, ir) * (res[n] - rm[n])
        dm[n] = r * (1.0 / THETA)
        lift[n] = lift[n] + xm[n] + ((1.0 + C1) / THETA + C2) * r
    mid_apply(
        get_d,
        lambda ia, ir: next_z(get_d(0, ia, ir)),
        lambda iz, ir: next_a(get_d(iz, 0, ir)),
        lambda iz, ia: next_r(get_d(iz, ia, 0)),
        c,
        rm,
    )
    for iz, ia, ir in NODES:
        n = node(iz, ia, ir)
        lift[n] = lift[n] - C2 * kind(iz, ia, ir) * rm[n]
    for iz in range(4):
        for ia in range(4):
            for ir in range(4):
                v = lift[node(iz % 3, ia % 3, ir % 3)]
                v = lroll(v, -(ia // 3 * ER + ir // 3))
                v = next_z(v) if iz == 3 else v
                n = (iz * 4 + ia) * 4 + ir
                xs[n * 8 : (n + 1) * 8, :] = v
    low = lane_iota((64, HALF)) < GROUP
    cols = []
    for h in range(2):
        one = xs[pl.ds(2 + 2 * h, 64, stride=8), :]
        two = xs[pl.ds(3 + 2 * h, 64, stride=8), :]
        cols.append(jnp.where(low, lroll(one, -32), lroll(two, 32)))
    xe = jnp.concatenate(cols, axis=1)
    raised = jnp.dot(kron[...], xe, preferred_element_type=jnp.float32, precision=lax.Precision.HIGHEST)
    g[...] = raised.reshape(8, 8, 8, 256)
    for iz, ia, sl in every_fine():
        x_out[iz, ia, :, sl] = x[iz, ia, :, sl] + g[iz, ia, :, sl]
    masks = radial_masks()
    fine_apply(g, q, rho, halves(ghost), -1.0)
    for iz, ia, sl in every_fine():
        q[iz, ia, :, sl] = radial_add(q[iz, ia, :, sl], masks)
    sum_inside(q)
    send_z(q, lambda iz, ia, h: inv[iz, ia, :, half_of(h)], m1, m2)


FINE = (8, 8, 8, 256)


def call(body, outs, scratch=(), name=None, far=0):
    shapes = [jax.ShapeDtypeStruct(s, jnp.float32) for s in outs]
    specs = dict(in_specs=[pl.BlockSpec(memory_space=pltpu.HBM)] * far) if far else {}
    return pl.pallas_call(
        body,
        out_shape=shapes,
        scratch_shapes=[pltpu.VMEM(s, jnp.float32) for s in scratch] + ([pltpu.SemaphoreType.DMA((far,))] if far else []),
        **specs,
        compiler_params=pltpu.CompilerParams(vmem_limit_bytes=32 * 1024 * 1024),
        name=name,
    )


def per_device(gz, row, rhs, stretch):
    mate_row = [(i, i ^ 1) for i in range(row)]
    other_row = [(i, (((i + 1) ^ 1) - 1) % row) for i in range(row)]
    mate_gz = [(i, i ^ 1) for i in range(gz)]
    other_gz = [(i, (((i + 1) ^ 1) - 1) % gz) for i in range(gz)]

    def swap_a(m1, m2):
        return lax.ppermute(m1, "row", mate_row), lax.ppermute(m2, "row", other_row)

    def swap_z(m1, m2):
        return lax.ppermute(m1, "gz", mate_gz), lax.ppermute(m2, "gz", other_gz)

    def message(entries):
        return (entries, 8, HALF)

    stretch = jnp.pad(stretch, ((0, 5), (0, 0)))
    ghosts = (6, 8, HALF)
    q, g, m1, m2 = call(k_first, [FINE, FINE, message(FIRST), message(FIRST)], [(8, 256), FINE], name="first", far=2)(rhs, stretch)
    z1, z2 = swap_z(m1, m2)
    m1, m2 = call(k_first_a, [message(FIRST), message(FIRST)], name="first_a")(q, g, stretch, z1, z2)
    r1, r2 = swap_a(m1, m2)
    inv, d, y = call(k_first_mean, [FINE, FINE, FINE], name="first_mean")(q, g, stretch, z1, z2)
    faces = (8, 2, 8, HALF)
    inv, x, rho, block, ghost = call(k_first_done, [FINE, FINE, FINE, (56, 256), ghosts], [faces, FINE], name="first_done")(
        rhs, q, g, inv, d, y, stretch, jnp.asarray(RESTRICT), z1, z2, r1, r2
    )

    rows = gz * EZ
    blocks = [block] + [lax.ppermute(block, "gz", [(i, (i + k) % gz) for i in range(gz)]) for k in range(1, gz)]
    column_ = call(functools.partial(k_column, rows), [(PACKED, rows, HALF)], [(56 * rows, HALF)], name="column")(*blocks)[0]
    r1, r2 = swap_a(column_, column_)
    cube, wide = (27, 8, HALF), (27, rows, 2 * HALF)
    coarse, res, xm, inv3, c3 = call(
        k_mid,
        [(4, rows, GROUP), cube, cube, (8, 8, HALF), (12, 8, HALF)],
        [wide, wide, wide, (27, rows, HALF)],
        name="mid",
    )(column_, r1, r2)

    bit = 1
    while bit < row:
        size = 2 if bit == 1 or bit * 2 >= row else 4
        digit = (lax.axis_index("row") // bit) % size
        parts = [coarse] + [lax.ppermute(coarse, "row", [(i, i ^ (k * bit)) for i in range(row)]) for k in range(1, size)]
        ordered = []
        for place in range(size):
            v = parts[place]
            for m in range(1, size):
                v = jnp.where(digit == m, parts[place ^ m], v)
            ordered.append(v)
        coarse = jnp.concatenate(ordered, 2)
        bit *= size

    x, q, m1, m2 = call(k_fifth, [FINE, FINE, message(8), message(8)], [cube, cube, cube, (512, HALF), FINE], name="fifth")(
        coarse, res, xm, inv3, c3, x, rho, inv, ghost, jnp.asarray(KRON73)
    )
    z1, z2 = swap_z(m1, m2)
    m1, m2 = call(k_later_a, [message(LATER), message(LATER)], name="later_a")(q, inv, z1, z2)
    r1, r2 = swap_a(m1, m2)
    d, y = call(k_later_mean, [FINE, FINE], name="later_mean")(q, inv, ghost, z1, z2)
    return call(k_last, [FINE], [faces, FINE], name="last")(q, inv, d, y, x, ghost, z1, z2, r1, r2)[0]


def solution(mesh):
    gz, row = mesh.shape["gz"], mesh.shape["row"]
    return jax.shard_map(
        functools.partial(per_device, gz, row),
        mesh=mesh,
        in_specs=(P(None, None, None, ("gz", "row")), P(None, ("gz", "row"))),
        out_specs=P(None, None, None, ("gz", "row")),
        check_vma=False,
    )
```

time: 753 us -> 61.5 us (0.08); the launches traced: 743 us -> 61.3 us
  blocking collectives: 360 us -> 0 us
  local copies, waits for them, and re-layouts: 125 us -> 1.75 us
  starting transfers between devices: 109 us -> 23.1 us
  other arithmetic: 38.8 us -> 0.12 us
  waiting for transfers between devices: 55.9 us -> 23.5 us
  between operations: 32.5 us -> 0.17 us
  matrix products: 21.9 us -> 0 us
  Pallas kernels: 0 us -> 12.7 us
    psum x9 -> x0, blocking collectives: 360 us -> none  [the longest x5 209 us: squared_norm(): return lax.psum(jnp.sum(weight * values * values), ('gz', 'row'))]
    ppermute x72 -> x17, starting transfers between devices: 109 us -> 23.1 us  [the longest x4 9.27 us: swap_z(): return (lax.ppermute(m1, 'gz', mate_gz), lax.ppermute(m2, 'gz', other_gz))]
    ppermute x72 -> x17, waiting for transfers between devices: 55.9 us -> 23.5 us  [the longest x3 8.01 us: swap_a(): lax.ppermute(m2, 'row', other_row)]
    scatter x77 -> x0, local copies, waits for them, and re-layouts: 27.1 us -> none  [the longest x37 15.4 us: face_add(): moved = moved.at[size - 1].set(high_face + from_above)]
    slice x147 -> x0, local copies, waits for them, and re-layouts: 27 us -> none  [the longest x36 7.99 us: face_add(): high_edge = high_face.reshape(split_shape)[..., count - 1, :]]
    dot_general x54 -> x0, matrix products: 21.9 us -> none  [the longest x13 6.6 us: element_apply(): jnp.einsum('ij,jbc...->ibc...', stiffness, field, precision=HIGHEST)]
    unnamed x143 -> x8, local copies, waits for them, and re-layouts: 19.4 us -> 1.06 us
    broadcast_in_dim x108 -> x0, local copies, waits for them, and re-layouts: 17.6 us -> none  [the longest x54 8.78 us: face_add(): jnp.broadcast_to(padded[3][..., None, :], split_shape)]
  transfers between devices with their start and end apart: 72 -> 17, of which waited for: 41 -> 11; matrix products, arithmetic and copies ran while one was open for 9% -> 0% of each run, Pallas kernels for 0% -> 3%
where the time goes in v1:
time: 61.5 us; the launch traced here: 61.3 us
  waiting for transfers between devices  23.5 us (38%)
  starting transfers between devices  23.1 us (38%)
  Pallas kernels  12.7 us (21%)
  local copies, waits for them, and re-layouts  1.75 us (3%)
    ppermute x4, starting transfers between devices, swap_z(): return (lax.ppermute(m1, 'gz', mate_gz), lax.ppermute(m2, 'gz', other_gz))  9.27 us
    ppermute x3, waiting for transfers between devices, swap_a(): lax.ppermute(m2, 'row', other_row)  8.01 us
    ppermute x4, waiting for transfers between devices, swap_z(): return (lax.ppermute(m1, 'gz', mate_gz), lax.ppermute(m2, 'gz', other_gz))  7.62 us
    ppermute x3, starting transfers between devices, swap_a(): lax.ppermute(m2, 'row', other_row)  6.24 us
    ppermute x3, waiting for transfers between devices, per_device(): lax.ppermute(block, 'gz', [(i, (i + k) % gz) for i in range(gz)])  4.27 us
    ppermute x3, starting transfers between devices, per_device(): lax.ppermute(block, 'gz', [(i, (i + k) % gz) for i in range(gz)])  3.87 us
    pallas_call x1, Pallas kernels, per_device(): call(k_fifth, [FINE, FINE, message(8), message(8)], [cube, cube, cube, (5...  3.72 us
    ppermute x4, waiting for transfers between devices, per_device(): lax.ppermute(coarse, 'row', [(i, i ^ k * bit) for i in range(row)])  3.59 us
  transfers between devices with their start and end apart: 17, of which 11 were waited for; matrix products, arithmetic and copies ran while one was open for 0% of the time, Pallas kernels for 3%

profile of v1, /device:TPU:0, one launch (start us, length us, event | category | flops | bytes accessed | tf_op | source)
XLA Modules:
  0.0 61.3 jit_solution(4541446786758509856)
XLA Ops:
  0.0 0.7 %pad.4.s_any.s_ref = f32[8,256]{1,0:T(8,128)S(1)} pad(f32[3,256]{1,0:T(4,128)} %param.5, f32[]{:T(128)} %constant.54.clone.1), padding=0_5x0_0 | pad | bytes 11268 | tf_op jit(solution)/shard_map/jit(_pad)/pad | solution.py:995
  0.7 1.0 %copy-done = f32[8,8,8,256]{3,2,1,0:T(8,128)S(1)} copy-done((f32[8,8,8,256]{3,2,1,0:T(8,128)S(1)}, f32[8,8,8,256]{3,2,1,0:T(8,128)}, u32[]{:S(2)}) %copy-start) | copy-done | bytes 524312
  1.7 1.2 %first.1 = (f32[8,8,8,256]{3,2,1,0:T(8,128)S(1)}, f32[8,8,8,256]{3,2,1,0:T(8,128)S(1)}, f32[17,8,128]{2,1,0:T(8,128)S(1)}, f32[17,8,128]{2,1,0:T(8,128)S(1)}) custom-call(f32[8,8,8,256]{3,2,1,0:T(8,128)S(1)} %copy-done, f32[8,256]{1,0:T(8,128)S(1)} %pad.4.s_any.s_ref), custom_call_target="tpu_custom_call" | custom-call | tf_op jit(solution)/shard_map/first/pallas_call | solution.py:997
  2.9 3.1 %collective-permute-start = (f32[17,8,128]{2,1,0:T(8,128)S(1)}, f32[17,8,128]{2,1,0:T(8,128)S(1)}, u32[]{:S(2)}, u32[]{:S(2)}) collective-permute-start(f32[17,8,128]{2,1,0:T(8,128)S(1)} %get-tuple-element.34), channel_id=1, source_target_pairs={{0,8},{8,0},{16,24},{24,16},{1,9},{9,1},{17,25},{25,17},{2,10},{10... | collective-permute-start | bytes 208904 | tf_op jit(solution)/shard_map/ppermute | solution.py:990
  6.0 2.5 %collective-permute-start.1 = (f32[17,8,128]{2,1,0:T(8,128)S(1)}, f32[17,8,128]{2,1,0:T(8,128)S(1)}, u32[]{:S(2)}, u32[]{:S(2)}) collective-permute-start(f32[17,8,128]{2,1,0:T(8,128)S(1)} %get-tuple-element.35), channel_id=1, source_target_pairs={{0,24},{8,16},{16,8},{24,0},{1,25},{9,17},{17,9},{25,1},{2,26},{10... | collective-permute-start | bytes 208904 | tf_op jit(solution)/shard_map/ppermute | solution.py:990
  8.5 3.8 %collective-permute-done.1.z2 = f32[17,8,128]{2,1,0:T(8,128)S(1)} collective-permute-done((f32[17,8,128]{2,1,0:T(8,128)S(1)}, f32[17,8,128]{2,1,0:T(8,128)S(1)}, u32[]{:S(2)}, u32[]{:S(2)}) %collective-permute-start.1) | collective-permute-done | bytes 69664 | tf_op jit(solution)/shard_map/ppermute | solution.py:990
  12.6 2.5 %collective-permute-start.3 = (f32[17,8,128]{2,1,0:T(8,128)S(1)}, f32[17,8,128]{2,1,0:T(8,128)S(1)}, u32[]{:S(2)}, u32[]{:S(2)}) collective-permute-start(f32[17,8,128]{2,1,0:T(8,128)S(1)} %get-tuple-element.40), channel_id=1, source_target_pairs={{0,7},{1,2},{2,1},{3,4},{4,3},{5,6},{6,5},{7,0},{8,15},{9,10},{10,... | collective-permute-start | bytes 208904 | tf_op jit(solution)/shard_map/ppermute | solution.py:987
  15.1 0.9 %first_mean.1 = (f32[8,8,8,256]{3,2,1,0:T(8,128)S(1)}, f32[8,8,8,256]{3,2,1,0:T(8,128)S(1)}, f32[8,8,8,256]{3,2,1,0:T(8,128)S(1)}) custom-call(f32[8,8,8,256]{3,2,1,0:T(8,128)S(1)} %get-tuple-element.32.q, f32[8,8,8,256]{3,2,1,0:T(8,128)S(1)} %get-tuple-element.33.g, f32[8,256]{1,0:T(8,128)S(1)} %pad.4.s_any.s_ref, ...), custom_call_target="tpu_custom_call" | custom-call | tf_op jit(solution)/shard_map/first_mean/pallas_call | solution.py:1001
  16.1 1.4 %collective-permute-done.3.r2 = f32[17,8,128]{2,1,0:T(8,128)S(1)} collective-permute-done((f32[17,8,128]{2,1,0:T(8,128)S(1)}, f32[17,8,128]{2,1,0:T(8,128)S(1)}, u32[]{:S(2)}, u32[]{:S(2)}) %collective-permute-start.3) | collective-permute-done | bytes 69664 | tf_op jit(solution)/shard_map/ppermute | solution.py:987
  17.4 2.1 %first_done.1 = (f32[8,8,8,256]{3,2,1,0:T(8,128)S(1)}, f32[8,8,8,256]{3,2,1,0:T(8,128)S(1)}, f32[8,8,8,256]{3,2,1,0:T(8,128)S(1)}, f32[56,256]{1,0:T(8,128)S(1)}, f32[6,8,128]{2,1,0:T(8,128)S(1)}) custom-call(f32[8,8,8,256]{3,2,1,0:T(8,128)S(1)} %copy-done.1, f32[8,8,8,256]{3,2,1,0:T(8,128)S(1)} %get-tuple-element.32.q, ...), custom_call_target="tpu_custom_call" | custom-call | tf_op jit(solution)/shard_map/first_done/pallas_call | solution.py:1003
  19.6 3.0 %collective-permute-start.5 = (f32[56,256]{1,0:T(8,128)S(1)}, f32[56,256]{1,0:T(8,128)S(1)}, u32[]{:S(2)}, u32[]{:S(2)}) collective-permute-start(f32[56,256]{1,0:T(8,128)S(1)} %get-tuple-element.41.refs_0_), channel_id=1, source_target_pairs={{0,16},{8,24},{16,0},{24,8},{1,17},{9,25},{17,1},{25,9},{2,18},{10... | collective-permute-start | bytes 172040 | tf_op jit(solution)/shard_map/ppermute | solution.py:1008
  22.6 0.8 %collective-permute-start.6 = (f32[56,256]{1,0:T(8,128)S(1)}, f32[56,256]{1,0:T(8,128)S(1)}, u32[]{:S(2)}, u32[]{:S(2)}) collective-permute-start(f32[56,256]{1,0:T(8,128)S(1)} %get-tuple-element.41.refs_0_), channel_id=1, source_target_pairs={{0,24},{8,0},{16,8},{24,16},{1,25},{9,1},{17,9},{25,17},{2,26},{10... | collective-permute-start | bytes 172040 | tf_op jit(solution)/shard_map/ppermute | solution.py:1008
  23.4 2.7 %collective-permute-done.4.refs_1_ = f32[56,256]{1,0:T(8,128)S(1)} collective-permute-done((f32[56,256]{1,0:T(8,128)S(1)}, f32[56,256]{1,0:T(8,128)S(1)}, u32[]{:S(2)}, u32[]{:S(2)}) %collective-permute-start.4) | collective-permute-done | bytes 57376 | tf_op jit(solution)/shard_map/ppermute | solution.py:1008
  26.2 1.5 %collective-permute-done.5.refs_2_ = f32[56,256]{1,0:T(8,128)S(1)} collective-permute-done((f32[56,256]{1,0:T(8,128)S(1)}, f32[56,256]{1,0:T(8,128)S(1)}, u32[]{:S(2)}, u32[]{:S(2)}) %collective-permute-start.5) | collective-permute-done | bytes 57376 | tf_op jit(solution)/shard_map/ppermute | solution.py:1008
  27.7 0.3 column.1.own
  28.1 1.8 %collective-permute-start.8 = (f32[17,16,128]{2,1,0:T(8,128)S(1)}, f32[17,16,128]{2,1,0:T(8,128)S(1)}, u32[]{:S(2)}, u32[]{:S(2)}) collective-permute-start(f32[17,16,128]{2,1,0:T(8,128)S(1)} %column.1.own), channel_id=1, source_target_pairs={{0,7},{1,2},{2,1},{3,4},{4,3},{5,6},{6,5},{7,0},{8,15},{9,10},{10,... | collective-permute-start | bytes 417800 | tf_op jit(solution)/shard_map/ppermute | solution.py:987
  29.9 4.9 %collective-permute-done.8.r2 = f32[17,16,128]{2,1,0:T(8,128)S(1)} collective-permute-done((f32[17,16,128]{2,1,0:T(8,128)S(1)}, f32[17,16,128]{2,1,0:T(8,128)S(1)}, u32[]{:S(2)}, u32[]{:S(2)}) %collective-permute-start.8) | collective-permute-done | bytes 139296 | tf_op jit(solution)/shard_map/ppermute | solution.py:987
  34.8 1.7 %mid.1 = (f32[4,16,64]{2,1,0:T(8,128)S(1)}, f32[27,8,128]{2,1,0:T(8,128)S(1)}, f32[27,8,128]{2,1,0:T(8,128)S(1)}, f32[8,8,128]{2,1,0:T(8,128)S(1)}, f32[12,8,128]{2,1,0:T(8,128)S(1)}) custom-call(f32[17,16,128]{2,1,0:T(8,128)S(1)} %column.1.own, f32[17,16,128]{2,1,0:T(8,128)S(1)} %collective-permute-done.7.r1, f32[17,16,128]{2,1,0:T(8,128)S(1)} %collective-permute-done.8.r2), custom_call_target="tpu_custom_call" | custom-call | tf_op jit(solution)/shard_map/mid/pallas_call | solution.py:1012
  36.5 1.2 %collective-permute-done.9 = f32[4,16,64]{2,1,0:T(8,128)S(1)} collective-permute-done((f32[4,16,64]{2,1,0:T(8,128)S(1)}, f32[4,16,64]{2,1,0:T(8,128)S(1)}, u32[]{:S(2)}, u32[]{:S(2)}) %collective-permute-start.9) | collective-permute-done | bytes 16416 | tf_op jit(solution)/shard_map/ppermute | solution.py:1023
  37.8 0.8 %collective-permute-start.10 = (f32[4,16,128]{2,1,0:T(8,128)S(1)}, f32[4,16,128]{2,1,0:T(8,128)S(1)}, u32[]{:S(2)}, u32[]{:S(2)}) collective-permute-start(f32[4,16,128]{2,1,0:T(8,128)S(1)} %pad_maximum_fusion.1), channel_id=1, source_target_pairs={{0,6},{1,7},{2,4},{3,5},{4,2},{5,3},{6,0},{7,1},{8,14},{9,15},{10,... | collective-permute-start | bytes 98312 | tf_op jit(solution)/shard_map/ppermute | solution.py:1023
  38.6 1.2 %collective-permute-start.11 = (f32[4,16,128]{2,1,0:T(8,128)S(1)}, f32[4,16,128]{2,1,0:T(8,128)S(1)}, u32[]{:S(2)}, u32[]{:S(2)}) collective-permute-start(f32[4,16,128]{2,1,0:T(8,128)S(1)} %pad_maximum_fusion.1), channel_id=1, source_target_pairs={{0,4},{1,5},{2,6},{3,7},{4,0},{5,1},{6,2},{7,3},{8,12},{9,13},{10,... | collective-permute-start | bytes 98312 | tf_op jit(solution)/shard_map/ppermute | solution.py:1023
  39.8 1.5 %collective-permute-start.12 = (f32[4,16,128]{2,1,0:T(8,128)S(1)}, f32[4,16,128]{2,1,0:T(8,128)S(1)}, u32[]{:S(2)}, u32[]{:S(2)}) collective-permute-start(f32[4,16,128]{2,1,0:T(8,128)S(1)} %pad_maximum_fusion.1), channel_id=1, source_target_pairs={{0,2},{1,3},{2,0},{3,1},{4,6},{5,7},{6,4},{7,5},{8,10},{9,11},{10,... | collective-permute-start | bytes 98312 | tf_op jit(solution)/shard_map/ppermute | solution.py:1023
  41.3 1.7 %collective-permute-done.10 = f32[4,16,128]{2,1,0:T(8,128)S(1)} collective-permute-done((f32[4,16,128]{2,1,0:T(8,128)S(1)}, f32[4,16,128]{2,1,0:T(8,128)S(1)}, u32[]{:S(2)}, u32[]{:S(2)}) %collective-permute-start.10) | collective-permute-done | bytes 32800 | tf_op jit(solution)/shard_map/ppermute | solution.py:1023
  42.9 0.8 %collective-permute-done.12 = f32[4,16,128]{2,1,0:T(8,128)S(1)} collective-permute-done((f32[4,16,128]{2,1,0:T(8,128)S(1)}, f32[4,16,128]{2,1,0:T(8,128)S(1)}, u32[]{:S(2)}, u32[]{:S(2)}) %collective-permute-start.12) | collective-permute-done | bytes 32800 | tf_op jit(solution)/shard_map/ppermute | solution.py:1023
  43.8 3.7 %fifth.1 = (f32[8,8,8,256]{3,2,1,0:T(8,128)S(1)}, f32[8,8,8,256]{3,2,1,0:T(8,128)S(1)}, f32[8,8,128]{2,1,0:T(8,128)S(1)}, f32[8,8,128]{2,1,0:T(8,128)S(1)}) custom-call(f32[4,16,512]{2,1,0:T(8,128)S(1)} %pad_maximum_fusion.whole, f32[27,8,128]{2,1,0:T(8,128)S(1)} %get-tuple-element.43.res, f32[27,8,128]{2,1,0:T(8,128)S(1)} %get-tuple-element.44.xm, ...), custom_call_target="tpu_custom_call" | custom-call | tf_op jit(solution)/shard_map/fifth/pallas_call | solution.py:1033
  47.5 1.8 %collective-permute-start.13 = (f32[8,8,128]{2,1,0:T(8,128)S(1)}, f32[8,8,128]{2,1,0:T(8,128)S(1)}, u32[]{:S(2)}, u32[]{:S(2)}) collective-permute-start(f32[8,8,128]{2,1,0:T(8,128)S(1)} %get-tuple-element.52), channel_id=1, source_target_pairs={{0,8},{8,0},{16,24},{24,16},{1,9},{9,1},{17,25},{25,17},{2,10},{10... | collective-permute-start | bytes 98312 | tf_op jit(solution)/shard_map/ppermute | solution.py:990
  49.3 1.9 %collective-permute-start.14 = (f32[8,8,128]{2,1,0:T(8,128)S(1)}, f32[8,8,128]{2,1,0:T(8,128)S(1)}, u32[]{:S(2)}, u32[]{:S(2)}) collective-permute-start(f32[8,8,128]{2,1,0:T(8,128)S(1)} %get-tuple-element.53), channel_id=1, source_target_pairs={{0,24},{8,16},{16,8},{24,0},{1,25},{9,17},{17,9},{25,1},{2,26},{10... | collective-permute-start | bytes 98312 | tf_op jit(solution)/shard_map/ppermute | solution.py:990
  51.5 3.6 %collective-permute-done.14.z2 = f32[8,8,128]{2,1,0:T(8,128)S(1)} collective-permute-done((f32[8,8,128]{2,1,0:T(8,128)S(1)}, f32[8,8,128]{2,1,0:T(8,128)S(1)}, u32[]{:S(2)}, u32[]{:S(2)}) %collective-permute-start.14) | collective-permute-done | bytes 32800 | tf_op jit(solution)/shard_map/ppermute | solution.py:990
  55.3 1.9 %collective-permute-start.16 = (f32[9,8,128]{2,1,0:T(8,128)S(1)}, f32[9,8,128]{2,1,0:T(8,128)S(1)}, u32[]{:S(2)}, u32[]{:S(2)}) collective-permute-start(f32[9,8,128]{2,1,0:T(8,128)S(1)} %get-tuple-element.58), channel_id=1, source_target_pairs={{0,7},{1,2},{2,1},{3,4},{4,3},{5,6},{6,5},{7,0},{8,15},{9,10},{10,... | collective-permute-start | bytes 110600 | tf_op jit(solution)/shard_map/ppermute | solution.py:987
  57.2 0.9 %later_mean.1 = (f32[8,8,8,256]{3,2,1,0:T(8,128)S(1)}, f32[8,8,8,256]{3,2,1,0:T(8,128)S(1)}) custom-call(f32[8,8,8,256]{3,2,1,0:T(8,128)S(1)} %get-tuple-element.51.q, f32[8,8,8,256]{3,2,1,0:T(8,128)S(1)} %get-tuple-element.49.inv, f32[6,8,128]{2,1,0:T(8,128)S(1)} %get-tuple-element.50.ghost, f32[8,8,128]{2,1,0:T(8,128)S(1)} %collective-permute-done.13.z1, ...), custom_call_target="tpu_custom_call" | custom-call | tf_op jit(solution)/shard_map/later_mean/pallas_call | solution.py:1039
  58.1 1.7 %collective-permute-done.16.r2 = f32[9,8,128]{2,1,0:T(8,128)S(1)} collective-permute-done((f32[9,8,128]{2,1,0:T(8,128)S(1)}, f32[9,8,128]{2,1,0:T(8,128)S(1)}, u32[]{:S(2)}, u32[]{:S(2)}) %collective-permute-start.16) | collective-permute-done | bytes 36896 | tf_op jit(solution)/shard_map/ppermute | solution.py:987
  59.8 1.5 %last.1 = f32[8,8,8,256]{3,2,1,0:T(8,128)} custom-call(f32[8,8,8,256]{3,2,1,0:T(8,128)S(1)} %get-tuple-element.51.q, f32[8,8,8,256]{3,2,1,0:T(8,128)S(1)} %get-tuple-element.49.inv, f32[8,8,8,256]{3,2,1,0:T(8,128)S(1)} %get-tuple-element.54.d, f32[8,8,8,256]{3,2,1,0:T(8,128)S(1)} %get-tuple-element.55.y0, f32[8,8,8,256]{3,2,1,0:T(8,128)S(1)} %get-tuple-element.56.x, ...), custom_call_target="tpu_custom_call" | custom-call | tf_op jit(solution)/shard_map/last/pallas_call | solution.py:1040
  (25 shorter events, 1.1 us)
Async XLA Ops:
  0.7 1.0 %copy-start = (f32[8,8,8,256]{3,2,1,0:T(8,128)S(1)}, f32[8,8,8,256]{3,2,1,0:T(8,128)}, u32[]{:S(2)}) copy-start(f32[8,8,8,256]{3,2,1,0:T(8,128)} %rhs.1) | copy-start | bytes 1572868
  2.9 5.6 %collective-permute-start = (f32[17,8,128]{2,1,0:T(8,128)S(1)}, f32[17,8,128]{2,1,0:T(8,128)S(1)}, u32[]{:S(2)}, u32[]{:S(2)}) collective-permute-start(f32[17,8,128]{2,1,0:T(8,128)S(1)} %get-tuple-element.34), channel_id=1, source_target_pairs={{0,8},{8,0},{16,24},{24,16},{1,9},{9,1},{17,25},{25,17},{2,10},{10... | collective-permute-start | bytes 208904 | tf_op jit(solution)/shard_map/ppermute | solution.py:990
  6.0 6.2 %collective-permute-start.1 = (f32[17,8,128]{2,1,0:T(8,128)S(1)}, f32[17,8,128]{2,1,0:T(8,128)S(1)}, u32[]{:S(2)}, u32[]{:S(2)}) collective-permute-start(f32[17,8,128]{2,1,0:T(8,128)S(1)} %get-tuple-element.35), channel_id=1, source_target_pairs={{0,24},{8,16},{16,8},{24,0},{1,25},{9,17},{17,9},{25,1},{2,26},{10... | collective-permute-start | bytes 208904 | tf_op jit(solution)/shard_map/ppermute | solution.py:990
  12.5 3.6 %collective-permute-start.2 = (f32[17,8,128]{2,1,0:T(8,128)S(1)}, f32[17,8,128]{2,1,0:T(8,128)S(1)}, u32[]{:S(2)}, u32[]{:S(2)}) collective-permute-start(f32[17,8,128]{2,1,0:T(8,128)S(1)} %get-tuple-element.39), channel_id=1, source_target_pairs={{0,1},{1,0},{2,3},{3,2},{4,5},{5,4},{6,7},{7,6},{8,9},{9,8},{10,11... | collective-permute-start | bytes 208904 | tf_op jit(solution)/shard_map/ppermute | solution.py:987
  12.6 4.9 %copy-start.1 = (f32[8,8,8,256]{3,2,1,0:T(8,128)S(1)}, f32[8,8,8,256]{3,2,1,0:T(8,128)}, u32[]{:S(2)}) copy-start(f32[8,8,8,256]{3,2,1,0:T(8,128)} %rhs.1) | copy-start | bytes 1572868
  12.6 4.9 %copy-start.3 = (f32[112,512]{1,0:T(8,128)S(1)}, f32[112,512]{1,0:T(8,128)}, u32[]{:S(2)}) copy-start(f32[112,512]{1,0:T(8,128)} %constant.55.clone.table) | copy-start | bytes 688132
  12.6 4.8 %collective-permute-start.3 = (f32[17,8,128]{2,1,0:T(8,128)S(1)}, f32[17,8,128]{2,1,0:T(8,128)S(1)}, u32[]{:S(2)}, u32[]{:S(2)}) collective-permute-start(f32[17,8,128]{2,1,0:T(8,128)S(1)} %get-tuple-element.40), channel_id=1, source_target_pairs={{0,7},{1,2},{2,1},{3,4},{4,3},{5,6},{6,5},{7,0},{8,15},{9,10},{10,... | collective-permute-start | bytes 208904 | tf_op jit(solution)/shard_map/ppermute | solution.py:987
  19.5 6.6 %collective-permute-start.4 = (f32[56,256]{1,0:T(8,128)S(1)}, f32[56,256]{1,0:T(8,128)S(1)}, u32[]{:S(2)}, u32[]{:S(2)}) collective-permute-start(f32[56,256]{1,0:T(8,128)S(1)} %get-tuple-element.41.refs_0_), channel_id=1, source_target_pairs={{0,8},{8,16},{16,24},{24,0},{1,9},{9,17},{17,25},{25,1},{2,10},{10... | collective-permute-start | bytes 172040 | tf_op jit(solution)/shard_map/ppermute | solution.py:1008
  19.6 8.1 %collective-permute-start.5 = (f32[56,256]{1,0:T(8,128)S(1)}, f32[56,256]{1,0:T(8,128)S(1)}, u32[]{:S(2)}, u32[]{:S(2)}) collective-permute-start(f32[56,256]{1,0:T(8,128)S(1)} %get-tuple-element.41.refs_0_), channel_id=1, source_target_pairs={{0,16},{8,24},{16,0},{24,8},{1,17},{9,25},{17,1},{25,9},{2,18},{10... | collective-permute-start | bytes 172040 | tf_op jit(solution)/shard_map/ppermute | solution.py:1008
  22.6 5.1 %collective-permute-start.6 = (f32[56,256]{1,0:T(8,128)S(1)}, f32[56,256]{1,0:T(8,128)S(1)}, u32[]{:S(2)}, u32[]{:S(2)}) collective-permute-start(f32[56,256]{1,0:T(8,128)S(1)} %get-tuple-element.41.refs_0_), channel_id=1, source_target_pairs={{0,24},{8,0},{16,8},{24,16},{1,25},{9,1},{17,9},{25,17},{2,26},{10... | collective-permute-start | bytes 172040 | tf_op jit(solution)/shard_map/ppermute | solution.py:1008
  28.0 1.9 %collective-permute-start.7 = (f32[17,16,128]{2,1,0:T(8,128)S(1)}, f32[17,16,128]{2,1,0:T(8,128)S(1)}, u32[]{:S(2)}, u32[]{:S(2)}) collective-permute-start(f32[17,16,128]{2,1,0:T(8,128)S(1)} %column.1.own), channel_id=1, source_target_pairs={{0,1},{1,0},{2,3},{3,2},{4,5},{5,4},{6,7},{7,6},{8,9},{9,8},{10,11... | collective-permute-start | bytes 417800 | tf_op jit(solution)/shard_map/ppermute | solution.py:987
  28.1 6.8 %collective-permute-start.8 = (f32[17,16,128]{2,1,0:T(8,128)S(1)}, f32[17,16,128]{2,1,0:T(8,128)S(1)}, u32[]{:S(2)}, u32[]{:S(2)}) collective-permute-start(f32[17,16,128]{2,1,0:T(8,128)S(1)} %column.1.own), channel_id=1, source_target_pairs={{0,7},{1,2},{2,1},{3,4},{4,3},{5,6},{6,5},{7,0},{8,15},{9,10},{10,... | collective-permute-start | bytes 417800 | tf_op jit(solution)/shard_map/ppermute | solution.py:987
  36.5 1.2 %collective-permute-start.9 = (f32[4,16,64]{2,1,0:T(8,128)S(1)}, f32[4,16,64]{2,1,0:T(8,128)S(1)}, u32[]{:S(2)}, u32[]{:S(2)}) collective-permute-start(f32[4,16,64]{2,1,0:T(8,128)S(1)} %get-tuple-element.42), channel_id=1, source_target_pairs={{0,1},{1,0},{2,3},{3,2},{4,5},{5,4},{6,7},{7,6},{8,9},{9,8},{10,11... | collective-permute-start | bytes 49160 | tf_op jit(solution)/shard_map/ppermute | solution.py:1023
  37.8 5.2 %collective-permute-start.10 = (f32[4,16,128]{2,1,0:T(8,128)S(1)}, f32[4,16,128]{2,1,0:T(8,128)S(1)}, u32[]{:S(2)}, u32[]{:S(2)}) collective-permute-start(f32[4,16,128]{2,1,0:T(8,128)S(1)} %pad_maximum_fusion.1), channel_id=1, source_target_pairs={{0,6},{1,7},{2,4},{3,5},{4,2},{5,3},{6,0},{7,1},{8,14},{9,15},{10,... | collective-permute-start | bytes 98312 | tf_op jit(solution)/shard_map/ppermute | solution.py:1023
  38.6 4.4 %collective-permute-start.11 = (f32[4,16,128]{2,1,0:T(8,128)S(1)}, f32[4,16,128]{2,1,0:T(8,128)S(1)}, u32[]{:S(2)}, u32[]{:S(2)}) collective-permute-start(f32[4,16,128]{2,1,0:T(8,128)S(1)} %pad_maximum_fusion.1), channel_id=1, source_target_pairs={{0,4},{1,5},{2,6},{3,7},{4,0},{5,1},{6,2},{7,3},{8,12},{9,13},{10,... | collective-permute-start | bytes 98312 | tf_op jit(solution)/shard_map/ppermute | solution.py:1023
  39.8 3.9 %collective-permute-start.12 = (f32[4,16,128]{2,1,0:T(8,128)S(1)}, f32[4,16,128]{2,1,0:T(8,128)S(1)}, u32[]{:S(2)}, u32[]{:S(2)}) collective-permute-start(f32[4,16,128]{2,1,0:T(8,128)S(1)} %pad_maximum_fusion.1), channel_id=1, source_target_pairs={{0,2},{1,3},{2,0},{3,1},{4,6},{5,7},{6,4},{7,5},{8,10},{9,11},{10,... | collective-permute-start | bytes 98312 | tf_op jit(solution)/shard_map/ppermute | solution.py:1023
  41.3 2.5 %copy-start.2 = (f32[512,64]{1,0:T(8,128)S(1)}, f32[512,64]{1,0:T(8,128)}, u32[]{:S(2)}) copy-start(f32[512,64]{1,0:T(8,128)} %constant.56.clone.kron) | copy-start | bytes 393220
  47.5 4.0 %collective-permute-start.13 = (f32[8,8,128]{2,1,0:T(8,128)S(1)}, f32[8,8,128]{2,1,0:T(8,128)S(1)}, u32[]{:S(2)}, u32[]{:S(2)}) collective-permute-start(f32[8,8,128]{2,1,0:T(8,128)S(1)} %get-tuple-element.52), channel_id=1, source_target_pairs={{0,8},{8,0},{16,24},{24,16},{1,9},{9,1},{17,25},{25,17},{2,10},{10... | collective-permute-start | bytes 98312 | tf_op jit(solution)/shard_map/ppermute | solution.py:990
  49.3 5.7 %collective-permute-start.14 = (f32[8,8,128]{2,1,0:T(8,128)S(1)}, f32[8,8,128]{2,1,0:T(8,128)S(1)}, u32[]{:S(2)}, u32[]{:S(2)}) collective-permute-start(f32[8,8,128]{2,1,0:T(8,128)S(1)} %get-tuple-element.53), channel_id=1, source_target_pairs={{0,24},{8,16},{16,8},{24,0},{1,25},{9,17},{17,9},{25,1},{2,26},{10... | collective-permute-start | bytes 98312 | tf_op jit(solution)/shard_map/ppermute | solution.py:990
  55.2 2.8 %collective-permute-start.15 = (f32[9,8,128]{2,1,0:T(8,128)S(1)}, f32[9,8,128]{2,1,0:T(8,128)S(1)}, u32[]{:S(2)}, u32[]{:S(2)}) collective-permute-start(f32[9,8,128]{2,1,0:T(8,128)S(1)} %get-tuple-element.57), channel_id=1, source_target_pairs={{0,1},{1,0},{2,3},{3,2},{4,5},{5,4},{6,7},{7,6},{8,9},{9,8},{10,11... | collective-permute-start | bytes 110600 | tf_op jit(solution)/shard_map/ppermute | solution.py:987
  55.3 4.5 %collective-permute-start.16 = (f32[9,8,128]{2,1,0:T(8,128)S(1)}, f32[9,8,128]{2,1,0:T(8,128)S(1)}, u32[]{:S(2)}, u32[]{:S(2)}) collective-permute-start(f32[9,8,128]{2,1,0:T(8,128)S(1)} %get-tuple-element.58), channel_id=1, source_target_pairs={{0,7},{1,2},{2,1},{3,4},{4,3},{5,6},{6,5},{7,0},{8,15},{9,10},{10,... | collective-permute-start | bytes 110600 | tf_op jit(solution)/shard_map/ppermute | solution.py:987

commit v2 on v1

--- a/solution.py
+++ b/solution.py
@@ -61,7 +61,15 @@
 W3, K3 = tables_of(3)
 J73 = interp_of(7, 3)
 J31 = interp_of(3, 1)
-KRON73 = np.kron(np.kron(J73, J73), J73).astype(np.float32)
+
+
+def halves_of(table):
+    high = table.astype(jnp.bfloat16)
+    return high, (table - high.astype(np.float64)).astype(jnp.bfloat16)
+
+
+KRON_HIGH, KRON_LOW = halves_of(np.kron(np.kron(J73, J73), J73))
+KRON73 = np.concatenate([KRON_HIGH, KRON_HIGH, KRON_LOW], axis=1)
 
 
 def weighted_sum(coefs, vals):
@@ -86,6 +94,11 @@
     return out
 
 
+def pair_of(v):
+    high = v.astype(jnp.bfloat16)
+    return high, (v - high.astype(jnp.float32)).astype(jnp.bfloat16)
+
+
 def sub_iota(shape=(8, HALF)):
     return lax.broadcasted_iota(jnp.int32, shape, len(shape) - 2)
 
@@ -147,7 +160,7 @@
 def fine_apply(src, dst, base, s_half, sign):
     rolls = radial_columns()
     wr = column(W7)
-    for h in range(2):
+    for h in range(len(s_half)):
         sl = half_of(h)
         s0, s1, s2 = [v * sign for v in stretch_rows(s_half[h])]
         s0, s1 = s0 * wr, s1 * wr
@@ -266,10 +279,9 @@
 FIRST, LATER = 17, 9
 
 
-def send_z(q, inverse, m1, m2):
+def faces_z(q, inverse):
     top_q = pack_z(lambda ia: q[7, ia, :, half_of(1)], True)
     bottom_q = pack_z(lambda ia: q[0, ia, :, half_of(0)], False)
-    post("gz", bottom_q, top_q, m1, m2, 0)
 
     def behind(ia, h):
         nodes = range(7) if h else range(1, 8)
@@ -278,7 +290,7 @@
 
     top_t = pack_z(lambda ia: behind(ia, 1), True)
     bottom_t = pack_z(lambda ia: behind(ia, 0), False)
-    post("gz", bottom_t, top_t, m1, m2, 4)
+    return bottom_q + bottom_t, top_q + top_t
 
 
 def edge_lines(f, ia, h):
@@ -306,7 +318,8 @@
     for iz, ia, sl in every_fine():
         q[iz, ia, :, sl] = radial_add(rhs[iz, ia, :, sl], masks)
     sum_inside(q)
-    send_z(q, lambda iz, ia, h: jnp.where(masks[2], 0.0, 1.0 / g[iz, ia, :, half_of(h)]), m1, m2)
+    bottom, top = faces_z(q, lambda iz, ia, h: jnp.where(masks[2], 0.0, 1.0 / g[iz, ia, :, half_of(h)]))
+    post("gz", bottom, top, m1, m2, 0)
     post(
         "gz",
         pack_z(lambda ia: g[0, ia, :, half_of(0)], False),
@@ -323,13 +336,13 @@
     m2[16] = jnp.where(even, bottom, top)
 
 
-def with_z(f, below, above, iz, ia, h):
+def with_z(f, beyond, iz, ia, h):
     v = f[iz, ia, :, half_of(h)]
     low = lane_iota() < GROUP
     if iz == 0 and h == 0:
-        v = v + jnp.where(low, unpack_z(below, ia, False), 0.0)
+        v = v + jnp.where(low, beyond[ia], 0.0)
     if iz == 7 and h == 1:
-        v = v + jnp.where(low, 0.0, unpack_z(above, ia, True))
+        v = v + jnp.where(low, 0.0, beyond[ia])
     return v
 
 
@@ -337,16 +350,13 @@
     return jnp.where(lane_iota() < GROUP, unpack_z(below, ia, False), unpack_z(above, ia, True))
 
 
-def send_a(first, q, g, z1, z2, m1, m2):
-    wall = radial_masks()[2]
-    q_below, q_above = got("gz", z1, z2, 0, 4)
-    if first:
-        g_below, g_above = got("gz", z1, z2, 8, 12)
-        diag = lambda iz, ia, h: with_z(g, g_below, g_above, iz, ia, h)
-        inverse = lambda iz, ia, h: jnp.where(wall, 0.0, 1.0 / diag(iz, ia, h))
-    else:
-        inverse = lambda iz, ia, h: g[iz, ia, :, half_of(h)]
-    full = lambda iz, ia, h: with_z(q, q_below, q_above, iz, ia, h)
+def from_z(z1, z2, start):
+    below, above = got("gz", z1, z2, start, start + 4)
+    return [both_z(below, above, ia) for ia in range(8)]
+
+
+def send_a(q, qz, inverse, m1, m2):
+    full = lambda iz, ia, h: with_z(q, qz, iz, ia, h)
     post("row", pack_a(lambda h, iz: full(iz, 0, h), 0), pack_a(lambda h, iz: full(iz, 7, h), EA - 1), m1, m2, 0)
     left, right = {}, {}
     for h in range(2):
@@ -358,9 +368,10 @@
 
 
 def k_first_a(q, g, s_ref, z1, z2, m1, m2):
-    send_a(True, q, g, z1, z2, m1, m2)
-    g_below, g_above = got("gz", z1, z2, 8, 12)
-    full = lambda iz, ia, h: with_z(g, g_below, g_above, iz, ia, h)
+    wall = radial_masks()[2]
+    gz = from_z(z1, z2, 8)
+    full = lambda iz, ia, h: with_z(g, gz, iz, ia, h)
+    send_a(q, from_z(z1, z2, 0), lambda iz, ia, h: jnp.where(wall, 0.0, 1.0 / full(iz, ia, h)), m1, m2)
     post("row", pack_a(lambda h, iz: full(iz, 0, h), 0), pack_a(lambda h, iz: full(iz, 7, h), EA - 1), m1, m2, 8)
     below, above = got("gz", z1, z2, 12, 16)
     post("row", [below[0], below[2], above[0], above[2]], [below[1], below[3], above[1], above[3]], m1, m2, 12)
@@ -379,20 +390,13 @@
     m2[16] = jnp.where(even, to_left, to_right)
 
 
-def k_later_a(q, inv, z1, z2, m1, m2):
-    send_a(False, q, inv, z1, z2, m1, m2)
-    below, above = got("gz", z1, z2, 4, 8)
-    post("row", [both_z(below, above, 0)], [both_z(below, above, 7)], m1, m2, 8)
-
-
-def complete(f, z1, z2, r1, r2, start, put):
+def complete(f, fz, r1, r2, start, put):
     place = place_of()
-    below, above = got("gz", z1, z2, start, start + 4)
     left, right = got("row", r1, r2, start, start + 4)
     for h in range(2):
         for iz in range(8):
             for ia in range(8):
-                v = with_z(f, below, above, iz, ia, h)
+                v = with_z(f, fz, iz, ia, h)
                 if ia == 0:
                     v = v + jnp.where(place == 0, unpack_a(left, 0, h, iz), 0.0)
                 if ia == 7:
@@ -408,12 +412,11 @@
     return [jnp.broadcast_to(v[k : k + 1], (8, HALF)) for k in range(3)]
 
 
-def meanwhile(q, z1, z2, inverse, ghost, d, y):
+def meanwhile(q, qz, inverse, ghost, d, y):
     place = place_of()
-    below, above = got("gz", z1, z2, 0, 4)
     for iz, ia, sl in every_fine():
         h = sl.start // HALF
-        v = inverse(iz, ia, h) * with_z(q, below, above, iz, ia, h) * (1.0 / THETA)
+        v = inverse(iz, ia, h) * with_z(q, qz, iz, ia, h) * (1.0 / THETA)
         if ia == 0:
             v = jnp.where(place == 0, 0.0, v)
         if ia == 7:
@@ -424,14 +427,14 @@
 
 def k_first_mean(q, g, s_ref, z1, z2, inv, d, y):
     wall = radial_masks()[2]
-    below, above = got("gz", z1, z2, 8, 12)
+    gz = from_z(z1, z2, 8)
     for iz, ia, sl in every_fine():
-        inv[iz, ia, :, sl] = jnp.where(wall, 0.0, 1.0 / with_z(g, below, above, iz, ia, sl.start // HALF))
-    meanwhile(q, z1, z2, lambda iz, ia, h: inv[iz, ia, :, half_of(h)], [s_ref[:, half_of(0)], s_ref[:, half_of(1)]], d, y)
-
-
-def k_later_mean(q, inv, ghost, z1, z2, d, y):
-    meanwhile(q, z1, z2, lambda iz, ia, h: inv[iz, ia, :, half_of(h)], halves(ghost), d, y)
+        inv[iz, ia, :, sl] = jnp.where(wall, 0.0, 1.0 / with_z(g, gz, iz, ia, sl.start // HALF))
+    meanwhile(q, from_z(z1, z2, 0), lambda iz, ia, h: inv[iz, ia, :, half_of(h)], [s_ref[:, half_of(0)], s_ref[:, half_of(1)]], d, y)
+
+
+def k_later_mean(q, inv, ghost, qz, d, y):
+    meanwhile(q, qz, lambda iz, ia, h: inv[iz, ia, :, half_of(h)], halves(ghost), d, y)
 
 
 def with_face(d, face):
@@ -446,14 +449,13 @@
     return whole
 
 
-def edge_faces(q, inv, z1, z2, r1, r2, put):
+def edge_faces(q, qz, r1, r2, put):
     place = place_of()
-    below, above = got("gz", z1, z2, 0, 4)
     left, right = got("row", r1, r2, 0, 4)
     for h in range(2):
         for iz in range(8):
-            low = with_z(q, below, above, iz, 0, h) + jnp.where(place == 0, unpack_a(left, 0, h, iz), 0.0)
-            high = with_z(q, below, above, iz, 7, h) + jnp.where(place == EA - 1, unpack_a(right, EA - 1, h, iz), 0.0)
+            low = with_z(q, qz, iz, 0, h) + jnp.where(place == 0, unpack_a(left, 0, h, iz), 0.0)
+            high = with_z(q, qz, iz, 7, h) + jnp.where(place == EA - 1, unpack_a(right, EA - 1, h, iz), 0.0)
             put(iz, h, low, high)
 
 
@@ -504,7 +506,7 @@
         join_z(y, ia, beyond[ia])
 
 
-def k_first_done(rhs, q, g, inv0, d, y0, s_ref, table, z1, z2, r1, r2, inv, x, rho, mid, ghost, face, y):
+def k_first_done(rhs, q, g, inv0, d, y0, s_ref, table, z1, z2, r1, r2, inv, x, rho, mid, up, down, ghost, face, y):
     masks = radial_masks()
     place, low = place_of(), lane_iota() < GROUP
     first, last = place == 0, place == EA - 1
@@ -512,20 +514,20 @@
         for h in range(2):
             for ia in range(1, 7):
                 inv[iz, ia, :, half_of(h)] = inv0[iz, ia, :, half_of(h)]
-    g_below, g_above = got("gz", z1, z2, 8, 12)
+    gz, qz = from_z(z1, z2, 8), from_z(z1, z2, 0)
     g_left, g_right = got("row", r1, r2, 8, 12)
     for iz in range(8):
         for h in range(2):
-            v = with_z(g, g_below, g_above, iz, 0, h) + jnp.where(first, unpack_a(g_left, 0, h, iz), 0.0)
+            v = with_z(g, gz, iz, 0, h) + jnp.where(first, unpack_a(g_left, 0, h, iz), 0.0)
             inv[iz, 0, :, half_of(h)] = jnp.where(masks[2], 0.0, 1.0 / v)
-            v = with_z(g, g_below, g_above, iz, 7, h) + jnp.where(last, unpack_a(g_right, EA - 1, h, iz), 0.0)
+            v = with_z(g, gz, iz, 7, h) + jnp.where(last, unpack_a(g_right, EA - 1, h, iz), 0.0)
             inv[iz, 7, :, half_of(h)] = jnp.where(masks[2], 0.0, 1.0 / v)
 
     def put_face(iz, h, lo, hi):
         lo, hi = inv[iz, 0, :, half_of(h)] * lo, inv[iz, 7, :, half_of(h)] * hi
         face[iz, h] = jnp.where(first, lo, jnp.where(last, hi, 0.0)) * (1.0 / THETA)
 
-    edge_faces(q, inv, z1, z2, r1, r2, put_face)
+    edge_faces(q, qz, r1, r2, put_face)
     below, above = got("gz", z1, z2, 16, 17)
     left, right = got("row", r1, r2, 16, 17)
     ghost[2] = jnp.where(low, below[0], lroll(above[0], GROUP))
@@ -548,8 +550,7 @@
             for shift in (64, 32, 16):
                 v = v + lroll(v, shift)
             t_edge[side][end] = v
-    below, above = got("gz", z1, z2, 4, 8)
-    t_z = [both_z(below, above, ia) for ia in range(8)]
+    t_z = from_z(z1, z2, 4)
     t_z[0] = jnp.where(place == 0, jnp.where(low, t_edge[0][0], t_edge[0][1]), t_z[0])
     t_z[7] = jnp.where(place == EA - 1, jnp.where(low, t_edge[1][0], t_edge[1][1]), t_z[7])
     t_left, t_right = got("row", r1, r2, 4, 8)
@@ -563,19 +564,30 @@
         r = v - radial_add(y[iz, ia, :, sl], masks)
         x[iz, ia, :, sl] = (1.0 + C1) * whole(iz, ia, h) + C2 * inv[iz, ia, :, sl] * r
 
-    complete(q, z1, z2, r1, r2, 0, put_x)
+    complete(q, qz, r1, r2, 0, put_x)
     fine_apply(x, rho, rhs, halves(ghost), -1.0)
     for iz, ia, sl in every_fine():
         y[iz, ia, :, sl] = jnp.where(masks[2], 0.0, rho[iz, ia, :, sl])
-    down = jnp.dot(table[...], y[...].reshape(512, 256), preferred_element_type=jnp.float32, precision=lax.Precision.HIGHEST)
+    high, low_part = pair_of(y[...].reshape(512, 256))
+    sums = jnp.dot(table[...], high, preferred_element_type=jnp.float32)
+    sums = sums[0:112] + sums[112:224] + jnp.dot(table[0:112, :], low_part, preferred_element_type=jnp.float32)
     inner = lane_iota((56, HALF)) % ER > 0
     for h in range(2):
         sl = half_of(h)
-        mid[:, sl] = down[0:56, sl] + jnp.where(inner, lroll(down[56:112, sl], 1), 0.0)
+        mid[:, sl] = sums[0:56, sl] + jnp.where(inner, lroll(sums[56:112, sl], 1), 0.0)
     mid[48:56, :] = s_ref[...]
-
-
-def k_last(q, inv, d, y0, x, ghost, z1, z2, r1, r2, out, face, y):
+    up[0:56, :] = mid[...]
+    down[0:56, :] = mid[...]
+    for iz, ia, sl in every_fine():
+        y[iz, ia, :, sl] = radial_add(rho[iz, ia, :, sl], masks)
+    sum_inside(y)
+    bottom, top = faces_z(y, lambda iz, ia, h: inv[iz, ia, :, half_of(h)])
+    for i in range(8):
+        up[56 + 8 * (i // 2) : 64 + 8 * (i // 2), half_of(i % 2)] = top[i]
+        down[56 + 8 * (i // 2) : 64 + 8 * (i // 2), half_of(i % 2)] = bottom[i]
+
+
+def k_last(q, inv, d, y0, x, ghost, qz, tz, r1, r2, out, face, y):
     masks = radial_masks()
     place = place_of()
     first, last = place == 0, place == EA - 1
@@ -584,9 +596,8 @@
         lo, hi = inv[iz, 0, :, half_of(h)] * lo, inv[iz, 7, :, half_of(h)] * hi
         face[iz, h] = jnp.where(first, lo, jnp.where(last, hi, 0.0)) * (1.0 / THETA)
 
-    edge_faces(q, inv, z1, z2, r1, r2, put_face)
-    below, above = got("gz", z1, z2, 4, 8)
-    t_z = [both_z(below, above, ia) for ia in range(8)]
+    edge_faces(q, qz, r1, r2, put_face)
+    t_z = [tz[ia] for ia in range(8)]
     left, right = got("row", r1, r2, 8, 9)
     t_z[0] = t_z[0] + jnp.where(first, lroll(left[0], -(EA - 1) * ER), 0.0)
     t_z[7] = t_z[7] + jnp.where(last, lroll(right[0], (EA - 1) * ER), 0.0)
@@ -601,7 +612,7 @@
         r = v - radial_add(y[iz, ia, :, sl], masks)
         out[iz, ia, :, sl] = x[iz, ia, :, sl] + (1.0 + C1) * whole(iz, ia, h) + C2 * inv[iz, ia, :, sl] * r
 
-    complete(q, z1, z2, r1, r2, 0, put_out)
+    complete(q, qz, r1, r2, 0, put_out)
 
 
 NODES = [(iz, ia, ir) for iz in range(3) for ia in range(3) for ir in range(3)]
@@ -621,7 +632,7 @@
         out[i] = np.kron(np.kron(J73[:, iz], J73[:, ia]), J73[:, ir])
         if ir == 0:
             out[56 + i] = np.kron(np.kron(J73[:, iz], J73[:, ia]), J73[:, 3])
-    return out.astype(np.float32)
+    return np.concatenate(halves_of(out), axis=0)
 
 
 RESTRICT = restrict_rows()
@@ -714,7 +725,7 @@
     blocks, out, wide = refs[:-2], refs[-2], refs[-1]
     for k, block in enumerate(blocks):
         for z in range(EZ):
-            v = block[:, half_of(z // 2)]
+            v = block[0:56, half_of(z // 2)]
             wide[pl.ds((2 - EZ * k + z) % rows, 56, stride=rows), :] = lroll(v, GROUP) if z % 2 else v
 
     def entry(i):
@@ -743,7 +754,7 @@
         out[15 + p] = v
 
 
-def k_mid(own, r1, r2, coarse, res, x, inv_out, c_out, b, d, y, y2):
+def k_mid(own, r1, r2, coarse, res, x, inv_out, c_out, far, b, d, y, y2):
     rows = own.shape[1]
     even = parity("row")
     lane = lane_iota((rows, HALF))
@@ -778,15 +789,22 @@
         second = jnp.where((lane >= 32) & (lane < 96), 1.0, second)
         coarse[1 + k] = lroll(first, -32)[:, 0:GROUP]
         s.append(jnp.concatenate([first, second], axis=1))
+        for layer, (lower, upper) in enumerate(((1, 6), (0, 7))):
+            lo, hi = first[lower : lower + 1], first[upper : upper + 1]
+            low, place = lane[0:1] < GROUP, ((lane // ER) % EA)[0:1]
+            far[layer, k : k + 1] = jnp.where(low, lroll(lo, -32), lroll(hi, 32))
+            left = jnp.where(low, lroll(lo, -16), lroll(hi, 48))
+            right = jnp.where(low, lroll(lo, -48), lroll(hi, 16))
+            far[2 + layer, k : k + 1] = jnp.where(place == EA - 1, right, left)
 
     inner = lane_iota((rows, 2 * HALF)) % ER > 0
     c = mid_coefs(s)
     inverse = mid_inverse(c, inner)
     for i, e in enumerate([(ez, ea, er) for ez in range(2) for ea in range(2) for er in range(2)]):
-        inv_out[i] = inverse[e][0:8, 0:HALF]
+        inv_out[i] = inverse[e][:, 0:HALF]
     for k in range(3):
         for i, e in enumerate([(0, 0), (0, 1), (1, 0), (1, 1)]):
-            c_out[4 * k + i] = c[k][e][0:8, 0:HALF]
+            c_out[4 * k + i] = c[k][e][:, 0:HALF]
 
     def kind(iz, ia, ir):
         return inverse[end(iz), end(ia), end(ir)]
@@ -808,7 +826,7 @@
     for iz, ia, ir in NODES:
         n = node(iz, ia, ir)
         d[n] = (1.0 + C1) * d[n] + C2 * kind(iz, ia, ir) * (b[n] - y[n])
-        x[n] = d[n, 0:8, 0:HALF]
+        x[n] = d[n, :, 0:HALF]
 
     def near(iz, ia, ir):
         return d[node(iz, ia, ir), :, 0:HALF]
@@ -827,7 +845,7 @@
         r = b[n, :, 0:HALF] - y2[n]
         r = r if ir else jnp.where(inner, r, 0.0)
         y2[n] = r
-        res[n] = r[0:8]
+        res[n] = r
 
     def gather(v, prev):
         return v[0] + v[1] * float(J31[1, 0]) + v[2] * float(J31[2, 0]) + prev(v[1] * float(J31[1, 1]) + v[2] * float(J31[2, 1]))
@@ -838,6 +856,29 @@
         planes.append(gather(lines, prev_a))
     vertex = jnp.where(inner, gather(planes, prev_z), 0.0)
     coarse[0] = lroll(vertex, -32)[:, 0:GROUP]
+
+
+def k_far(far, inv):
+    masks, place = radial_masks(), place_of()
+    wr, kr = column(W7), column(np.diag(K7))
+    near, next_, near_n, next_n = [stretch_rows(far[i]) for i in range(4)]
+
+    def diag(s, iz, ia):
+        return (s[0] * float(K7[iz, iz] * W7[ia]) + s[1] * float(W7[iz] * K7[ia, ia])) * wr + s[2] * (kr * float(W7[iz] * W7[ia]))
+
+    for j in range(1, 8):
+
+        def whole(s, t, ia):
+            v = diag(s, j, ia)
+            return radial_add(v + diag(t, 0, ia) if j == 7 else v, masks)
+
+        line = [whole(near, next_, ia) for ia in range(8)]
+        beyond = whole(near_n, next_n, 0)
+        lo = line[0] + jnp.where(place > 0, lroll(line[7], ER), beyond)
+        hi = line[7] + jnp.where(place < EA - 1, lroll(line[0], -ER), beyond)
+        line[0], line[7] = lo, hi
+        for ia in range(8):
+            inv[j - 1, ia] = jnp.where(masks[2], 0.0, 1.0 / line[ia])
 
 
 def vertex_solve(s0, s1, s2, b):
@@ -877,16 +918,18 @@
     return e
 
 
-def k_fifth(whole, res, xm, inv3, c_in, x, rho, inv, ghost, kron, x_out, q, m1, m2, lift, dm, rm, xs, g):
+def k_fifth(
+    whole, res, xm, inv3, c_in, x, rho, inv, ghost, kron, far, inv_far, from_below, from_above, x_out, q, qz, tz, m1, m2, lift, dm, rm, xs, g, gf, yf
+):
     e = vertex_solve(whole[1], whole[2], whole[3], whole[0])
-    lanes = e.shape[1]
+    rows, lanes = e.shape
     e = pltpu.roll(e, (lanes + 32 - GROUP * lax.axis_index("row")) % lanes, 1)
     corner = {}
     for cz in range(2):
         for ca in range(2):
             for cr in range(2):
                 v = next_z(e) if cz else e
-                corner[cz, ca, cr] = lroll(v, -(ca * ER + cr))[0:8, 0:HALF]
+                corner[cz, ca, cr] = lroll(v, -(ca * ER + cr))[:, 0:HALF]
 
     def three(a, b):
         return [a] + [a * float(J31[i, 0]) + b * float(J31[i, 1]) for i in (1, 2)]
@@ -941,16 +984,22 @@
                 v = lroll(v, -(ia // 3 * ER + ir // 3))
                 v = next_z(v) if iz == 3 else v
                 n = (iz * 4 + ia) * 4 + ir
-                xs[n * 8 : (n + 1) * 8, :] = v
+                xs[n * rows : (n + 1) * rows, :] = v
     low = lane_iota((64, HALF)) < GROUP
     cols = []
     for h in range(2):
-        one = xs[pl.ds(2 + 2 * h, 64, stride=8), :]
-        two = xs[pl.ds(3 + 2 * h, 64, stride=8), :]
+        one = xs[pl.ds(2 + 2 * h, 64, stride=rows), :]
+        two = xs[pl.ds(3 + 2 * h, 64, stride=rows), :]
         cols.append(jnp.where(low, lroll(one, -32), lroll(two, 32)))
-    xe = jnp.concatenate(cols, axis=1)
-    raised = jnp.dot(kron[...], xe, preferred_element_type=jnp.float32, precision=lax.Precision.HIGHEST)
-    g[...] = raised.reshape(8, 8, 8, 256)
+    for lower, upper in ((1, 6), (0, 7)):
+        one = xs[pl.ds(lower, 64, stride=rows), :]
+        one = jnp.concatenate([one[48:64], one[32:48], one[16:32], one[0:16]], axis=0)
+        two = xs[pl.ds(upper, 64, stride=rows), :]
+        cols.append(jnp.where(low, lroll(one, -32), lroll(two, 32)))
+    high, low_part = pair_of(jnp.concatenate(cols, axis=1))
+    raised = jnp.dot(kron[...], jnp.concatenate([high, low_part, high], axis=0), preferred_element_type=jnp.float32)
+    g[...] = raised[:, 0:256].reshape(8, 8, 8, 256)
+    gf[...] = raised[:, 256:512].reshape(8, 8, 8, 256)
     for iz, ia, sl in every_fine():
         x_out[iz, ia, :, sl] = x[iz, ia, :, sl] + g[iz, ia, :, sl]
     masks = radial_masks()
@@ -958,7 +1007,42 @@
     for iz, ia, sl in every_fine():
         q[iz, ia, :, sl] = radial_add(q[iz, ia, :, sl], masks)
     sum_inside(q)
-    send_z(q, lambda iz, ia, h: inv[iz, ia, :, half_of(h)], m1, m2)
+
+    fine_apply(gf, yf, None, [far[0]], 1.0)
+    s0, s1, s2 = stretch_rows(far[1])
+    wr, rolls, place = column(W7), radial_columns(), place_of()
+    second = half_of(1)
+    part_a = along(K7, [gf[0, ia, :, second] for ia in range(8)])
+    for ia in range(8):
+        part_z = weighted_sum(K7[0], [gf[j, ia, :, second] for j in range(8)])
+        part_r = radial_apply(rolls, gf[0, ia, :, second])
+        v = s0 * wr * part_z * float(W7[ia]) + (s1 * wr * part_a[ia] + s2 * part_r * float(W7[ia])) * float(W7[0])
+        yf[7, ia] = yf[7, ia] + v
+    for j in range(8):
+        line = [radial_add(yf[j, ia], masks) for ia in range(8)]
+        lo = line[0] + jnp.where(place > 0, lroll(line[7], ER), 0.0)
+        hi = line[7] + jnp.where(place < EA - 1, lroll(line[0], -ER), 0.0)
+        line[0], line[7] = lo, hi
+        for ia in range(8):
+            if j:
+                line[ia] = inv_far[j - 1, ia] * line[ia] * float(K7[0, j] / THETA)
+            yf[j, ia] = line[ia]
+
+    def entries(block, start):
+        out = []
+        for i in range(start, start + 4):
+            out.append(block[56 + 8 * (i // 2) : 64 + 8 * (i // 2), half_of(i % 2)])
+        return out
+
+    q_below, q_above, t_below, t_above = entries(from_below, 0), entries(from_above, 0), entries(from_below, 4), entries(from_above, 4)
+    for ia in range(8):
+        qz[ia] = both_z(q_below, q_above, ia) - yf[0, ia]
+        total = yf[1, ia]
+        for j in range(2, 8):
+            total = total + yf[j, ia]
+        tz[ia] = both_z(t_below, t_above, ia) - total
+    send_a(q, qz, lambda iz, ia, h: inv[iz, ia, :, half_of(h)], m1, m2)
+    post("row", [tz[0]], [tz[7]], m1, m2, 8)
 
 
 FINE = (8, 8, 8, 256)
@@ -1000,21 +1084,25 @@
     r1, r2 = swap_a(m1, m2)
     inv, d, y = call(k_first_mean, [FINE, FINE, FINE], name="first_mean")(q, g, stretch, z1, z2)
     faces = (8, 2, 8, HALF)
-    inv, x, rho, block, ghost = call(k_first_done, [FINE, FINE, FINE, (56, 256), ghosts], [faces, FINE], name="first_done")(
+    inv, x, rho, block, up, down, ghost = call(k_first_done, [FINE, FINE, FINE, (56, 256), (88, 256), (88, 256), ghosts], [faces, FINE], name="first_done")(
         rhs, q, g, inv, d, y, stretch, jnp.asarray(RESTRICT), z1, z2, r1, r2
     )
 
     rows = gz * EZ
-    blocks = [block] + [lax.ppermute(block, "gz", [(i, (i + k) % gz) for i in range(gz)]) for k in range(1, gz)]
+    blocks = [block] + [
+        lax.ppermute(up if k == 1 else down if k == gz - 1 else block, "gz", [(i, (i + k) % gz) for i in range(gz)]) for k in range(1, gz)
+    ]
     column_ = call(functools.partial(k_column, rows), [(PACKED, rows, HALF)], [(56 * rows, HALF)], name="column")(*blocks)[0]
     r1, r2 = swap_a(column_, column_)
-    cube, wide = (27, 8, HALF), (27, rows, 2 * HALF)
-    coarse, res, xm, inv3, c3 = call(
+    cube, wide = (27, rows, HALF), (27, rows, 2 * HALF)
+    coarse, res, xm, inv3, c3, far = call(
         k_mid,
-        [(4, rows, GROUP), cube, cube, (8, 8, HALF), (12, 8, HALF)],
+        [(4, rows, GROUP), cube, cube, (8, rows, HALF), (12, rows, HALF), (4, 8, HALF)],
         [wide, wide, wide, (27, rows, HALF)],
         name="mid",
     )(column_, r1, r2)
+
+    inv_far = call(k_far, [(7, 8, 8, HALF)], name="far")(far)[0]
 
     bit = 1
     while bit < row:
@@ -1030,14 +1118,16 @@
         coarse = jnp.concatenate(ordered, 2)
         bit *= size
 
-    x, q, m1, m2 = call(k_fifth, [FINE, FINE, message(8), message(8)], [cube, cube, cube, (512, HALF), FINE], name="fifth")(
-        coarse, res, xm, inv3, c3, x, rho, inv, ghost, jnp.asarray(KRON73)
-    )
-    z1, z2 = swap_z(m1, m2)
-    m1, m2 = call(k_later_a, [message(LATER), message(LATER)], name="later_a")(q, inv, z1, z2)
+    line = (8, 8, HALF)
+    x, q, qz, tz, m1, m2 = call(
+        k_fifth,
+        [FINE, FINE, line, line, message(LATER), message(LATER)],
+        [cube, cube, cube, (64 * rows, HALF), FINE, FINE, (8, 8, 8, HALF)],
+        name="fifth",
+    )(coarse, res, xm, inv3, c3, x, rho, inv, ghost, jnp.asarray(KRON73), far, inv_far, blocks[1], blocks[gz - 1])
     r1, r2 = swap_a(m1, m2)
-    d, y = call(k_later_mean, [FINE, FINE], name="later_mean")(q, inv, ghost, z1, z2)
-    return call(k_last, [FINE], [faces, FINE], name="last")(q, inv, d, y, x, ghost, z1, z2, r1, r2)[0]
+    d, y = call(k_later_mean, [FINE, FINE], name="later_mean")(q, inv, ghost, qz)
+    return call(k_last, [FINE], [faces, FINE], name="last")(q, inv, d, y, x, ghost, qz, tz, r1, r2)[0]
 
 
 def solution(mesh):

time: 61.5 us -> 57.3 us (0.932)
  starting transfers between devices: 23.1 us -> 20 us
  waiting for transfers between devices: 23.5 us -> 21.7 us
  Pallas kernels: 12.7 us -> 13.4 us
    ppermute x4 -> x2, waiting for transfers between devices: 7.62 us -> 3.77 us  [swap_z(): return (lax.ppermute(m1, 'gz', mate_gz), lax.ppermute(m2, 'gz', other_gz))]
    ppermute x4 -> x2, starting transfers between devices: 9.27 us -> 5.56 us  [swap_z(): return (lax.ppermute(m1, 'gz', mate_gz), lax.ppermute(m2, 'gz', other_gz))]
    ppermute x3, waiting for transfers between devices: 4.27 us -> 6.16 us  [per_device(): lax.ppermute(up if k == 1 else down if k == gz - 1 else block, 'gz', [(i,...]
    pallas_call x5, Pallas kernels: 8.55 us -> 9.28 us  [the longest x1 4.24 us: per_device(): call(k_fifth, [FINE, FINE, line, line, message(LATER), message(LATER)], [...]
    ppermute x4, waiting for transfers between devices: 3.59 us -> 4.27 us  [per_device(): lax.ppermute(coarse, 'row', [(i, i ^ k * bit) for i in range(row)])]
  transfers between devices with their start and end apart: 17 -> 15, of which waited for: 11 -> 9; matrix products, arithmetic and copies ran while one was open for 0% -> 0% of each run, Pallas kernels for 3% -> 3%
where the time goes in v2:
time: 57.3 us; the launch traced here: 57.1 us
  waiting for transfers between devices  21.7 us (38%)
  starting transfers between devices  20 us (35%)
  Pallas kernels  13.4 us (23%)
  local copies, waits for them, and re-layouts  1.75 us (3%)
    ppermute x3, waiting for transfers between devices, swap_a(): lax.ppermute(m2, 'row', other_row)  7.53 us
    ppermute x3, starting transfers between devices, swap_a(): lax.ppermute(m2, 'row', other_row)  6.76 us
    ppermute x3, waiting for transfers between devices, per_device(): lax.ppermute(up if k == 1 else down if k == gz - 1 else block, 'gz', [(i,...  6.16 us
    ppermute x2, starting transfers between devices, swap_z(): return (lax.ppermute(m1, 'gz', mate_gz), lax.ppermute(m2, 'gz', other_gz))  5.56 us
    ppermute x4, waiting for transfers between devices, per_device(): lax.ppermute(coarse, 'row', [(i, i ^ k * bit) for i in range(row)])  4.27 us
    pallas_call x1, Pallas kernels, per_device(): call(k_fifth, [FINE, FINE, line, line, message(LATER), message(LATER)], [...  4.24 us
    ppermute x3, starting transfers between devices, per_device(): lax.ppermute(up if k == 1 else down if k == gz - 1 else block, 'gz', [(i,...  3.87 us
    ppermute x2, waiting for transfers between devices, swap_z(): return (lax.ppermute(m1, 'gz', mate_gz), lax.ppermute(m2, 'gz', other_gz))  3.77 us
  transfers between devices with their start and end apart: 15, of which 9 were waited for; matrix products, arithmetic and copies ran while one was open for 0% of the time, Pallas kernels for 3%

profile of v2, /device:TPU:0, one launch (start us, length us, event | category | flops | bytes accessed | tf_op | source)
XLA Modules:
  0.0 57.1 jit_solution(14490483765858328120)
XLA Ops:
  0.0 0.7 %pad.4.s_any.s_ref = f32[8,256]{1,0:T(8,128)S(1)} pad(f32[3,256]{1,0:T(4,128)} %param.5, f32[]{:T(128)} %constant.54.clone.1), padding=0_5x0_0 | pad | bytes 11268 | tf_op jit(solution)/shard_map/jit(_pad)/pad | solution.py:1079
  0.7 1.0 %copy-done = f32[8,8,8,256]{3,2,1,0:T(8,128)S(1)} copy-done((f32[8,8,8,256]{3,2,1,0:T(8,128)S(1)}, f32[8,8,8,256]{3,2,1,0:T(8,128)}, u32[]{:S(2)}) %copy-start) | copy-done | bytes 524312
  1.7 1.2 %first.1 = (f32[8,8,8,256]{3,2,1,0:T(8,128)S(1)}, f32[8,8,8,256]{3,2,1,0:T(8,128)S(1)}, f32[17,8,128]{2,1,0:T(8,128)S(1)}, f32[17,8,128]{2,1,0:T(8,128)S(1)}) custom-call(f32[8,8,8,256]{3,2,1,0:T(8,128)S(1)} %copy-done, f32[8,256]{1,0:T(8,128)S(1)} %pad.4.s_any.s_ref), custom_call_target="tpu_custom_call" | custom-call | tf_op jit(solution)/shard_map/first/pallas_call | solution.py:1081
  2.9 3.1 %collective-permute-start = (f32[17,8,128]{2,1,0:T(8,128)S(1)}, f32[17,8,128]{2,1,0:T(8,128)S(1)}, u32[]{:S(2)}, u32[]{:S(2)}) collective-permute-start(f32[17,8,128]{2,1,0:T(8,128)S(1)} %get-tuple-element.37), channel_id=1, source_target_pairs={{0,8},{8,0},{16,24},{24,16},{1,9},{9,1},{17,25},{25,17},{2,10},{10... | collective-permute-start | bytes 208904 | tf_op jit(solution)/shard_map/ppermute | solution.py:1074
  6.0 2.5 %collective-permute-start.1 = (f32[17,8,128]{2,1,0:T(8,128)S(1)}, f32[17,8,128]{2,1,0:T(8,128)S(1)}, u32[]{:S(2)}, u32[]{:S(2)}) collective-permute-start(f32[17,8,128]{2,1,0:T(8,128)S(1)} %get-tuple-element.38), channel_id=1, source_target_pairs={{0,24},{8,16},{16,8},{24,0},{1,25},{9,17},{17,9},{25,1},{2,26},{10... | collective-permute-start | bytes 208904 | tf_op jit(solution)/shard_map/ppermute | solution.py:1074
  8.5 3.8 %collective-permute-done.1.z2 = f32[17,8,128]{2,1,0:T(8,128)S(1)} collective-permute-done((f32[17,8,128]{2,1,0:T(8,128)S(1)}, f32[17,8,128]{2,1,0:T(8,128)S(1)}, u32[]{:S(2)}, u32[]{:S(2)}) %collective-permute-start.1) | collective-permute-done | bytes 69664 | tf_op jit(solution)/shard_map/ppermute | solution.py:1074
  12.2 0.2 first_a.1
  12.6 2.5 %collective-permute-start.3 = (f32[17,8,128]{2,1,0:T(8,128)S(1)}, f32[17,8,128]{2,1,0:T(8,128)S(1)}, u32[]{:S(2)}, u32[]{:S(2)}) collective-permute-start(f32[17,8,128]{2,1,0:T(8,128)S(1)} %get-tuple-element.43), channel_id=1, source_target_pairs={{0,7},{1,2},{2,1},{3,4},{4,3},{5,6},{6,5},{7,0},{8,15},{9,10},{10,... | collective-permute-start | bytes 208904 | tf_op jit(solution)/shard_map/ppermute | solution.py:1071
  15.1 0.9 %first_mean.1 = (f32[8,8,8,256]{3,2,1,0:T(8,128)S(1)}, f32[8,8,8,256]{3,2,1,0:T(8,128)S(1)}, f32[8,8,8,256]{3,2,1,0:T(8,128)S(1)}) custom-call(f32[8,8,8,256]{3,2,1,0:T(8,128)S(1)} %get-tuple-element.35.q, f32[8,8,8,256]{3,2,1,0:T(8,128)S(1)} %get-tuple-element.36.g, f32[8,256]{1,0:T(8,128)S(1)} %pad.4.s_any.s_ref, ...), custom_call_target="tpu_custom_call" | custom-call | tf_op jit(solution)/shard_map/first_mean/pallas_call | solution.py:1085
  16.0 1.4 %collective-permute-done.3.r2 = f32[17,8,128]{2,1,0:T(8,128)S(1)} collective-permute-done((f32[17,8,128]{2,1,0:T(8,128)S(1)}, f32[17,8,128]{2,1,0:T(8,128)S(1)}, u32[]{:S(2)}, u32[]{:S(2)}) %collective-permute-start.3) | collective-permute-done | bytes 69664 | tf_op jit(solution)/shard_map/ppermute | solution.py:1071
  17.4 2.2 %first_done.1 = (f32[8,8,8,256]{3,2,1,0:T(8,128)S(1)}, f32[8,8,8,256]{3,2,1,0:T(8,128)S(1)}, f32[8,8,8,256]{3,2,1,0:T(8,128)S(1)}, f32[56,256]{1,0:T(8,128)S(1)}...) custom-call(f32[8,8,8,256]{3,2,1,0:T(8,128)S(1)} %copy-done.1, ...), custom_call_target="tpu_custom_call" | custom-call | tf_op jit(solution)/shard_map/first_done/pallas_call | solution.py:1087
  19.7 3.8 %collective-permute-start.6 = (f32[88,256]{1,0:T(8,128)S(1)}, f32[88,256]{1,0:T(8,128)S(1)}, u32[]{:S(2)}, u32[]{:S(2)}) collective-permute-start(f32[88,256]{1,0:T(8,128)S(1)} %get-tuple-element.46), channel_id=1, source_target_pairs={{0,24},{8,0},{16,8},{24,16},{1,25},{9,1},{17,9},{25,17},{2,26},{10... | collective-permute-start | bytes 270344 | tf_op jit(solution)/shard_map/ppermute | solution.py:1093
  23.5 6.2 %collective-permute-done.5.refs_2_ = f32[56,256]{1,0:T(8,128)S(1)} collective-permute-done((f32[56,256]{1,0:T(8,128)S(1)}, f32[56,256]{1,0:T(8,128)S(1)}, u32[]{:S(2)}, u32[]{:S(2)}) %collective-permute-start.5) | collective-permute-done | bytes 57376 | tf_op jit(solution)/shard_map/ppermute | solution.py:1093
  29.7 0.3 column.1.own
  30.0 0.1 collective-permute-start.7
  30.0 2.6 %collective-permute-start.8 = (f32[17,16,128]{2,1,0:T(8,128)S(1)}, f32[17,16,128]{2,1,0:T(8,128)S(1)}, u32[]{:S(2)}, u32[]{:S(2)}) collective-permute-start(f32[17,16,128]{2,1,0:T(8,128)S(1)} %column.1.own), channel_id=1, source_target_pairs={{0,7},{1,2},{2,1},{3,4},{4,3},{5,6},{6,5},{7,0},{8,15},{9,10},{10,... | collective-permute-start | bytes 417800 | tf_op jit(solution)/shard_map/ppermute | solution.py:1071
  32.6 4.0 %collective-permute-done.8.r2 = f32[17,16,128]{2,1,0:T(8,128)S(1)} collective-permute-done((f32[17,16,128]{2,1,0:T(8,128)S(1)}, f32[17,16,128]{2,1,0:T(8,128)S(1)}, u32[]{:S(2)}, u32[]{:S(2)}) %collective-permute-start.8) | collective-permute-done | bytes 139296 | tf_op jit(solution)/shard_map/ppermute | solution.py:1071
  36.6 1.8 %mid.1 = (f32[4,16,64]{2,1,0:T(8,128)S(1)}, f32[27,16,128]{2,1,0:T(8,128)S(1)}, f32[27,16,128]{2,1,0:T(8,128)S(1)}, f32[8,16,128]{2,1,0:T(8,128)S(1)}, f32[12,16...) custom-call(f32[17,16,128]{2,1,0:T(8,128)S(1)} %column.1.own, f32[17,16,128]{2,1,0:T(8,128)S(1)} %collective-permute-done.7.r1, ...), custom_call_target="tpu_custom_call" | custom-call | tf_op jit(solution)/shard_map/mid/pallas_call | solution.py:1098
  38.5 1.1 %collective-permute-done.9 = f32[4,16,64]{2,1,0:T(8,128)S(1)} collective-permute-done((f32[4,16,64]{2,1,0:T(8,128)S(1)}, f32[4,16,64]{2,1,0:T(8,128)S(1)}, u32[]{:S(2)}, u32[]{:S(2)}) %collective-permute-start.9) | collective-permute-done | bytes 16416 | tf_op jit(solution)/shard_map/ppermute | solution.py:1111
  39.6 0.1 pad_maximum_fusion.1
  39.7 1.7 %collective-permute-start.10 = (f32[4,16,128]{2,1,0:T(8,128)S(1)}, f32[4,16,128]{2,1,0:T(8,128)S(1)}, u32[]{:S(2)}, u32[]{:S(2)}) collective-permute-start(f32[4,16,128]{2,1,0:T(8,128)S(1)} %pad_maximum_fusion.1), channel_id=1, source_target_pairs={{0,6},{1,7},{2,4},{3,5},{4,2},{5,3},{6,0},{7,1},{8,14},{9,15},{10,... | collective-permute-start | bytes 98312 | tf_op jit(solution)/shard_map/ppermute | solution.py:1111
  41.4 1.2 %collective-permute-start.11 = (f32[4,16,128]{2,1,0:T(8,128)S(1)}, f32[4,16,128]{2,1,0:T(8,128)S(1)}, u32[]{:S(2)}, u32[]{:S(2)}) collective-permute-start(f32[4,16,128]{2,1,0:T(8,128)S(1)} %pad_maximum_fusion.1), channel_id=1, source_target_pairs={{0,4},{1,5},{2,6},{3,7},{4,0},{5,1},{6,2},{7,3},{8,12},{9,13},{10,... | collective-permute-start | bytes 98312 | tf_op jit(solution)/shard_map/ppermute | solution.py:1111
  42.6 0.6 %collective-permute-start.12 = (f32[4,16,128]{2,1,0:T(8,128)S(1)}, f32[4,16,128]{2,1,0:T(8,128)S(1)}, u32[]{:S(2)}, u32[]{:S(2)}) collective-permute-start(f32[4,16,128]{2,1,0:T(8,128)S(1)} %pad_maximum_fusion.1), channel_id=1, source_target_pairs={{0,2},{1,3},{2,0},{3,1},{4,6},{5,7},{6,4},{7,5},{8,10},{9,11},{10,... | collective-permute-start | bytes 98312 | tf_op jit(solution)/shard_map/ppermute | solution.py:1111
  43.2 0.2 far.1.inv_far
  43.4 1.2 %collective-permute-done.10 = f32[4,16,128]{2,1,0:T(8,128)S(1)} collective-permute-done((f32[4,16,128]{2,1,0:T(8,128)S(1)}, f32[4,16,128]{2,1,0:T(8,128)S(1)}, u32[]{:S(2)}, u32[]{:S(2)}) %collective-permute-start.10) | collective-permute-done | bytes 32800 | tf_op jit(solution)/shard_map/ppermute | solution.py:1111
  44.6 0.7 %collective-permute-done.11 = f32[4,16,128]{2,1,0:T(8,128)S(1)} collective-permute-done((f32[4,16,128]{2,1,0:T(8,128)S(1)}, f32[4,16,128]{2,1,0:T(8,128)S(1)}, u32[]{:S(2)}, u32[]{:S(2)}) %collective-permute-start.11) | collective-permute-done | bytes 32800 | tf_op jit(solution)/shard_map/ppermute | solution.py:1111
  45.3 1.2 %collective-permute-done.12 = f32[4,16,128]{2,1,0:T(8,128)S(1)} collective-permute-done((f32[4,16,128]{2,1,0:T(8,128)S(1)}, f32[4,16,128]{2,1,0:T(8,128)S(1)}, u32[]{:S(2)}, u32[]{:S(2)}) %collective-permute-start.12) | collective-permute-done | bytes 32800 | tf_op jit(solution)/shard_map/ppermute | solution.py:1111
  46.6 4.2 %fifth.1 = (f32[8,8,8,256]{3,2,1,0:T(8,128)S(1)}, f32[8,8,8,256]{3,2,1,0:T(8,128)S(1)}, f32[8,8,128]{2,1,0:T(8,128)S(1)}, f32[8,8,128]{2,1,0:T(8,128)S(1)}, f32[...) custom-call(f32[4,16,512]{2,1,0:T(8,128)S(1)} %pad_maximum_fusion.whole, f32[27,16,128]{2,1,0:T(8,128)S(1)} %get-tuple-element.48.res, ...), custom_call_target="tpu_custom_call" | custom-call | tf_op jit(solution)/shard_map/fifth/pallas_call | solution.py:1122
  50.9 1.7 %collective-permute-start.14 = (f32[9,8,128]{2,1,0:T(8,128)S(1)}, f32[9,8,128]{2,1,0:T(8,128)S(1)}, u32[]{:S(2)}, u32[]{:S(2)}) collective-permute-start(f32[9,8,128]{2,1,0:T(8,128)S(1)} %get-tuple-element.64), channel_id=1, source_target_pairs={{0,7},{1,2},{2,1},{3,4},{4,3},{5,6},{6,5},{7,0},{8,15},{9,10},{10,... | collective-permute-start | bytes 110600 | tf_op jit(solution)/shard_map/ppermute | solution.py:1071
  52.6 0.9 %later_mean.1 = (f32[8,8,8,256]{3,2,1,0:T(8,128)S(1)}, f32[8,8,8,256]{3,2,1,0:T(8,128)S(1)}) custom-call(f32[8,8,8,256]{3,2,1,0:T(8,128)S(1)} %get-tuple-element.57.q, f32[8,8,8,256]{3,2,1,0:T(8,128)S(1)} %get-tuple-element.54.inv, f32[6,8,128]{2,1,0:T(8,128)S(1)} %get-tuple-element.55.ghost, f32[8,8,128]{2,1,0:T(8,128)S(1)} %get-tuple-element.58.qz), custom_call_target="tpu_custom_call" | custom-call | tf_op jit(solution)/shard_map/later_mean/pallas_call | solution.py:1129
  53.5 2.1 %collective-permute-done.14.r2 = f32[9,8,128]{2,1,0:T(8,128)S(1)} collective-permute-done((f32[9,8,128]{2,1,0:T(8,128)S(1)}, f32[9,8,128]{2,1,0:T(8,128)S(1)}, u32[]{:S(2)}, u32[]{:S(2)}) %collective-permute-start.14) | collective-permute-done | bytes 36896 | tf_op jit(solution)/shard_map/ppermute | solution.py:1071
  55.6 1.5 %last.1 = f32[8,8,8,256]{3,2,1,0:T(8,128)} custom-call(f32[8,8,8,256]{3,2,1,0:T(8,128)S(1)} %get-tuple-element.57.q, f32[8,8,8,256]{3,2,1,0:T(8,128)S(1)} %get-tuple-element.54.inv, f32[8,8,8,256]{3,2,1,0:T(8,128)S(1)} %get-tuple-element.59.d, f32[8,8,8,256]{3,2,1,0:T(8,128)S(1)} %get-tuple-element.60.y0, f32[8,8,8,256]{3,2,1,0:T(8,128)S(1)} %get-tuple-element.61.x, ...), custom_call_target="tpu_custom_call" | custom-call | tf_op jit(solution)/shard_map/last/pallas_call | solution.py:1130
  (21 shorter events, 0.3 us)
Async XLA Ops:
  0.7 1.0 %copy-start = (f32[8,8,8,256]{3,2,1,0:T(8,128)S(1)}, f32[8,8,8,256]{3,2,1,0:T(8,128)}, u32[]{:S(2)}) copy-start(f32[8,8,8,256]{3,2,1,0:T(8,128)} %rhs.1) | copy-start | bytes 1572868
  2.9 5.6 %collective-permute-start = (f32[17,8,128]{2,1,0:T(8,128)S(1)}, f32[17,8,128]{2,1,0:T(8,128)S(1)}, u32[]{:S(2)}, u32[]{:S(2)}) collective-permute-start(f32[17,8,128]{2,1,0:T(8,128)S(1)} %get-tuple-element.37), channel_id=1, source_target_pairs={{0,8},{8,0},{16,24},{24,16},{1,9},{9,1},{17,25},{25,17},{2,10},{10... | collective-permute-start | bytes 208904 | tf_op jit(solution)/shard_map/ppermute | solution.py:1074
  6.0 6.2 %collective-permute-start.1 = (f32[17,8,128]{2,1,0:T(8,128)S(1)}, f32[17,8,128]{2,1,0:T(8,128)S(1)}, u32[]{:S(2)}, u32[]{:S(2)}) collective-permute-start(f32[17,8,128]{2,1,0:T(8,128)S(1)} %get-tuple-element.38), channel_id=1, source_target_pairs={{0,24},{8,16},{16,8},{24,0},{1,25},{9,17},{17,9},{25,1},{2,26},{10... | collective-permute-start | bytes 208904 | tf_op jit(solution)/shard_map/ppermute | solution.py:1074
  12.5 3.6 %collective-permute-start.2 = (f32[17,8,128]{2,1,0:T(8,128)S(1)}, f32[17,8,128]{2,1,0:T(8,128)S(1)}, u32[]{:S(2)}, u32[]{:S(2)}) collective-permute-start(f32[17,8,128]{2,1,0:T(8,128)S(1)} %get-tuple-element.42), channel_id=1, source_target_pairs={{0,1},{1,0},{2,3},{3,2},{4,5},{5,4},{6,7},{7,6},{8,9},{9,8},{10,11... | collective-permute-start | bytes 208904 | tf_op jit(solution)/shard_map/ppermute | solution.py:1071
  12.6 4.9 %copy-start.1 = (f32[8,8,8,256]{3,2,1,0:T(8,128)S(1)}, f32[8,8,8,256]{3,2,1,0:T(8,128)}, u32[]{:S(2)}) copy-start(f32[8,8,8,256]{3,2,1,0:T(8,128)} %rhs.1) | copy-start | bytes 1572868
  12.6 4.9 %copy-start.3 = (bf16[224,512]{1,0:T(8,128)(2,1)S(1)}, bf16[224,512]{1,0:T(8,128)(2,1)}, u32[]{:S(2)}) copy-start(bf16[224,512]{1,0:T(8,128)(2,1)} %constant.55.clone.table) | copy-start | bytes 688132
  12.6 4.8 %collective-permute-start.3 = (f32[17,8,128]{2,1,0:T(8,128)S(1)}, f32[17,8,128]{2,1,0:T(8,128)S(1)}, u32[]{:S(2)}, u32[]{:S(2)}) collective-permute-start(f32[17,8,128]{2,1,0:T(8,128)S(1)} %get-tuple-element.43), channel_id=1, source_target_pairs={{0,7},{1,2},{2,1},{3,4},{4,3},{5,6},{6,5},{7,0},{8,15},{9,10},{10,... | collective-permute-start | bytes 208904 | tf_op jit(solution)/shard_map/ppermute | solution.py:1071
  19.6 10.0 %collective-permute-start.4 = (f32[88,256]{1,0:T(8,128)S(1)}, f32[88,256]{1,0:T(8,128)S(1)}, u32[]{:S(2)}, u32[]{:S(2)}) collective-permute-start(f32[88,256]{1,0:T(8,128)S(1)} %get-tuple-element.45), channel_id=1, source_target_pairs={{0,8},{8,16},{16,24},{24,0},{1,9},{9,17},{17,25},{25,1},{2,10},{10... | collective-permute-start | bytes 270344 | tf_op jit(solution)/shard_map/ppermute | solution.py:1093
  19.7 10.0 %collective-permute-start.6 = (f32[88,256]{1,0:T(8,128)S(1)}, f32[88,256]{1,0:T(8,128)S(1)}, u32[]{:S(2)}, u32[]{:S(2)}) collective-permute-start(f32[88,256]{1,0:T(8,128)S(1)} %get-tuple-element.46), channel_id=1, source_target_pairs={{0,24},{8,0},{16,8},{24,16},{1,25},{9,1},{17,9},{25,17},{2,26},{10... | collective-permute-start | bytes 270344 | tf_op jit(solution)/shard_map/ppermute | solution.py:1093
  23.5 6.2 %collective-permute-start.5 = (f32[56,256]{1,0:T(8,128)S(1)}, f32[56,256]{1,0:T(8,128)S(1)}, u32[]{:S(2)}, u32[]{:S(2)}) collective-permute-start(f32[56,256]{1,0:T(8,128)S(1)} %get-tuple-element.44.refs_0_), channel_id=1, source_target_pairs={{0,16},{8,24},{16,0},{24,8},{1,17},{9,25},{17,1},{25,9},{2,18},{10... | collective-permute-start | bytes 172040 | tf_op jit(solution)/shard_map/ppermute | solution.py:1093
  30.0 2.6 %collective-permute-start.7 = (f32[17,16,128]{2,1,0:T(8,128)S(1)}, f32[17,16,128]{2,1,0:T(8,128)S(1)}, u32[]{:S(2)}, u32[]{:S(2)}) collective-permute-start(f32[17,16,128]{2,1,0:T(8,128)S(1)} %column.1.own), channel_id=1, source_target_pairs={{0,1},{1,0},{2,3},{3,2},{4,5},{5,4},{6,7},{7,6},{8,9},{9,8},{10,11... | collective-permute-start | bytes 417800 | tf_op jit(solution)/shard_map/ppermute | solution.py:1071
  30.0 6.6 %collective-permute-start.8 = (f32[17,16,128]{2,1,0:T(8,128)S(1)}, f32[17,16,128]{2,1,0:T(8,128)S(1)}, u32[]{:S(2)}, u32[]{:S(2)}) collective-permute-start(f32[17,16,128]{2,1,0:T(8,128)S(1)} %column.1.own), channel_id=1, source_target_pairs={{0,7},{1,2},{2,1},{3,4},{4,3},{5,6},{6,5},{7,0},{8,15},{9,10},{10,... | collective-permute-start | bytes 417800 | tf_op jit(solution)/shard_map/ppermute | solution.py:1071
  38.4 1.2 %collective-permute-start.9 = (f32[4,16,64]{2,1,0:T(8,128)S(1)}, f32[4,16,64]{2,1,0:T(8,128)S(1)}, u32[]{:S(2)}, u32[]{:S(2)}) collective-permute-start(f32[4,16,64]{2,1,0:T(8,128)S(1)} %get-tuple-element.47), channel_id=1, source_target_pairs={{0,1},{1,0},{2,3},{3,2},{4,5},{5,4},{6,7},{7,6},{8,9},{9,8},{10,11... | collective-permute-start | bytes 49160 | tf_op jit(solution)/shard_map/ppermute | solution.py:1111
  39.7 4.9 %collective-permute-start.10 = (f32[4,16,128]{2,1,0:T(8,128)S(1)}, f32[4,16,128]{2,1,0:T(8,128)S(1)}, u32[]{:S(2)}, u32[]{:S(2)}) collective-permute-start(f32[4,16,128]{2,1,0:T(8,128)S(1)} %pad_maximum_fusion.1), channel_id=1, source_target_pairs={{0,6},{1,7},{2,4},{3,5},{4,2},{5,3},{6,0},{7,1},{8,14},{9,15},{10,... | collective-permute-start | bytes 98312 | tf_op jit(solution)/shard_map/ppermute | solution.py:1111
  41.4 3.9 %collective-permute-start.11 = (f32[4,16,128]{2,1,0:T(8,128)S(1)}, f32[4,16,128]{2,1,0:T(8,128)S(1)}, u32[]{:S(2)}, u32[]{:S(2)}) collective-permute-start(f32[4,16,128]{2,1,0:T(8,128)S(1)} %pad_maximum_fusion.1), channel_id=1, source_target_pairs={{0,4},{1,5},{2,6},{3,7},{4,0},{5,1},{6,2},{7,3},{8,12},{9,13},{10,... | collective-permute-start | bytes 98312 | tf_op jit(solution)/shard_map/ppermute | solution.py:1111
  42.6 3.9 %collective-permute-start.12 = (f32[4,16,128]{2,1,0:T(8,128)S(1)}, f32[4,16,128]{2,1,0:T(8,128)S(1)}, u32[]{:S(2)}, u32[]{:S(2)}) collective-permute-start(f32[4,16,128]{2,1,0:T(8,128)S(1)} %pad_maximum_fusion.1), channel_id=1, source_target_pairs={{0,2},{1,3},{2,0},{3,1},{4,6},{5,7},{6,4},{7,5},{8,10},{9,11},{10,... | collective-permute-start | bytes 98312 | tf_op jit(solution)/shard_map/ppermute | solution.py:1111
  43.4 3.2 %copy-start.2 = (bf16[512,192]{1,0:T(8,128)(2,1)S(1)}, bf16[512,192]{1,0:T(8,128)(2,1)}, u32[]{:S(2)}) copy-start(bf16[512,192]{1,0:T(8,128)(2,1)} %constant.56.clone.kron) | copy-start | bytes 589828
  50.8 2.6 %collective-permute-start.13 = (f32[9,8,128]{2,1,0:T(8,128)S(1)}, f32[9,8,128]{2,1,0:T(8,128)S(1)}, u32[]{:S(2)}, u32[]{:S(2)}) collective-permute-start(f32[9,8,128]{2,1,0:T(8,128)S(1)} %get-tuple-element.63), channel_id=1, source_target_pairs={{0,1},{1,0},{2,3},{3,2},{4,5},{5,4},{6,7},{7,6},{8,9},{9,8},{10,11... | collective-permute-start | bytes 110600 | tf_op jit(solution)/shard_map/ppermute | solution.py:1071
  50.9 4.7 %collective-permute-start.14 = (f32[9,8,128]{2,1,0:T(8,128)S(1)}, f32[9,8,128]{2,1,0:T(8,128)S(1)}, u32[]{:S(2)}, u32[]{:S(2)}) collective-permute-start(f32[9,8,128]{2,1,0:T(8,128)S(1)} %get-tuple-element.64), channel_id=1, source_target_pairs={{0,7},{1,2},{2,1},{3,4},{4,3},{5,6},{6,5},{7,0},{8,15},{9,10},{10,... | collective-permute-start | bytes 110600 | tf_op jit(solution)/shard_map/ppermute | solution.py:1071

commit v3 on v2

--- a/solution.py
+++ b/solution.py
@@ -576,15 +576,13 @@
         sl = half_of(h)
         mid[:, sl] = sums[0:56, sl] + jnp.where(inner, lroll(sums[56:112, sl], 1), 0.0)
     mid[48:56, :] = s_ref[...]
-    up[0:56, :] = mid[...]
-    down[0:56, :] = mid[...]
     for iz, ia, sl in every_fine():
         y[iz, ia, :, sl] = radial_add(rho[iz, ia, :, sl], masks)
     sum_inside(y)
     bottom, top = faces_z(y, lambda iz, ia, h: inv[iz, ia, :, half_of(h)])
     for i in range(8):
-        up[56 + 8 * (i // 2) : 64 + 8 * (i // 2), half_of(i % 2)] = top[i]
-        down[56 + 8 * (i // 2) : 64 + 8 * (i // 2), half_of(i % 2)] = bottom[i]
+        up[i] = top[i]
+        down[i] = bottom[i]
 
 
 def k_last(q, inv, d, y0, x, ghost, qz, tz, r1, r2, out, face, y):
@@ -722,10 +720,12 @@
 
 
 def k_column(rows, *refs):
-    blocks, out, wide = refs[:-2], refs[-2], refs[-1]
+    up_in, down_in, *blocks, out, up, down, wide = refs
+    up[...] = up_in[...]
+    down[...] = down_in[...]
     for k, block in enumerate(blocks):
         for z in range(EZ):
-            v = block[0:56, half_of(z // 2)]
+            v = block[:, half_of(z // 2)]
             wide[pl.ds((2 - EZ * k + z) % rows, 56, stride=rows), :] = lroll(v, GROUP) if z % 2 else v
 
     def entry(i):
@@ -754,7 +754,7 @@
         out[15 + p] = v
 
 
-def k_mid(own, r1, r2, coarse, res, x, inv_out, c_out, far, b, d, y, y2):
+def k_mid(own, r1, r2, below, above, coarse, res, x, inv_out, c_out, far, b, d, y, y2):
     rows = own.shape[1]
     even = parity("row")
     lane = lane_iota((rows, HALF))
@@ -1028,13 +1028,8 @@
                 line[ia] = inv_far[j - 1, ia] * line[ia] * float(K7[0, j] / THETA)
             yf[j, ia] = line[ia]
 
-    def entries(block, start):
-        out = []
-        for i in range(start, start + 4):
-            out.append(block[56 + 8 * (i // 2) : 64 + 8 * (i // 2), half_of(i % 2)])
-        return out
-
-    q_below, q_above, t_below, t_above = entries(from_below, 0), entries(from_above, 0), entries(from_below, 4), entries(from_above, 4)
+    q_below, q_above = [from_below[i] for i in range(4)], [from_above[i] for i in range(4)]
+    t_below, t_above = [from_below[i] for i in range(4, 8)], [from_above[i] for i in range(4, 8)]
     for ia in range(8):
         qz[ia] = both_z(q_below, q_above, ia) - yf[0, ia]
         total = yf[1, ia]
@@ -1084,23 +1079,29 @@
     r1, r2 = swap_a(m1, m2)
     inv, d, y = call(k_first_mean, [FINE, FINE, FINE], name="first_mean")(q, g, stretch, z1, z2)
     faces = (8, 2, 8, HALF)
-    inv, x, rho, block, up, down, ghost = call(k_first_done, [FINE, FINE, FINE, (56, 256), (88, 256), (88, 256), ghosts], [faces, FINE], name="first_done")(
+    inv, x, rho, block, up, down, ghost = call(k_first_done, [FINE, FINE, FINE, (56, 256), message(8), message(8), ghosts], [faces, FINE], name="first_done")(
         rhs, q, g, inv, d, y, stretch, jnp.asarray(RESTRICT), z1, z2, r1, r2
     )
 
     rows = gz * EZ
-    blocks = [block] + [
-        lax.ppermute(up if k == 1 else down if k == gz - 1 else block, "gz", [(i, (i + k) % gz) for i in range(gz)]) for k in range(1, gz)
-    ]
-    column_ = call(functools.partial(k_column, rows), [(PACKED, rows, HALF)], [(56 * rows, HALF)], name="column")(*blocks)[0]
+    blocks = {0: block}
+    for k in sorted(range(1, gz), key=lambda k: -min(k, gz - k)):
+        blocks[k] = lax.ppermute(block, "gz", [(i, (i + k) % gz) for i in range(gz)])
+    blocks = [blocks[k] for k in range(gz)]
+    face = (8, 8, HALF)
+    column_, up, down = call(functools.partial(k_column, rows), [(PACKED, rows, HALF), face, face], [(56 * rows, HALF)], name="column")(
+        up, down, *blocks
+    )
     r1, r2 = swap_a(column_, column_)
+    below = lax.ppermute(up, "gz", [(i, (i + 1) % gz) for i in range(gz)])
+    above = lax.ppermute(down, "gz", [(i, (i - 1) % gz) for i in range(gz)])
     cube, wide = (27, rows, HALF), (27, rows, 2 * HALF)
     coarse, res, xm, inv3, c3, far = call(
         k_mid,
         [(4, rows, GROUP), cube, cube, (8, rows, HALF), (12, rows, HALF), (4, 8, HALF)],
         [wide, wide, wide, (27, rows, HALF)],
         name="mid",
-    )(column_, r1, r2)
+    )(column_, r1, r2, below, above)
 
     inv_far = call(k_far, [(7, 8, 8, HALF)], name="far")(far)[0]
 
@@ -1124,7 +1125,7 @@
         [FINE, FINE, line, line, message(LATER), message(LATER)],
         [cube, cube, cube, (64 * rows, HALF), FINE, FINE, (8, 8, 8, HALF)],
         name="fifth",
-    )(coarse, res, xm, inv3, c3, x, rho, inv, ghost, jnp.asarray(KRON73), far, inv_far, blocks[1], blocks[gz - 1])
+    )(coarse, res, xm, inv3, c3, x, rho, inv, ghost, jnp.asarray(KRON73), far, inv_far, below, above)
     r1, r2 = swap_a(m1, m2)
     d, y = call(k_later_mean, [FINE, FINE], name="later_mean")(q, inv, ghost, qz)
     return call(k_last, [FINE], [faces, FINE], name="last")(q, inv, d, y, x, ghost, qz, tz, r1, r2)[0]

time: 57.3 us -> 58.4 us (1.019)
  starting transfers between devices: 20 us -> 23 us
  waiting for transfers between devices: 21.7 us -> 19.8 us
    ppermute x3, waiting for transfers between devices: 7.53 us -> 3.16 us  [swap_a(): lax.ppermute(m2, 'row', other_row)]
    ppermute x3 -> x5, waiting for transfers between devices: 6.16 us -> 9.98 us  [the longest x3 4.27 us: per_device(): lax.ppermute(block, 'gz', [(i, (i + k) % gz) for i in range(gz)])]
    ppermute x3 -> x5, starting transfers between devices: 3.87 us -> 7.47 us  [the longest x3 3.87 us: per_device(): lax.ppermute(block, 'gz', [(i, (i + k) % gz) for i in range(gz)])]
    ppermute x4, waiting for transfers between devices: 4.27 us -> 2.89 us  [per_device(): lax.ppermute(coarse, 'row', [(i, i ^ k * bit) for i in range(row)])]
  transfers between devices with their start and end apart: 15 -> 17, of which waited for: 9 -> 10; matrix products, arithmetic and copies ran while one was open for 0% -> 0% of each run, Pallas kernels for 3% -> 3%
where the time goes in v3:
time: 58.4 us; the launch traced here: 58.2 us
  starting transfers between devices  23 us (39%)
  waiting for transfers between devices  19.8 us (34%)
  Pallas kernels  13.4 us (23%)
  local copies, waits for them, and re-layouts  1.75 us (3%)
    ppermute x3, starting transfers between devices, swap_a(): lax.ppermute(m2, 'row', other_row)  6.23 us
    ppermute x2, starting transfers between devices, swap_z(): return (lax.ppermute(m1, 'gz', mate_gz), lax.ppermute(m2, 'gz', other_gz))  5.56 us
    ppermute x3, waiting for transfers between devices, per_device(): lax.ppermute(block, 'gz', [(i, (i + k) % gz) for i in range(gz)])  4.27 us
    pallas_call x1, Pallas kernels, per_device(): call(k_fifth, [FINE, FINE, line, line, message(LATER), message(LATER)], [...  4.24 us
    ppermute x1, waiting for transfers between devices, per_device(): below = lax.ppermute(up, 'gz', [(i, (i + 1) % gz) for i in range(gz)])  4.11 us
    ppermute x3, starting transfers between devices, per_device(): lax.ppermute(block, 'gz', [(i, (i + k) % gz) for i in range(gz)])  3.87 us
    ppermute x2, waiting for transfers between devices, swap_z(): return (lax.ppermute(m1, 'gz', mate_gz), lax.ppermute(m2, 'gz', other_gz))  3.77 us
    ppermute x1, starting transfers between devices, per_device(): above = lax.ppermute(down, 'gz', [(i, (i - 1) % gz) for i in range(gz)])  3.6 us
  transfers between devices with their start and end apart: 17, of which 10 were waited for; matrix products, arithmetic and copies ran while one was open for 0% of the time, Pallas kernels for 3%

profile of v3, /device:TPU:0, one launch (start us, length us, event | category | flops | bytes accessed | tf_op | source)
XLA Modules:
  0.0 58.2 jit_solution(648788413865183173)
XLA Ops:
  0.0 0.7 %pad.4.s_any.s_ref = f32[8,256]{1,0:T(8,128)S(1)} pad(f32[3,256]{1,0:T(4,128)} %param.5, f32[]{:T(128)} %constant.54.clone.1), padding=0_5x0_0 | pad | bytes 11268 | tf_op jit(solution)/shard_map/jit(_pad)/pad | solution.py:1074
  0.7 1.0 %copy-done = f32[8,8,8,256]{3,2,1,0:T(8,128)S(1)} copy-done((f32[8,8,8,256]{3,2,1,0:T(8,128)S(1)}, f32[8,8,8,256]{3,2,1,0:T(8,128)}, u32[]{:S(2)}) %copy-start) | copy-done | bytes 524312
  1.7 1.2 %first.1 = (f32[8,8,8,256]{3,2,1,0:T(8,128)S(1)}, f32[8,8,8,256]{3,2,1,0:T(8,128)S(1)}, f32[17,8,128]{2,1,0:T(8,128)S(1)}, f32[17,8,128]{2,1,0:T(8,128)S(1)}) custom-call(f32[8,8,8,256]{3,2,1,0:T(8,128)S(1)} %copy-done, f32[8,256]{1,0:T(8,128)S(1)} %pad.4.s_any.s_ref), custom_call_target="tpu_custom_call" | custom-call | tf_op jit(solution)/shard_map/first/pallas_call | solution.py:1076
  2.9 3.1 %collective-permute-start = (f32[17,8,128]{2,1,0:T(8,128)S(1)}, f32[17,8,128]{2,1,0:T(8,128)S(1)}, u32[]{:S(2)}, u32[]{:S(2)}) collective-permute-start(f32[17,8,128]{2,1,0:T(8,128)S(1)} %get-tuple-element.40), channel_id=1, source_target_pairs={{0,8},{8,0},{16,24},{24,16},{1,9},{9,1},{17,25},{25,17},{2,10},{10... | collective-permute-start | bytes 208904 | tf_op jit(solution)/shard_map/ppermute | solution.py:1069
  6.0 2.5 %collective-permute-start.1 = (f32[17,8,128]{2,1,0:T(8,128)S(1)}, f32[17,8,128]{2,1,0:T(8,128)S(1)}, u32[]{:S(2)}, u32[]{:S(2)}) collective-permute-start(f32[17,8,128]{2,1,0:T(8,128)S(1)} %get-tuple-element.41), channel_id=1, source_target_pairs={{0,24},{8,16},{16,8},{24,0},{1,25},{9,17},{17,9},{25,1},{2,26},{10... | collective-permute-start | bytes 208904 | tf_op jit(solution)/shard_map/ppermute | solution.py:1069
  8.5 3.8 %collective-permute-done.1.z2 = f32[17,8,128]{2,1,0:T(8,128)S(1)} collective-permute-done((f32[17,8,128]{2,1,0:T(8,128)S(1)}, f32[17,8,128]{2,1,0:T(8,128)S(1)}, u32[]{:S(2)}, u32[]{:S(2)}) %collective-permute-start.1) | collective-permute-done | bytes 69664 | tf_op jit(solution)/shard_map/ppermute | solution.py:1069
  12.2 0.2 first_a.1
  12.6 2.5 %collective-permute-start.3 = (f32[17,8,128]{2,1,0:T(8,128)S(1)}, f32[17,8,128]{2,1,0:T(8,128)S(1)}, u32[]{:S(2)}, u32[]{:S(2)}) collective-permute-start(f32[17,8,128]{2,1,0:T(8,128)S(1)} %get-tuple-element.46), channel_id=1, source_target_pairs={{0,7},{1,2},{2,1},{3,4},{4,3},{5,6},{6,5},{7,0},{8,15},{9,10},{10,... | collective-permute-start | bytes 208904 | tf_op jit(solution)/shard_map/ppermute | solution.py:1066
  15.1 0.9 %first_mean.1 = (f32[8,8,8,256]{3,2,1,0:T(8,128)S(1)}, f32[8,8,8,256]{3,2,1,0:T(8,128)S(1)}, f32[8,8,8,256]{3,2,1,0:T(8,128)S(1)}) custom-call(f32[8,8,8,256]{3,2,1,0:T(8,128)S(1)} %get-tuple-element.38.q, f32[8,8,8,256]{3,2,1,0:T(8,128)S(1)} %get-tuple-element.39.g, f32[8,256]{1,0:T(8,128)S(1)} %pad.4.s_any.s_ref, ...), custom_call_target="tpu_custom_call" | custom-call | tf_op jit(solution)/shard_map/first_mean/pallas_call | solution.py:1080
  16.0 1.4 %collective-permute-done.3.r2 = f32[17,8,128]{2,1,0:T(8,128)S(1)} collective-permute-done((f32[17,8,128]{2,1,0:T(8,128)S(1)}, f32[17,8,128]{2,1,0:T(8,128)S(1)}, u32[]{:S(2)}, u32[]{:S(2)}) %collective-permute-start.3) | collective-permute-done | bytes 69664 | tf_op jit(solution)/shard_map/ppermute | solution.py:1066
  17.4 2.2 %first_done.1 = (f32[8,8,8,256]{3,2,1,0:T(8,128)S(1)}, f32[8,8,8,256]{3,2,1,0:T(8,128)S(1)}, f32[8,8,8,256]{3,2,1,0:T(8,128)S(1)}, f32[56,256]{1,0:T(8,128)S(1)}...) custom-call(f32[8,8,8,256]{3,2,1,0:T(8,128)S(1)} %copy-done.1, ...), custom_call_target="tpu_custom_call" | custom-call | tf_op jit(solution)/shard_map/first_done/pallas_call | solution.py:1082
  19.7 3.0 %collective-permute-start.5 = (f32[56,256]{1,0:T(8,128)S(1)}, f32[56,256]{1,0:T(8,128)S(1)}, u32[]{:S(2)}, u32[]{:S(2)}) collective-permute-start(f32[56,256]{1,0:T(8,128)S(1)} %get-tuple-element.49.refs_2_), channel_id=1, source_target_pairs={{0,16},{8,24},{16,0},{24,8},{1,17},{9,25},{17,1},{25,9},{2,18},{10... | collective-permute-start | bytes 172040 | tf_op jit(solution)/shard_map/ppermute | solution.py:1089
  22.7 0.8 %collective-permute-start.6 = (f32[56,256]{1,0:T(8,128)S(1)}, f32[56,256]{1,0:T(8,128)S(1)}, u32[]{:S(2)}, u32[]{:S(2)}) collective-permute-start(f32[56,256]{1,0:T(8,128)S(1)} %get-tuple-element.49.refs_2_), channel_id=1, source_target_pairs={{0,24},{8,0},{16,8},{24,16},{1,25},{9,1},{17,9},{25,17},{2,26},{10... | collective-permute-start | bytes 172040 | tf_op jit(solution)/shard_map/ppermute | solution.py:1089
  23.5 2.7 %collective-permute-done.4.refs_3_ = f32[56,256]{1,0:T(8,128)S(1)} collective-permute-done((f32[56,256]{1,0:T(8,128)S(1)}, f32[56,256]{1,0:T(8,128)S(1)}, u32[]{:S(2)}, u32[]{:S(2)}) %collective-permute-start.4) | collective-permute-done | bytes 57376 | tf_op jit(solution)/shard_map/ppermute | solution.py:1089
  26.3 1.5 %collective-permute-done.5.refs_4_ = f32[56,256]{1,0:T(8,128)S(1)} collective-permute-done((f32[56,256]{1,0:T(8,128)S(1)}, f32[56,256]{1,0:T(8,128)S(1)}, u32[]{:S(2)}, u32[]{:S(2)}) %collective-permute-start.5) | collective-permute-done | bytes 57376 | tf_op jit(solution)/shard_map/ppermute | solution.py:1089
  27.8 0.3 column.1
  28.2 1.8 %collective-permute-start.8 = (f32[17,16,128]{2,1,0:T(8,128)S(1)}, f32[17,16,128]{2,1,0:T(8,128)S(1)}, u32[]{:S(2)}, u32[]{:S(2)}) collective-permute-start(f32[17,16,128]{2,1,0:T(8,128)S(1)} %get-tuple-element.50.own), channel_id=1, source_target_pairs={{0,7},{1,2},{2,1},{3,4},{4,3},{5,6},{6,5},{7,0},{8,15},{9,10},{10,... | collective-permute-start | bytes 417800 | tf_op jit(solution)/shard_map/ppermute | solution.py:1066
  30.0 3.6 %collective-permute-start.10 = (f32[8,8,128]{2,1,0:T(8,128)S(1)}, f32[8,8,128]{2,1,0:T(8,128)S(1)}, u32[]{:S(2)}, u32[]{:S(2)}) collective-permute-start(f32[8,8,128]{2,1,0:T(8,128)S(1)} %get-tuple-element.52), channel_id=1, source_target_pairs={{0,24},{8,0},{16,8},{24,16},{1,25},{9,1},{17,9},{25,17},{2,26},{10... | collective-permute-start | bytes 98312 | tf_op jit(solution)/shard_map/ppermute | solution.py:1097
  33.6 1.6 %collective-permute-done.10.above.from_above = f32[8,8,128]{2,1,0:T(8,128)S(1)} collective-permute-done((f32[8,8,128]{2,1,0:T(8,128)S(1)}, f32[8,8,128]{2,1,0:T(8,128)S(1)}, u32[]{:S(2)}, u32[]{:S(2)}) %collective-permute-start.10) | collective-permute-done | bytes 32800 | tf_op jit(solution)/shard_map/ppermute | solution.py:1097
  35.2 4.1 %collective-permute-done.9.below.from_below = f32[8,8,128]{2,1,0:T(8,128)S(1)} collective-permute-done((f32[8,8,128]{2,1,0:T(8,128)S(1)}, f32[8,8,128]{2,1,0:T(8,128)S(1)}, u32[]{:S(2)}, u32[]{:S(2)}) %collective-permute-start.9) | collective-permute-done | bytes 32800 | tf_op jit(solution)/shard_map/ppermute | solution.py:1096
  39.3 1.8 %mid.1 = (f32[4,16,64]{2,1,0:T(8,128)S(1)}, f32[27,16,128]{2,1,0:T(8,128)S(1)}, f32[27,16,128]{2,1,0:T(8,128)S(1)}, f32[8,16,128]{2,1,0:T(8,128)S(1)}, f32[12,16...) custom-call(f32[17,16,128]{2,1,0:T(8,128)S(1)} %get-tuple-element.50.own, f32[17,16,128]{2,1,0:T(8,128)S(1)} %collective-permute-done.7.r1, ...), custom_call_target="tpu_custom_call" | custom-call | tf_op jit(solution)/shard_map/mid/pallas_call | solution.py:1099
  41.1 1.2 %collective-permute-done.11 = f32[4,16,64]{2,1,0:T(8,128)S(1)} collective-permute-done((f32[4,16,64]{2,1,0:T(8,128)S(1)}, f32[4,16,64]{2,1,0:T(8,128)S(1)}, u32[]{:S(2)}, u32[]{:S(2)}) %collective-permute-start.11) | collective-permute-done | bytes 16416 | tf_op jit(solution)/shard_map/ppermute | solution.py:1112
  42.5 0.8 %collective-permute-start.13 = (f32[4,16,128]{2,1,0:T(8,128)S(1)}, f32[4,16,128]{2,1,0:T(8,128)S(1)}, u32[]{:S(2)}, u32[]{:S(2)}) collective-permute-start(f32[4,16,128]{2,1,0:T(8,128)S(1)} %pad_maximum_fusion.1), channel_id=1, source_target_pairs={{0,4},{1,5},{2,6},{3,7},{4,0},{5,1},{6,2},{7,3},{8,12},{9,13},{10,... | collective-permute-start | bytes 98312 | tf_op jit(solution)/shard_map/ppermute | solution.py:1112
  43.3 2.6 %collective-permute-start.14 = (f32[4,16,128]{2,1,0:T(8,128)S(1)}, f32[4,16,128]{2,1,0:T(8,128)S(1)}, u32[]{:S(2)}, u32[]{:S(2)}) collective-permute-start(f32[4,16,128]{2,1,0:T(8,128)S(1)} %pad_maximum_fusion.1), channel_id=1, source_target_pairs={{0,2},{1,3},{2,0},{3,1},{4,6},{5,7},{6,4},{7,5},{8,10},{9,11},{10,... | collective-permute-start | bytes 98312 | tf_op jit(solution)/shard_map/ppermute | solution.py:1112
  45.9 0.2 far.1.inv_far
  46.1 1.1 %collective-permute-done.12 = f32[4,16,128]{2,1,0:T(8,128)S(1)} collective-permute-done((f32[4,16,128]{2,1,0:T(8,128)S(1)}, f32[4,16,128]{2,1,0:T(8,128)S(1)}, u32[]{:S(2)}, u32[]{:S(2)}) %collective-permute-start.12) | collective-permute-done | bytes 32800 | tf_op jit(solution)/shard_map/ppermute | solution.py:1112
  47.2 0.6 collective-permute-done.14
  47.9 4.2 %fifth.1 = (f32[8,8,8,256]{3,2,1,0:T(8,128)S(1)}, f32[8,8,8,256]{3,2,1,0:T(8,128)S(1)}, f32[8,8,128]{2,1,0:T(8,128)S(1)}, f32[8,8,128]{2,1,0:T(8,128)S(1)}, f32[...) custom-call(f32[4,16,512]{2,1,0:T(8,128)S(1)} %pad_maximum_fusion.whole, f32[27,16,128]{2,1,0:T(8,128)S(1)} %get-tuple-element.54.res, ...), custom_call_target="tpu_custom_call" | custom-call | tf_op jit(solution)/shard_map/fifth/pallas_call | solution.py:1123
  52.2 1.9 %collective-permute-start.16 = (f32[9,8,128]{2,1,0:T(8,128)S(1)}, f32[9,8,128]{2,1,0:T(8,128)S(1)}, u32[]{:S(2)}, u32[]{:S(2)}) collective-permute-start(f32[9,8,128]{2,1,0:T(8,128)S(1)} %get-tuple-element.70), channel_id=1, source_target_pairs={{0,7},{1,2},{2,1},{3,4},{4,3},{5,6},{6,5},{7,0},{8,15},{9,10},{10,... | collective-permute-start | bytes 110600 | tf_op jit(solution)/shard_map/ppermute | solution.py:1066
  54.0 0.9 %later_mean.1 = (f32[8,8,8,256]{3,2,1,0:T(8,128)S(1)}, f32[8,8,8,256]{3,2,1,0:T(8,128)S(1)}) custom-call(f32[8,8,8,256]{3,2,1,0:T(8,128)S(1)} %get-tuple-element.63.q, f32[8,8,8,256]{3,2,1,0:T(8,128)S(1)} %get-tuple-element.60.inv, f32[6,8,128]{2,1,0:T(8,128)S(1)} %get-tuple-element.61.ghost, f32[8,8,128]{2,1,0:T(8,128)S(1)} %get-tuple-element.64.qz), custom_call_target="tpu_custom_call" | custom-call | tf_op jit(solution)/shard_map/later_mean/pallas_call | solution.py:1130
  54.9 1.8 %collective-permute-done.16.r2 = f32[9,8,128]{2,1,0:T(8,128)S(1)} collective-permute-done((f32[9,8,128]{2,1,0:T(8,128)S(1)}, f32[9,8,128]{2,1,0:T(8,128)S(1)}, u32[]{:S(2)}, u32[]{:S(2)}) %collective-permute-start.16) | collective-permute-done | bytes 36896 | tf_op jit(solution)/shard_map/ppermute | solution.py:1066
  56.7 1.5 %last.1 = f32[8,8,8,256]{3,2,1,0:T(8,128)} custom-call(f32[8,8,8,256]{3,2,1,0:T(8,128)S(1)} %get-tuple-element.63.q, f32[8,8,8,256]{3,2,1,0:T(8,128)S(1)} %get-tuple-element.60.inv, f32[8,8,8,256]{3,2,1,0:T(8,128)S(1)} %get-tuple-element.65.d, f32[8,8,8,256]{3,2,1,0:T(8,128)S(1)} %get-tuple-element.66.y0, f32[8,8,8,256]{3,2,1,0:T(8,128)S(1)} %get-tuple-element.67.x, ...), custom_call_target="tpu_custom_call" | custom-call | tf_op jit(solution)/shard_map/last/pallas_call | solution.py:1131
  (25 shorter events, 0.5 us)
Async XLA Ops:
  0.7 1.0 %copy-start = (f32[8,8,8,256]{3,2,1,0:T(8,128)S(1)}, f32[8,8,8,256]{3,2,1,0:T(8,128)}, u32[]{:S(2)}) copy-start(f32[8,8,8,256]{3,2,1,0:T(8,128)} %rhs.1) | copy-start | bytes 1572868
  2.9 5.6 %collective-permute-start = (f32[17,8,128]{2,1,0:T(8,128)S(1)}, f32[17,8,128]{2,1,0:T(8,128)S(1)}, u32[]{:S(2)}, u32[]{:S(2)}) collective-permute-start(f32[17,8,128]{2,1,0:T(8,128)S(1)} %get-tuple-element.40), channel_id=1, source_target_pairs={{0,8},{8,0},{16,24},{24,16},{1,9},{9,1},{17,25},{25,17},{2,10},{10... | collective-permute-start | bytes 208904 | tf_op jit(solution)/shard_map/ppermute | solution.py:1069
  6.0 6.2 %collective-permute-start.1 = (f32[17,8,128]{2,1,0:T(8,128)S(1)}, f32[17,8,128]{2,1,0:T(8,128)S(1)}, u32[]{:S(2)}, u32[]{:S(2)}) collective-permute-start(f32[17,8,128]{2,1,0:T(8,128)S(1)} %get-tuple-element.41), channel_id=1, source_target_pairs={{0,24},{8,16},{16,8},{24,0},{1,25},{9,17},{17,9},{25,1},{2,26},{10... | collective-permute-start | bytes 208904 | tf_op jit(solution)/shard_map/ppermute | solution.py:1069
  12.5 3.6 %collective-permute-start.2 = (f32[17,8,128]{2,1,0:T(8,128)S(1)}, f32[17,8,128]{2,1,0:T(8,128)S(1)}, u32[]{:S(2)}, u32[]{:S(2)}) collective-permute-start(f32[17,8,128]{2,1,0:T(8,128)S(1)} %get-tuple-element.45), channel_id=1, source_target_pairs={{0,1},{1,0},{2,3},{3,2},{4,5},{5,4},{6,7},{7,6},{8,9},{9,8},{10,11... | collective-permute-start | bytes 208904 | tf_op jit(solution)/shard_map/ppermute | solution.py:1066
  12.6 4.9 %copy-start.1 = (f32[8,8,8,256]{3,2,1,0:T(8,128)S(1)}, f32[8,8,8,256]{3,2,1,0:T(8,128)}, u32[]{:S(2)}) copy-start(f32[8,8,8,256]{3,2,1,0:T(8,128)} %rhs.1) | copy-start | bytes 1572868
  12.6 4.9 %copy-start.3 = (bf16[224,512]{1,0:T(8,128)(2,1)S(1)}, bf16[224,512]{1,0:T(8,128)(2,1)}, u32[]{:S(2)}) copy-start(bf16[224,512]{1,0:T(8,128)(2,1)} %constant.55.clone.table) | copy-start | bytes 688132
  12.6 4.8 %collective-permute-start.3 = (f32[17,8,128]{2,1,0:T(8,128)S(1)}, f32[17,8,128]{2,1,0:T(8,128)S(1)}, u32[]{:S(2)}, u32[]{:S(2)}) collective-permute-start(f32[17,8,128]{2,1,0:T(8,128)S(1)} %get-tuple-element.46), channel_id=1, source_target_pairs={{0,7},{1,2},{2,1},{3,4},{4,3},{5,6},{6,5},{7,0},{8,15},{9,10},{10,... | collective-permute-start | bytes 208904 | tf_op jit(solution)/shard_map/ppermute | solution.py:1066
  19.6 6.6 %collective-permute-start.4 = (f32[56,256]{1,0:T(8,128)S(1)}, f32[56,256]{1,0:T(8,128)S(1)}, u32[]{:S(2)}, u32[]{:S(2)}) collective-permute-start(f32[56,256]{1,0:T(8,128)S(1)} %get-tuple-element.49.refs_2_), channel_id=1, source_target_pairs={{0,8},{8,16},{16,24},{24,0},{1,9},{9,17},{17,25},{25,1},{2,10},{10... | collective-permute-start | bytes 172040 | tf_op jit(solution)/shard_map/ppermute | solution.py:1089
  19.7 8.1 %collective-permute-start.5 = (f32[56,256]{1,0:T(8,128)S(1)}, f32[56,256]{1,0:T(8,128)S(1)}, u32[]{:S(2)}, u32[]{:S(2)}) collective-permute-start(f32[56,256]{1,0:T(8,128)S(1)} %get-tuple-element.49.refs_2_), channel_id=1, source_target_pairs={{0,16},{8,24},{16,0},{24,8},{1,17},{9,25},{17,1},{25,9},{2,18},{10... | collective-permute-start | bytes 172040 | tf_op jit(solution)/shard_map/ppermute | solution.py:1089
  22.7 5.1 %collective-permute-start.6 = (f32[56,256]{1,0:T(8,128)S(1)}, f32[56,256]{1,0:T(8,128)S(1)}, u32[]{:S(2)}, u32[]{:S(2)}) collective-permute-start(f32[56,256]{1,0:T(8,128)S(1)} %get-tuple-element.49.refs_2_), channel_id=1, source_target_pairs={{0,24},{8,0},{16,8},{24,16},{1,25},{9,1},{17,9},{25,17},{2,26},{10... | collective-permute-start | bytes 172040 | tf_op jit(solution)/shard_map/ppermute | solution.py:1089
  28.1 11.2 %collective-permute-start.7 = (f32[17,16,128]{2,1,0:T(8,128)S(1)}, f32[17,16,128]{2,1,0:T(8,128)S(1)}, u32[]{:S(2)}, u32[]{:S(2)}) collective-permute-start(f32[17,16,128]{2,1,0:T(8,128)S(1)} %get-tuple-element.50.own), channel_id=1, source_target_pairs={{0,1},{1,0},{2,3},{3,2},{4,5},{5,4},{6,7},{7,6},{8,9},{9,8},{10,11... | collective-permute-start | bytes 417800 | tf_op jit(solution)/shard_map/ppermute | solution.py:1066
  28.2 11.2 %collective-permute-start.8 = (f32[17,16,128]{2,1,0:T(8,128)S(1)}, f32[17,16,128]{2,1,0:T(8,128)S(1)}, u32[]{:S(2)}, u32[]{:S(2)}) collective-permute-start(f32[17,16,128]{2,1,0:T(8,128)S(1)} %get-tuple-element.50.own), channel_id=1, source_target_pairs={{0,7},{1,2},{2,1},{3,4},{4,3},{5,6},{6,5},{7,0},{8,15},{9,10},{10,... | collective-permute-start | bytes 417800 | tf_op jit(solution)/shard_map/ppermute | solution.py:1066
  30.0 5.2 %collective-permute-start.10 = (f32[8,8,128]{2,1,0:T(8,128)S(1)}, f32[8,8,128]{2,1,0:T(8,128)S(1)}, u32[]{:S(2)}, u32[]{:S(2)}) collective-permute-start(f32[8,8,128]{2,1,0:T(8,128)S(1)} %get-tuple-element.52), channel_id=1, source_target_pairs={{0,24},{8,0},{16,8},{24,16},{1,25},{9,1},{17,9},{25,17},{2,26},{10... | collective-permute-start | bytes 98312 | tf_op jit(solution)/shard_map/ppermute | solution.py:1097
  33.6 5.7 %collective-permute-start.9 = (f32[8,8,128]{2,1,0:T(8,128)S(1)}, f32[8,8,128]{2,1,0:T(8,128)S(1)}, u32[]{:S(2)}, u32[]{:S(2)}) collective-permute-start(f32[8,8,128]{2,1,0:T(8,128)S(1)} %get-tuple-element.51), channel_id=1, source_target_pairs={{0,8},{8,16},{16,24},{24,0},{1,9},{9,17},{17,25},{25,1},{2,10},{10... | collective-permute-start | bytes 98312 | tf_op jit(solution)/shard_map/ppermute | solution.py:1096
  41.1 1.2 %collective-permute-start.11 = (f32[4,16,64]{2,1,0:T(8,128)S(1)}, f32[4,16,64]{2,1,0:T(8,128)S(1)}, u32[]{:S(2)}, u32[]{:S(2)}) collective-permute-start(f32[4,16,64]{2,1,0:T(8,128)S(1)} %get-tuple-element.53), channel_id=1, source_target_pairs={{0,1},{1,0},{2,3},{3,2},{4,5},{5,4},{6,7},{7,6},{8,9},{9,8},{10,11... | collective-permute-start | bytes 49160 | tf_op jit(solution)/shard_map/ppermute | solution.py:1112
  42.4 4.8 %collective-permute-start.12 = (f32[4,16,128]{2,1,0:T(8,128)S(1)}, f32[4,16,128]{2,1,0:T(8,128)S(1)}, u32[]{:S(2)}, u32[]{:S(2)}) collective-permute-start(f32[4,16,128]{2,1,0:T(8,128)S(1)} %pad_maximum_fusion.1), channel_id=1, source_target_pairs={{0,6},{1,7},{2,4},{3,5},{4,2},{5,3},{6,0},{7,1},{8,14},{9,15},{10,... | collective-permute-start | bytes 98312 | tf_op jit(solution)/shard_map/ppermute | solution.py:1112
  42.5 4.8 %collective-permute-start.13 = (f32[4,16,128]{2,1,0:T(8,128)S(1)}, f32[4,16,128]{2,1,0:T(8,128)S(1)}, u32[]{:S(2)}, u32[]{:S(2)}) collective-permute-start(f32[4,16,128]{2,1,0:T(8,128)S(1)} %pad_maximum_fusion.1), channel_id=1, source_target_pairs={{0,4},{1,5},{2,6},{3,7},{4,0},{5,1},{6,2},{7,3},{8,12},{9,13},{10,... | collective-permute-start | bytes 98312 | tf_op jit(solution)/shard_map/ppermute | solution.py:1112
  43.3 4.5 %collective-permute-start.14 = (f32[4,16,128]{2,1,0:T(8,128)S(1)}, f32[4,16,128]{2,1,0:T(8,128)S(1)}, u32[]{:S(2)}, u32[]{:S(2)}) collective-permute-start(f32[4,16,128]{2,1,0:T(8,128)S(1)} %pad_maximum_fusion.1), channel_id=1, source_target_pairs={{0,2},{1,3},{2,0},{3,1},{4,6},{5,7},{6,4},{7,5},{8,10},{9,11},{10,... | collective-permute-start | bytes 98312 | tf_op jit(solution)/shard_map/ppermute | solution.py:1112
  46.1 1.8 %copy-start.2 = (bf16[512,192]{1,0:T(8,128)(2,1)S(1)}, bf16[512,192]{1,0:T(8,128)(2,1)}, u32[]{:S(2)}) copy-start(bf16[512,192]{1,0:T(8,128)(2,1)} %constant.56.clone.kron) | copy-start | bytes 589828
  52.1 2.8 %collective-permute-start.15 = (f32[9,8,128]{2,1,0:T(8,128)S(1)}, f32[9,8,128]{2,1,0:T(8,128)S(1)}, u32[]{:S(2)}, u32[]{:S(2)}) collective-permute-start(f32[9,8,128]{2,1,0:T(8,128)S(1)} %get-tuple-element.69), channel_id=1, source_target_pairs={{0,1},{1,0},{2,3},{3,2},{4,5},{5,4},{6,7},{7,6},{8,9},{9,8},{10,11... | collective-permute-start | bytes 110600 | tf_op jit(solution)/shard_map/ppermute | solution.py:1066
  52.2 4.5 %collective-permute-start.16 = (f32[9,8,128]{2,1,0:T(8,128)S(1)}, f32[9,8,128]{2,1,0:T(8,128)S(1)}, u32[]{:S(2)}, u32[]{:S(2)}) collective-permute-start(f32[9,8,128]{2,1,0:T(8,128)S(1)} %get-tuple-element.70), channel_id=1, source_target_pairs={{0,7},{1,2},{2,1},{3,4},{4,3},{5,6},{6,5},{7,0},{8,15},{9,10},{10,... | collective-permute-start | bytes 110600 | tf_op jit(solution)/shard_map/ppermute | solution.py:1066

commit v4 on v2

--- a/solution.py
+++ b/solution.py
@@ -303,18 +303,16 @@
     return out
 
 
-def k_first(rhs_any, s_any, q, g, m1, m2, s_ref, rhs, sems):
-    copy_s = pltpu.make_async_copy(s_any, s_ref, sems.at[0])
-    copy_rhs = pltpu.make_async_copy(rhs_any, rhs, sems.at[1])
-    copy_s.start()
-    copy_rhs.start()
+def k_diag(s_ref, g):
     masks = radial_masks()
     wr, kr = column(W7), column(np.diag(K7))
-    copy_s.wait()
     for iz, ia, sl in every_fine():
         g[iz, ia, :, sl] = radial_add(diag_at(s_ref, sl.start // HALF, iz, ia, wr, kr), masks)
     sum_inside(g)
-    copy_rhs.wait()
+
+
+def k_first(rhs, s_ref, g, q, m1, m2):
+    masks = radial_masks()
     for iz, ia, sl in every_fine():
         q[iz, ia, :, sl] = radial_add(rhs[iz, ia, :, sl], masks)
     sum_inside(q)
@@ -1048,15 +1046,14 @@
 FINE = (8, 8, 8, 256)
 
 
-def call(body, outs, scratch=(), name=None, far=0):
+def call(body, outs, scratch=(), name=None, cost=None):
     shapes = [jax.ShapeDtypeStruct(s, jnp.float32) for s in outs]
-    specs = dict(in_specs=[pl.BlockSpec(memory_space=pltpu.HBM)] * far) if far else {}
     return pl.pallas_call(
         body,
         out_shape=shapes,
-        scratch_shapes=[pltpu.VMEM(s, jnp.float32) for s in scratch] + ([pltpu.SemaphoreType.DMA((far,))] if far else []),
-        **specs,
+        scratch_shapes=[pltpu.VMEM(s, jnp.float32) for s in scratch],
         compiler_params=pltpu.CompilerParams(vmem_limit_bytes=32 * 1024 * 1024),
+        cost_estimate=cost,
         name=name,
     )
 
@@ -1078,7 +1075,9 @@
 
     stretch = jnp.pad(stretch, ((0, 5), (0, 0)))
     ghosts = (6, 8, HALF)
-    q, g, m1, m2 = call(k_first, [FINE, FINE, message(FIRST), message(FIRST)], [(8, 256), FINE], name="first", far=2)(rhs, stretch)
+    work = pl.CostEstimate(flops=40 * rhs.size, bytes_accessed=4 * rhs.size, transcendentals=0)
+    g = call(k_diag, [FINE], name="diag", cost=work)(stretch)[0]
+    q, m1, m2 = call(k_first, [FINE, message(FIRST), message(FIRST)], name="first")(rhs, stretch, g)
     z1, z2 = swap_z(m1, m2)
     m1, m2 = call(k_first_a, [message(FIRST), message(FIRST)], name="first_a")(q, g, stretch, z1, z2)
     r1, r2 = swap_a(m1, m2)

time: 57.3 us -> 56.1 us (0.979)
  local copies, waits for them, and re-layouts: 1.75 us -> 0.77 us
    unnamed x8 -> x6, local copies, waits for them, and re-layouts: 1.06 us -> 0.02 us
    pallas_call x1 -> x2, Pallas kernels: 1.17 us -> 1.1 us  [the longest x1 0.63 us: per_device(): call(k_first, [FINE, message(FIRST), message(FIRST)], name='first')]
  transfers between devices with their start and end apart: 15 -> 15, of which waited for: 9 -> 9; matrix products, arithmetic and copies ran while one was open for 0% -> 0% of each run, Pallas kernels for 3% -> 4%
where the time goes in v4:
time: 56.1 us; the launch traced here: 56 us
  waiting for transfers between devices  21.6 us (39%)
  starting transfers between devices  20 us (36%)
  Pallas kernels  13.3 us (24%)
  local copies, waits for them, and re-layouts  0.77 us (1%)
    ppermute x3, waiting for transfers between devices, swap_a(): lax.ppermute(m2, 'row', other_row)  7.43 us
    ppermute x3, starting transfers between devices, swap_a(): lax.ppermute(m2, 'row', other_row)  6.77 us
    ppermute x3, waiting for transfers between devices, per_device(): lax.ppermute(up if k == 1 else down if k == gz - 1 else block, 'gz', [(i,...  6.16 us
    ppermute x2, starting transfers between devices, swap_z(): return (lax.ppermute(m1, 'gz', mate_gz), lax.ppermute(m2, 'gz', other_gz))  5.56 us
    ppermute x4, waiting for transfers between devices, per_device(): lax.ppermute(coarse, 'row', [(i, i ^ k * bit) for i in range(row)])  4.26 us
    pallas_call x1, Pallas kernels, per_device(): call(k_fifth, [FINE, FINE, line, line, message(LATER), message(LATER)], [...  4.24 us
    ppermute x3, starting transfers between devices, per_device(): lax.ppermute(up if k == 1 else down if k == gz - 1 else block, 'gz', [(i,...  3.87 us
    ppermute x2, waiting for transfers between devices, swap_z(): return (lax.ppermute(m1, 'gz', mate_gz), lax.ppermute(m2, 'gz', other_gz))  3.77 us
  transfers between devices with their start and end apart: 15, of which 9 were waited for; matrix products, arithmetic and copies ran while one was open for 0% of the time, Pallas kernels for 4%

profile of v4, /device:TPU:0, one launch (start us, length us, event | category | flops | bytes accessed | tf_op | source)
XLA Modules:
  0.0 56.0 jit_solution(7083493597188334239)
XLA Ops:
  0.0 0.7 %pad.4.s_ref = f32[8,256]{1,0:T(8,128)S(1)} pad(f32[3,256]{1,0:T(4,128)} %param.5, f32[]{:T(128)} %constant.54.clone.1), padding=0_5x0_0 | pad | bytes 11268 | tf_op jit(solution)/shard_map/jit(_pad)/pad | solution.py:1076
  0.8 0.5 diag.1.g
  1.2 0.6 %first.1 = (f32[8,8,8,256]{3,2,1,0:T(8,128)S(1)}, f32[17,8,128]{2,1,0:T(8,128)S(1)}, f32[17,8,128]{2,1,0:T(8,128)S(1)}) custom-call(f32[8,8,8,256]{3,2,1,0:T(8,128)S(1)} %copy-done, f32[8,256]{1,0:T(8,128)S(1)} %pad.4.s_ref, f32[8,8,8,256]{3,2,1,0:T(8,128)S(1)} %diag.1.g), custom_call_target="tpu_custom_call" | custom-call | tf_op jit(solution)/shard_map/first/pallas_call | solution.py:1080
  1.9 3.1 %collective-permute-start = (f32[17,8,128]{2,1,0:T(8,128)S(1)}, f32[17,8,128]{2,1,0:T(8,128)S(1)}, u32[]{:S(2)}, u32[]{:S(2)}) collective-permute-start(f32[17,8,128]{2,1,0:T(8,128)S(1)} %get-tuple-element.35), channel_id=1, source_target_pairs={{0,8},{8,0},{16,24},{24,16},{1,9},{9,1},{17,25},{25,17},{2,10},{10... | collective-permute-start | bytes 208904 | tf_op jit(solution)/shard_map/ppermute | solution.py:1071
  5.0 2.5 %collective-permute-start.1 = (f32[17,8,128]{2,1,0:T(8,128)S(1)}, f32[17,8,128]{2,1,0:T(8,128)S(1)}, u32[]{:S(2)}, u32[]{:S(2)}) collective-permute-start(f32[17,8,128]{2,1,0:T(8,128)S(1)} %get-tuple-element.36), channel_id=1, source_target_pairs={{0,24},{8,16},{16,8},{24,0},{1,25},{9,17},{17,9},{25,1},{2,26},{10... | collective-permute-start | bytes 208904 | tf_op jit(solution)/shard_map/ppermute | solution.py:1071
  7.4 3.8 %collective-permute-done.1.z2 = f32[17,8,128]{2,1,0:T(8,128)S(1)} collective-permute-done((f32[17,8,128]{2,1,0:T(8,128)S(1)}, f32[17,8,128]{2,1,0:T(8,128)S(1)}, u32[]{:S(2)}, u32[]{:S(2)}) %collective-permute-start.1) | collective-permute-done | bytes 69664 | tf_op jit(solution)/shard_map/ppermute | solution.py:1071
  11.2 0.2 first_a.1
  11.5 2.5 %collective-permute-start.3 = (f32[17,8,128]{2,1,0:T(8,128)S(1)}, f32[17,8,128]{2,1,0:T(8,128)S(1)}, u32[]{:S(2)}, u32[]{:S(2)}) collective-permute-start(f32[17,8,128]{2,1,0:T(8,128)S(1)} %get-tuple-element.41), channel_id=1, source_target_pairs={{0,7},{1,2},{2,1},{3,4},{4,3},{5,6},{6,5},{7,0},{8,15},{9,10},{10,... | collective-permute-start | bytes 208904 | tf_op jit(solution)/shard_map/ppermute | solution.py:1068
  14.1 1.0 %first_mean.1 = (f32[8,8,8,256]{3,2,1,0:T(8,128)S(1)}, f32[8,8,8,256]{3,2,1,0:T(8,128)S(1)}, f32[8,8,8,256]{3,2,1,0:T(8,128)S(1)}) custom-call(f32[8,8,8,256]{3,2,1,0:T(8,128)S(1)} %get-tuple-element.34.q, f32[8,8,8,256]{3,2,1,0:T(8,128)S(1)} %diag.1.g, f32[8,256]{1,0:T(8,128)S(1)} %pad.4.s_ref, f32[17,8,128]{2,1,0:T(8,128)S(1)} %collective-permute-done.z1, ...), custom_call_target="tpu_custom_call" | custom-call | tf_op jit(solution)/shard_map/first_mean/pallas_call | solution.py:1084
  15.0 1.3 %collective-permute-done.3.r2 = f32[17,8,128]{2,1,0:T(8,128)S(1)} collective-permute-done((f32[17,8,128]{2,1,0:T(8,128)S(1)}, f32[17,8,128]{2,1,0:T(8,128)S(1)}, u32[]{:S(2)}, u32[]{:S(2)}) %collective-permute-start.3) | collective-permute-done | bytes 69664 | tf_op jit(solution)/shard_map/ppermute | solution.py:1068
  16.4 2.2 %first_done.1 = (f32[8,8,8,256]{3,2,1,0:T(8,128)S(1)}, f32[8,8,8,256]{3,2,1,0:T(8,128)S(1)}, f32[8,8,8,256]{3,2,1,0:T(8,128)S(1)}, f32[56,256]{1,0:T(8,128)S(1)}...) custom-call(f32[8,8,8,256]{3,2,1,0:T(8,128)S(1)} %copy-done, ...), custom_call_target="tpu_custom_call" | custom-call | tf_op jit(solution)/shard_map/first_done/pallas_call | solution.py:1086
  18.6 3.8 %collective-permute-start.6 = (f32[88,256]{1,0:T(8,128)S(1)}, f32[88,256]{1,0:T(8,128)S(1)}, u32[]{:S(2)}, u32[]{:S(2)}) collective-permute-start(f32[88,256]{1,0:T(8,128)S(1)} %get-tuple-element.44), channel_id=1, source_target_pairs={{0,24},{8,0},{16,8},{24,16},{1,25},{9,1},{17,9},{25,17},{2,26},{10... | collective-permute-start | bytes 270344 | tf_op jit(solution)/shard_map/ppermute | solution.py:1092
  22.4 6.2 %collective-permute-done.5.refs_2_ = f32[56,256]{1,0:T(8,128)S(1)} collective-permute-done((f32[56,256]{1,0:T(8,128)S(1)}, f32[56,256]{1,0:T(8,128)S(1)}, u32[]{:S(2)}, u32[]{:S(2)}) %collective-permute-start.5) | collective-permute-done | bytes 57376 | tf_op jit(solution)/shard_map/ppermute | solution.py:1092
  28.6 0.3 column.1.own
  29.0 2.5 %collective-permute-start.8 = (f32[17,16,128]{2,1,0:T(8,128)S(1)}, f32[17,16,128]{2,1,0:T(8,128)S(1)}, u32[]{:S(2)}, u32[]{:S(2)}) collective-permute-start(f32[17,16,128]{2,1,0:T(8,128)S(1)} %column.1.own), channel_id=1, source_target_pairs={{0,7},{1,2},{2,1},{3,4},{4,3},{5,6},{6,5},{7,0},{8,15},{9,10},{10,... | collective-permute-start | bytes 417800 | tf_op jit(solution)/shard_map/ppermute | solution.py:1068
  31.5 4.0 %collective-permute-done.8.r2 = f32[17,16,128]{2,1,0:T(8,128)S(1)} collective-permute-done((f32[17,16,128]{2,1,0:T(8,128)S(1)}, f32[17,16,128]{2,1,0:T(8,128)S(1)}, u32[]{:S(2)}, u32[]{:S(2)}) %collective-permute-start.8) | collective-permute-done | bytes 139296 | tf_op jit(solution)/shard_map/ppermute | solution.py:1068
  35.5 1.8 %mid.1 = (f32[4,16,64]{2,1,0:T(8,128)S(1)}, f32[27,16,128]{2,1,0:T(8,128)S(1)}, f32[27,16,128]{2,1,0:T(8,128)S(1)}, f32[8,16,128]{2,1,0:T(8,128)S(1)}, f32[12,16...) custom-call(f32[17,16,128]{2,1,0:T(8,128)S(1)} %column.1.own, f32[17,16,128]{2,1,0:T(8,128)S(1)} %collective-permute-done.7.r1, ...), custom_call_target="tpu_custom_call" | custom-call | tf_op jit(solution)/shard_map/mid/pallas_call | solution.py:1097
  37.3 0.1 collective-permute-start.9
  37.4 1.1 %collective-permute-done.9 = f32[4,16,64]{2,1,0:T(8,128)S(1)} collective-permute-done((f32[4,16,64]{2,1,0:T(8,128)S(1)}, f32[4,16,64]{2,1,0:T(8,128)S(1)}, u32[]{:S(2)}, u32[]{:S(2)}) %collective-permute-start.9) | collective-permute-done | bytes 16416 | tf_op jit(solution)/shard_map/ppermute | solution.py:1110
  38.5 0.1 pad_maximum_fusion.1
  38.6 1.7 %collective-permute-start.10 = (f32[4,16,128]{2,1,0:T(8,128)S(1)}, f32[4,16,128]{2,1,0:T(8,128)S(1)}, u32[]{:S(2)}, u32[]{:S(2)}) collective-permute-start(f32[4,16,128]{2,1,0:T(8,128)S(1)} %pad_maximum_fusion.1), channel_id=1, source_target_pairs={{0,6},{1,7},{2,4},{3,5},{4,2},{5,3},{6,0},{7,1},{8,14},{9,15},{10,... | collective-permute-start | bytes 98312 | tf_op jit(solution)/shard_map/ppermute | solution.py:1110
  40.3 1.2 %collective-permute-start.11 = (f32[4,16,128]{2,1,0:T(8,128)S(1)}, f32[4,16,128]{2,1,0:T(8,128)S(1)}, u32[]{:S(2)}, u32[]{:S(2)}) collective-permute-start(f32[4,16,128]{2,1,0:T(8,128)S(1)} %pad_maximum_fusion.1), channel_id=1, source_target_pairs={{0,4},{1,5},{2,6},{3,7},{4,0},{5,1},{6,2},{7,3},{8,12},{9,13},{10,... | collective-permute-start | bytes 98312 | tf_op jit(solution)/shard_map/ppermute | solution.py:1110
  41.5 0.6 %collective-permute-start.12 = (f32[4,16,128]{2,1,0:T(8,128)S(1)}, f32[4,16,128]{2,1,0:T(8,128)S(1)}, u32[]{:S(2)}, u32[]{:S(2)}) collective-permute-start(f32[4,16,128]{2,1,0:T(8,128)S(1)} %pad_maximum_fusion.1), channel_id=1, source_target_pairs={{0,2},{1,3},{2,0},{3,1},{4,6},{5,7},{6,4},{7,5},{8,10},{9,11},{10,... | collective-permute-start | bytes 98312 | tf_op jit(solution)/shard_map/ppermute | solution.py:1110
  42.1 0.2 far.1.inv_far
  42.3 1.1 %collective-permute-done.10 = f32[4,16,128]{2,1,0:T(8,128)S(1)} collective-permute-done((f32[4,16,128]{2,1,0:T(8,128)S(1)}, f32[4,16,128]{2,1,0:T(8,128)S(1)}, u32[]{:S(2)}, u32[]{:S(2)}) %collective-permute-start.10) | collective-permute-done | bytes 32800 | tf_op jit(solution)/shard_map/ppermute | solution.py:1110
  43.4 0.7 %collective-permute-done.11 = f32[4,16,128]{2,1,0:T(8,128)S(1)} collective-permute-done((f32[4,16,128]{2,1,0:T(8,128)S(1)}, f32[4,16,128]{2,1,0:T(8,128)S(1)}, u32[]{:S(2)}, u32[]{:S(2)}) %collective-permute-start.11) | collective-permute-done | bytes 32800 | tf_op jit(solution)/shard_map/ppermute | solution.py:1110
  44.2 1.2 %collective-permute-done.12 = f32[4,16,128]{2,1,0:T(8,128)S(1)} collective-permute-done((f32[4,16,128]{2,1,0:T(8,128)S(1)}, f32[4,16,128]{2,1,0:T(8,128)S(1)}, u32[]{:S(2)}, u32[]{:S(2)}) %collective-permute-start.12) | collective-permute-done | bytes 32800 | tf_op jit(solution)/shard_map/ppermute | solution.py:1110
  45.5 4.2 %fifth.1 = (f32[8,8,8,256]{3,2,1,0:T(8,128)S(1)}, f32[8,8,8,256]{3,2,1,0:T(8,128)S(1)}, f32[8,8,128]{2,1,0:T(8,128)S(1)}, f32[8,8,128]{2,1,0:T(8,128)S(1)}, f32[...) custom-call(f32[4,16,512]{2,1,0:T(8,128)S(1)} %pad_maximum_fusion.whole, f32[27,16,128]{2,1,0:T(8,128)S(1)} %get-tuple-element.46.res, ...), custom_call_target="tpu_custom_call" | custom-call | tf_op jit(solution)/shard_map/fifth/pallas_call | solution.py:1121
  49.8 1.7 %collective-permute-start.14 = (f32[9,8,128]{2,1,0:T(8,128)S(1)}, f32[9,8,128]{2,1,0:T(8,128)S(1)}, u32[]{:S(2)}, u32[]{:S(2)}) collective-permute-start(f32[9,8,128]{2,1,0:T(8,128)S(1)} %get-tuple-element.62), channel_id=1, source_target_pairs={{0,7},{1,2},{2,1},{3,4},{4,3},{5,6},{6,5},{7,0},{8,15},{9,10},{10,... | collective-permute-start | bytes 110600 | tf_op jit(solution)/shard_map/ppermute | solution.py:1068
  51.5 0.9 %later_mean.1 = (f32[8,8,8,256]{3,2,1,0:T(8,128)S(1)}, f32[8,8,8,256]{3,2,1,0:T(8,128)S(1)}) custom-call(f32[8,8,8,256]{3,2,1,0:T(8,128)S(1)} %get-tuple-element.55.q, f32[8,8,8,256]{3,2,1,0:T(8,128)S(1)} %get-tuple-element.52.inv, f32[6,8,128]{2,1,0:T(8,128)S(1)} %get-tuple-element.53.ghost, f32[8,8,128]{2,1,0:T(8,128)S(1)} %get-tuple-element.56.qz), custom_call_target="tpu_custom_call" | custom-call | tf_op jit(solution)/shard_map/later_mean/pallas_call | solution.py:1128
  52.4 2.1 %collective-permute-done.14.r2 = f32[9,8,128]{2,1,0:T(8,128)S(1)} collective-permute-done((f32[9,8,128]{2,1,0:T(8,128)S(1)}, f32[9,8,128]{2,1,0:T(8,128)S(1)}, u32[]{:S(2)}, u32[]{:S(2)}) %collective-permute-start.14) | collective-permute-done | bytes 36896 | tf_op jit(solution)/shard_map/ppermute | solution.py:1068
  54.5 1.5 %last.1 = f32[8,8,8,256]{3,2,1,0:T(8,128)} custom-call(f32[8,8,8,256]{3,2,1,0:T(8,128)S(1)} %get-tuple-element.55.q, f32[8,8,8,256]{3,2,1,0:T(8,128)S(1)} %get-tuple-element.52.inv, f32[8,8,8,256]{3,2,1,0:T(8,128)S(1)} %get-tuple-element.57.d, f32[8,8,8,256]{3,2,1,0:T(8,128)S(1)} %get-tuple-element.58.y0, f32[8,8,8,256]{3,2,1,0:T(8,128)S(1)} %get-tuple-element.59.x, ...), custom_call_target="tpu_custom_call" | custom-call | tf_op jit(solution)/shard_map/last/pallas_call | solution.py:1129
  (20 shorter events, 0.3 us)
Async XLA Ops:
  0.0 1.2 %copy-start = (f32[8,8,8,256]{3,2,1,0:T(8,128)S(1)}, f32[8,8,8,256]{3,2,1,0:T(8,128)}, u32[]{:S(2)}) copy-start(f32[8,8,8,256]{3,2,1,0:T(8,128)} %rhs.3) | copy-start | bytes 1572868
  1.9 5.6 %collective-permute-start = (f32[17,8,128]{2,1,0:T(8,128)S(1)}, f32[17,8,128]{2,1,0:T(8,128)S(1)}, u32[]{:S(2)}, u32[]{:S(2)}) collective-permute-start(f32[17,8,128]{2,1,0:T(8,128)S(1)} %get-tuple-element.35), channel_id=1, source_target_pairs={{0,8},{8,0},{16,24},{24,16},{1,9},{9,1},{17,25},{25,17},{2,10},{10... | collective-permute-start | bytes 208904 | tf_op jit(solution)/shard_map/ppermute | solution.py:1071
  5.0 6.2 %collective-permute-start.1 = (f32[17,8,128]{2,1,0:T(8,128)S(1)}, f32[17,8,128]{2,1,0:T(8,128)S(1)}, u32[]{:S(2)}, u32[]{:S(2)}) collective-permute-start(f32[17,8,128]{2,1,0:T(8,128)S(1)} %get-tuple-element.36), channel_id=1, source_target_pairs={{0,24},{8,16},{16,8},{24,0},{1,25},{9,17},{17,9},{25,1},{2,26},{10... | collective-permute-start | bytes 208904 | tf_op jit(solution)/shard_map/ppermute | solution.py:1071
  11.4 3.6 %collective-permute-start.2 = (f32[17,8,128]{2,1,0:T(8,128)S(1)}, f32[17,8,128]{2,1,0:T(8,128)S(1)}, u32[]{:S(2)}, u32[]{:S(2)}) collective-permute-start(f32[17,8,128]{2,1,0:T(8,128)S(1)} %get-tuple-element.40), channel_id=1, source_target_pairs={{0,1},{1,0},{2,3},{3,2},{4,5},{5,4},{6,7},{7,6},{8,9},{9,8},{10,11... | collective-permute-start | bytes 208904 | tf_op jit(solution)/shard_map/ppermute | solution.py:1068
  11.5 4.9 %copy-start.2 = (bf16[224,512]{1,0:T(8,128)(2,1)S(1)}, bf16[224,512]{1,0:T(8,128)(2,1)}, u32[]{:S(2)}) copy-start(bf16[224,512]{1,0:T(8,128)(2,1)} %constant.55.clone.table) | copy-start | bytes 688132
  11.5 4.8 %collective-permute-start.3 = (f32[17,8,128]{2,1,0:T(8,128)S(1)}, f32[17,8,128]{2,1,0:T(8,128)S(1)}, u32[]{:S(2)}, u32[]{:S(2)}) collective-permute-start(f32[17,8,128]{2,1,0:T(8,128)S(1)} %get-tuple-element.41), channel_id=1, source_target_pairs={{0,7},{1,2},{2,1},{3,4},{4,3},{5,6},{6,5},{7,0},{8,15},{9,10},{10,... | collective-permute-start | bytes 208904 | tf_op jit(solution)/shard_map/ppermute | solution.py:1068
  18.6 10.0 %collective-permute-start.4 = (f32[88,256]{1,0:T(8,128)S(1)}, f32[88,256]{1,0:T(8,128)S(1)}, u32[]{:S(2)}, u32[]{:S(2)}) collective-permute-start(f32[88,256]{1,0:T(8,128)S(1)} %get-tuple-element.43), channel_id=1, source_target_pairs={{0,8},{8,16},{16,24},{24,0},{1,9},{9,17},{17,25},{25,1},{2,10},{10... | collective-permute-start | bytes 270344 | tf_op jit(solution)/shard_map/ppermute | solution.py:1092
  18.6 10.0 %collective-permute-start.6 = (f32[88,256]{1,0:T(8,128)S(1)}, f32[88,256]{1,0:T(8,128)S(1)}, u32[]{:S(2)}, u32[]{:S(2)}) collective-permute-start(f32[88,256]{1,0:T(8,128)S(1)} %get-tuple-element.44), channel_id=1, source_target_pairs={{0,24},{8,0},{16,8},{24,16},{1,25},{9,1},{17,9},{25,17},{2,26},{10... | collective-permute-start | bytes 270344 | tf_op jit(solution)/shard_map/ppermute | solution.py:1092
  22.4 6.2 %collective-permute-start.5 = (f32[56,256]{1,0:T(8,128)S(1)}, f32[56,256]{1,0:T(8,128)S(1)}, u32[]{:S(2)}, u32[]{:S(2)}) collective-permute-start(f32[56,256]{1,0:T(8,128)S(1)} %get-tuple-element.42.refs_0_), channel_id=1, source_target_pairs={{0,16},{8,24},{16,0},{24,8},{1,17},{9,25},{17,1},{25,9},{2,18},{10... | collective-permute-start | bytes 172040 | tf_op jit(solution)/shard_map/ppermute | solution.py:1092
  28.9 2.6 %collective-permute-start.7 = (f32[17,16,128]{2,1,0:T(8,128)S(1)}, f32[17,16,128]{2,1,0:T(8,128)S(1)}, u32[]{:S(2)}, u32[]{:S(2)}) collective-permute-start(f32[17,16,128]{2,1,0:T(8,128)S(1)} %column.1.own), channel_id=1, source_target_pairs={{0,1},{1,0},{2,3},{3,2},{4,5},{5,4},{6,7},{7,6},{8,9},{9,8},{10,11... | collective-permute-start | bytes 417800 | tf_op jit(solution)/shard_map/ppermute | solution.py:1068
  29.0 6.6 %collective-permute-start.8 = (f32[17,16,128]{2,1,0:T(8,128)S(1)}, f32[17,16,128]{2,1,0:T(8,128)S(1)}, u32[]{:S(2)}, u32[]{:S(2)}) collective-permute-start(f32[17,16,128]{2,1,0:T(8,128)S(1)} %column.1.own), channel_id=1, source_target_pairs={{0,7},{1,2},{2,1},{3,4},{4,3},{5,6},{6,5},{7,0},{8,15},{9,10},{10,... | collective-permute-start | bytes 417800 | tf_op jit(solution)/shard_map/ppermute | solution.py:1068
  37.3 1.2 %collective-permute-start.9 = (f32[4,16,64]{2,1,0:T(8,128)S(1)}, f32[4,16,64]{2,1,0:T(8,128)S(1)}, u32[]{:S(2)}, u32[]{:S(2)}) collective-permute-start(f32[4,16,64]{2,1,0:T(8,128)S(1)} %get-tuple-element.45), channel_id=1, source_target_pairs={{0,1},{1,0},{2,3},{3,2},{4,5},{5,4},{6,7},{7,6},{8,9},{9,8},{10,11... | collective-permute-start | bytes 49160 | tf_op jit(solution)/shard_map/ppermute | solution.py:1110
  38.6 4.8 %collective-permute-start.10 = (f32[4,16,128]{2,1,0:T(8,128)S(1)}, f32[4,16,128]{2,1,0:T(8,128)S(1)}, u32[]{:S(2)}, u32[]{:S(2)}) collective-permute-start(f32[4,16,128]{2,1,0:T(8,128)S(1)} %pad_maximum_fusion.1), channel_id=1, source_target_pairs={{0,6},{1,7},{2,4},{3,5},{4,2},{5,3},{6,0},{7,1},{8,14},{9,15},{10,... | collective-permute-start | bytes 98312 | tf_op jit(solution)/shard_map/ppermute | solution.py:1110
  40.3 3.9 %collective-permute-start.11 = (f32[4,16,128]{2,1,0:T(8,128)S(1)}, f32[4,16,128]{2,1,0:T(8,128)S(1)}, u32[]{:S(2)}, u32[]{:S(2)}) collective-permute-start(f32[4,16,128]{2,1,0:T(8,128)S(1)} %pad_maximum_fusion.1), channel_id=1, source_target_pairs={{0,4},{1,5},{2,6},{3,7},{4,0},{5,1},{6,2},{7,3},{8,12},{9,13},{10,... | collective-permute-start | bytes 98312 | tf_op jit(solution)/shard_map/ppermute | solution.py:1110
  41.5 3.9 %collective-permute-start.12 = (f32[4,16,128]{2,1,0:T(8,128)S(1)}, f32[4,16,128]{2,1,0:T(8,128)S(1)}, u32[]{:S(2)}, u32[]{:S(2)}) collective-permute-start(f32[4,16,128]{2,1,0:T(8,128)S(1)} %pad_maximum_fusion.1), channel_id=1, source_target_pairs={{0,2},{1,3},{2,0},{3,1},{4,6},{5,7},{6,4},{7,5},{8,10},{9,11},{10,... | collective-permute-start | bytes 98312 | tf_op jit(solution)/shard_map/ppermute | solution.py:1110
  42.3 3.2 %copy-start.1 = (bf16[512,192]{1,0:T(8,128)(2,1)S(1)}, bf16[512,192]{1,0:T(8,128)(2,1)}, u32[]{:S(2)}) copy-start(bf16[512,192]{1,0:T(8,128)(2,1)} %constant.56.clone.kron) | copy-start | bytes 589828
  49.7 2.7 %collective-permute-start.13 = (f32[9,8,128]{2,1,0:T(8,128)S(1)}, f32[9,8,128]{2,1,0:T(8,128)S(1)}, u32[]{:S(2)}, u32[]{:S(2)}) collective-permute-start(f32[9,8,128]{2,1,0:T(8,128)S(1)} %get-tuple-element.61), channel_id=1, source_target_pairs={{0,1},{1,0},{2,3},{3,2},{4,5},{5,4},{6,7},{7,6},{8,9},{9,8},{10,11... | collective-permute-start | bytes 110600 | tf_op jit(solution)/shard_map/ppermute | solution.py:1068
  49.8 4.7 %collective-permute-start.14 = (f32[9,8,128]{2,1,0:T(8,128)S(1)}, f32[9,8,128]{2,1,0:T(8,128)S(1)}, u32[]{:S(2)}, u32[]{:S(2)}) collective-permute-start(f32[9,8,128]{2,1,0:T(8,128)S(1)} %get-tuple-element.62), channel_id=1, source_target_pairs={{0,7},{1,2},{2,1},{3,4},{4,3},{5,6},{6,5},{7,0},{8,15},{9,10},{10,... | collective-permute-start | bytes 110600 | tf_op jit(solution)/shard_map/ppermute | solution.py:1068
